TPU v7x, 32 devices: a whole 2x2x4 slice. The times are simulated.
32 devices in a mesh: shard: 8 (over z, x), heads: 4 (over y, core).
Axes of the slice: x: 2, y: 2, z: 4, core: 2. Of those that a mesh axis runs over, the one named last changes fastest.
Arguments:
- tokens: bfloat16 [8192, 1024], P('shard', 'heads'), may hold values from -6 to 6
- z_weight: bfloat16 [1024, 2048], P('shard', 'heads'), may hold values from -0.1875 to 0.1875
- x_weight: bfloat16 [1024, 2048], P('shard', 'heads'), may hold values from -0.1875 to 0.1875
- bc_weight: bfloat16 [1024, 256], P('shard'), may hold values from -0.1875 to 0.1875
- dt_weight: bfloat16 [1024, 32], P('shard', 'heads'), may hold values from -0.1875 to 0.1875
- out_weight: bfloat16 [2048, 1024], P('heads', 'shard'), may hold values from -0.125 to 0.125
- norm_gain: float32 [1024], replicated, may hold values from 0.5 to 1.5
- gate_gain: float32 [2048], P('heads'), may hold values from 0.5 to 1.5
- x_conv_weight: float32 [4, 2048], P(None, 'heads'), may hold values from -3 to 3
- x_conv_bias: float32 [2048], P('heads'), may hold values from -3 to 3
- bc_conv_weight: float32 [4, 256], replicated, may hold values from -3 to 3
- bc_conv_bias: float32 [256], replicated, may hold values from -3 to 3
- step_bias: float32 [32], P('heads'), may hold values from -5 to -2
- decay_log: float32 [32], P('heads'), may hold values from -1 to 2.7
- skip_gain: float32 [32], P('heads'), may hold values from 0.5 to 1.5
- cotangent: bfloat16 [8192, 1024], P('shard', 'heads'), may hold values from -6 to 6
Outputs:
- mixed: bfloat16 [8192, 1024], P('shard', 'heads')
- tokens_grad: bfloat16 [8192, 1024], P('shard', 'heads')
- z_weight_grad: float32 [1024, 2048], P('shard', 'heads')
- x_weight_grad: float32 [1024, 2048], P('shard', 'heads')
- bc_weight_grad: float32 [1024, 256], P('shard', 'heads')
- dt_weight_grad: float32 [1024, 32], P('shard', 'heads')
- out_weight_grad: float32 [2048, 1024], P('heads', 'shard')
- norm_gain_grad: float32 [1024], P('heads')
- gate_gain_grad: float32 [2048], P('heads')
- x_conv_weight_grad: float32 [4, 2048], P(None, 'heads')
- x_conv_bias_grad: float32 [2048], P('heads')
- bc_conv_weight_grad: float32 [4, 256], replicated
- bc_conv_bias_grad: float32 [256], replicated
- step_bias_grad: float32 [32], P('heads')
- decay_log_grad: float32 [32], P('heads')
- skip_gain_grad: float32 [32], P('heads')
All inputs are finite; a program needn't handle non-finite values.
Results may differ from a plain program's by a relative error of at most 0.0095.
Values may be sent and summed in bfloat16 or wider, within the bound.
No kernel may reach another device: no remote copies, remote signals or barrier semaphores. Data moves between devices by JAX's collectives and lax.ppermute only.
A program may use at most 128 MiB of HBM per device.

v0:
```python
import jax
import jax.numpy as jnp
from jax import lax
from jax.sharding import PartitionSpec as P

CONV_WIDTH = 4
BLOCK_LEN = 256
LEN = 1024


epsilon = 1e-05
highest = lax.Precision.HIGHEST


def conv_silu(values, weights, biases):
    length = values.shape[1]
    padded = jnp.pad(values, ((0, 0), (CONV_WIDTH - 1, 0), (0, 0)))
    summed = biases + weights[0] * padded[:, 0:length]
    for tap_index in range(1, CONV_WIDTH):
        summed = summed + weights[tap_index] * padded[:, tap_index : tap_index + length]
    return jax.nn.silu(summed)


def to_blocks(values):
    seq_count, length = (values.shape[0], values.shape[1])
    shaped = values.reshape((seq_count, length // BLOCK_LEN, BLOCK_LEN) + values.shape[2:])
    return jnp.moveaxis(shaped, 1, 0)


def scan_step(state, pieces, decay_rate, skip_gain):
    block_x, block_b, block_c, block_dt = pieces
    cumulative = jnp.cumsum(block_dt * decay_rate, axis=1)
    by_head = jnp.swapaxes(cumulative, 1, 2)
    lower = jnp.tril(jnp.ones((BLOCK_LEN, BLOCK_LEN), dtype=bool))
    spread = by_head[:, :, :, None] - by_head[:, :, None, :]
    decays = jnp.where(lower, jnp.exp(jnp.where(lower, spread, 0.0)), 0.0)
    scores = jnp.einsum("stn,sun->stu", block_c, block_b, precision=highest)
    mixing = decays * scores[:, None] * jnp.swapaxes(block_dt, 1, 2)[:, :, None, :]
    within = jnp.einsum("shtu,suhp->sthp", mixing, block_x, precision=highest)
    carried = (
        jnp.einsum("shpn,stn->sthp", state, block_c, precision=highest)
        * jnp.exp(cumulative)[..., None]
    )
    final = cumulative[:, -1]
    weights_in = jnp.exp(final[:, None, :] - cumulative) * block_dt
    updated = jnp.exp(final)[:, :, None, None] * state + jnp.einsum(
        "suh,suhp,sun->shpn", weights_in, block_x, block_b, precision=highest
    )
    outputs = within + carried + skip_gain[:, None] * block_x
    return (updated, outputs)


def state_space(inputs_x, inputs_b, inputs_c, steps_dt, decay_rate, skip_gain):
    seq_count, length, head_count, head_size = inputs_x.shape
    initial = jnp.zeros((seq_count, head_count, head_size, inputs_b.shape[-1]), jnp.float32)

    def stepper(state, pieces):
        return scan_step(state, pieces, decay_rate, skip_gain)

    ignored, results = lax.scan(
        jax.checkpoint(stepper),
        initial,
        (to_blocks(inputs_x), to_blocks(inputs_b), to_blocks(inputs_c), to_blocks(steps_dt)),
    )
    return jnp.moveaxis(results, 0, 1).reshape(inputs_x.shape)


def round_keep(values):
    return lax.optimization_barrier(values.astype(jnp.bfloat16)).astype(jnp.float32)


def contract_last(leading, trailing):
    return lax.dot_general(
        leading, trailing, (((1,), (1,)), ((), ())), preferred_element_type=jnp.float32
    )


def contract_first(leading, trailing):
    return lax.dot_general(
        leading, trailing, (((0,), (0,)), ((), ())), preferred_element_type=jnp.float32
    )


def body(
    tokens,
    z_weight,
    x_weight,
    bc_weight,
    dt_weight,
    out_weight,
    norm_gain,
    gate_gain,
    x_conv_weight,
    x_conv_bias,
    bc_conv_weight,
    bc_conv_bias,
    step_bias,
    decay_log,
    skip_gain,
    cotangent,
):
    full_rows, full_cot = (
        lax.all_gather(tokens, "heads", axis=1, tiled=True),
        lax.all_gather(cotangent, "heads", axis=1, tiled=True),
    )
    head_index = lax.axis_index("heads")
    head_groups = lax.axis_size("heads")
    row_count = tokens.shape[0]
    feature_share = tokens.shape[1]
    feature_total = feature_share * head_groups
    inner_share = z_weight.shape[1]
    inner_total = inner_share * head_groups
    head_share = dt_weight.shape[1]
    head_size = inner_share // head_share
    state_width = bc_weight.shape[1]
    state_share = state_width // head_groups
    seq_count = row_count // LEN
    rows_f32 = full_rows.astype(jnp.float32)
    scale_in = lax.rsqrt(jnp.mean(rows_f32 * rows_f32, axis=-1, keepdims=True) + epsilon)
    normed = (rows_f32 * scale_in * norm_gain).astype(jnp.bfloat16)
    whole_z, whole_x, whole_bc, whole_dt, whole_out = (
        lax.all_gather(z_weight, "shard", axis=0, tiled=True),
        lax.all_gather(x_weight, "shard", axis=0, tiled=True),
        lax.all_gather(bc_weight, "shard", axis=0, tiled=True),
        lax.all_gather(dt_weight, "shard", axis=0, tiled=True),
        lax.all_gather(out_weight, "shard", axis=1, tiled=True),
    )
    gate_in = jnp.dot(normed, whole_z, preferred_element_type=jnp.float32)
    inner_in = jnp.dot(normed, whole_x, preferred_element_type=jnp.float32)
    state_in = jnp.dot(normed, whole_bc, preferred_element_type=jnp.float32)
    step_in = jnp.dot(normed, whole_dt, preferred_element_type=jnp.float32)
    inner_conv, inner_conv_back = jax.vjp(
        conv_silu, inner_in.reshape(seq_count, LEN, inner_share), x_conv_weight, x_conv_bias
    )
    state_conv, state_conv_back = jax.vjp(
        conv_silu, state_in.reshape(seq_count, LEN, state_width), bc_conv_weight, bc_conv_bias
    )
    inner_round = round_keep(inner_conv)
    state_round = round_keep(state_conv)
    step_pre = step_in.reshape(seq_count, LEN, head_share) + step_bias
    steps_dt = jax.nn.softplus(step_pre)
    decay_rate = -jnp.exp(decay_log)
    half_state = state_width // 2
    scanned, scan_back = jax.vjp(
        state_space,
        inner_round.reshape(seq_count, LEN, head_share, head_size),
        state_round[..., :half_state],
        state_round[..., half_state:],
        steps_dt,
        decay_rate,
        skip_gain,
    )
    scanned = scanned.reshape(row_count, inner_share)
    gate_sig = jax.nn.sigmoid(gate_in)
    gate_act = gate_in * gate_sig
    mixed_in = scanned * gate_act
    square_sum = lax.psum(jnp.sum(mixed_in * mixed_in, axis=-1), "heads")
    scale_mid = lax.rsqrt(square_sum / inner_total + epsilon)[:, None]
    mid_hat = mixed_in * scale_mid
    normed_mid = (mid_hat * gate_gain).astype(jnp.bfloat16)
    partial_out = jnp.dot(normed_mid, whole_out, preferred_element_type=jnp.float32)
    out_share = lax.psum_scatter(partial_out, "heads", scatter_dimension=1, tiled=True)
    mixed = (tokens.astype(jnp.float32) + out_share).astype(jnp.bfloat16)
    grad_mid = contract_last(full_cot, whole_out)
    gate_gain_grad = jnp.sum(mid_hat * grad_mid, axis=0)
    grad_hat = grad_mid * gate_gain
    mid_stat = lax.psum(jnp.sum(grad_hat * mid_hat, axis=-1), "heads")
    grad_mixed = scale_mid * (grad_hat - mid_hat * (mid_stat / inner_total)[:, None])
    grad_scanned = grad_mixed * gate_act
    grad_gate = (grad_mixed * scanned * gate_sig * (1.0 + gate_in * (1.0 - gate_sig))).astype(
        jnp.bfloat16
    )
    grad_x4, grad_b, grad_c, grad_dt, grad_rate, skip_gain_grad = scan_back(
        grad_scanned.reshape(seq_count, LEN, head_share, head_size)
    )
    decay_log_grad = grad_rate * decay_rate
    grad_step_pre = grad_dt * jax.nn.sigmoid(step_pre)
    step_bias_grad = jnp.sum(grad_step_pre, axis=(0, 1))
    grad_step = grad_step_pre.reshape(row_count, head_share).astype(jnp.bfloat16)
    state_total = lax.psum(jnp.concatenate([grad_b, grad_c], axis=-1), "heads")
    grad_inner3, x_conv_weight_grad, x_conv_bias_grad = inner_conv_back(
        grad_x4.reshape(seq_count, LEN, inner_share)
    )
    grad_state3, bc_conv_weight_grad, bc_conv_bias_grad = state_conv_back(state_total)
    grad_inner = grad_inner3.reshape(row_count, inner_share).astype(jnp.bfloat16)
    grad_state = grad_state3.reshape(row_count, state_width).astype(jnp.bfloat16)
    state_start = head_index * state_share
    state_part = lax.dynamic_slice_in_dim(grad_state, state_start, state_share, 1)
    grad_joined = jnp.concatenate([grad_gate, grad_inner, state_part, grad_step], axis=1)
    weights_joined = jnp.concatenate(
        [
            whole_z,
            whole_x,
            lax.dynamic_slice_in_dim(whole_bc, state_start, state_share, 1),
            whole_dt,
        ],
        axis=1,
    )
    grad_normed = contract_last(grad_joined, weights_joined)
    grad_share = lax.psum_scatter(grad_normed, "heads", scatter_dimension=1, tiled=True)
    tokens_hat = tokens.astype(jnp.float32) * scale_in
    gain_share = lax.dynamic_slice_in_dim(norm_gain, head_index * feature_share, feature_share, 0)
    norm_gain_grad = jnp.sum(tokens_hat * grad_share, axis=0)
    grad_scaled = grad_share * gain_share
    norm_stat = lax.psum(jnp.sum(grad_scaled * tokens_hat, axis=-1), "heads")
    tokens_grad = (
        cotangent.astype(jnp.float32)
        + scale_in * (grad_scaled - tokens_hat * (norm_stat / feature_total)[:, None])
    ).astype(jnp.bfloat16)
    grad_block = lax.psum_scatter(
        jnp.concatenate(
            [contract_first(normed, grad_joined), contract_first(full_cot, normed_mid)], axis=1
        ),
        "shard",
        scatter_dimension=0,
        tiled=True,
    )
    offset_bc = 2 * inner_share
    offset_dt = offset_bc + state_share
    offset_out = offset_dt + head_share
    z_weight_grad = grad_block[:, :inner_share]
    x_weight_grad = grad_block[:, inner_share:offset_bc]
    bc_weight_grad = grad_block[:, offset_bc:offset_dt]
    dt_weight_grad = grad_block[:, offset_dt:offset_out]
    out_weight_grad = grad_block[:, offset_out:].T
    summed_small = lax.psum(
        (
            norm_gain_grad,
            gate_gain_grad,
            x_conv_weight_grad,
            x_conv_bias_grad,
            bc_conv_weight_grad,
            bc_conv_bias_grad,
            step_bias_grad,
            decay_log_grad,
            skip_gain_grad,
        ),
        "shard",
    )
    return (
        mixed,
        tokens_grad,
        z_weight_grad,
        x_weight_grad,
        bc_weight_grad,
        dt_weight_grad,
        out_weight_grad,
        summed_small[0],
        summed_small[1],
        summed_small[2],
        summed_small[3],
        summed_small[4],
        summed_small[5],
        summed_small[6],
        summed_small[7],
        summed_small[8],
    )


def solution(mesh):
    placed = (
        P("shard", "heads"),
        P("shard", "heads"),
        P("shard", "heads"),
        P("shard", None),
        P("shard", "heads"),
        P("heads", "shard"),
        P(),
        P("heads"),
        P(None, "heads"),
        P("heads"),
        P(),
        P(),
        P("heads"),
        P("heads"),
        P("heads"),
        P("shard", "heads"),
    )
    return jax.shard_map(
        body,
        mesh=mesh,
        in_specs=placed,
        out_specs=(
            P("shard", "heads"),
            P("shard", "heads"),
            P("shard", "heads"),
            P("shard", "heads"),
            P("shard", "heads"),
            P("shard", "heads"),
            P("heads", "shard"),
            P("heads"),
            P("heads"),
            P(None, "heads"),
            P("heads"),
            P(),
            P(),
            P("heads"),
            P("heads"),
            P("heads"),
        ),
        check_vma=False,
    )
```

profile of v0, /device:TPU:0, one launch (start us, length us, event | category | flops | bytes accessed | tf_op | source)
XLA Modules:
  0.0 620.2 jit_solution(389479067078133263)
XLA Ops:
  10.7 33.5 %all_gather.24 = bf16[1024,256]{1,0:T(8,128)(2,1)S(1)} all-gather(bf16[128,256]{1,0:T(8,128)(2,1)} %param.23), channel_id=1, replica_groups=mesh['shard'=8,'heads'=4] {'shard'}, dimensions={0}, use_global_device_ids=true | all-gather | bytes 589824 | tf_op jit(solution)/shard_map/all_gather | solution.py:124
  44.4 26.0 %all_gather.22 = bf16[1024,8]{0,1:T(8,128)(2,1)S(1)} all-gather(bf16[128,8]{0,1:T(8,128)(2,1)S(1)} %copy-done.50), channel_id=1, replica_groups=mesh['shard'=8,'heads'=4] {'shard'}, dimensions={0}, use_global_device_ids=true | all-gather | bytes 18432 | tf_op jit(solution)/shard_map/all_gather | solution.py:125
  70.8 24.6 %all-gather.10.cloned.1.call-done = bf16[1024,512]{1,0:T(8,128)(2,1)} async-done(((bf16[128,512]{1,0:T(8,128)(2,1)}), bf16[1024,512]{1,0:T(8,128)(2,1)}) %all-gather.10.cloned.1.call-update) | async-done | bytes 1048592 | tf_op jit(solution)/shard_map/all_gather | solution.py:122
  95.4 4.8 concatenate.14
  100.2 18.4 %all-gather.6.cloned.1.call-done = bf16[1024,1024]{1,0:T(8,128)(2,1)} async-done(((bf16[1024,256]{1,0:T(8,128)(2,1)}), bf16[1024,1024]{1,0:T(8,128)(2,1)}) %all-gather.6.cloned.1.call-update) | async-done | bytes 2097168 | tf_op jit(solution)/shard_map/all_gather | solution.py:103
  130.8 3.9 copy.103
  136.4 50.0 %while.46 = (s32[]{:T(128)}, f32[1,8,64,128]{3,2,1,0:T(8,128)S(1)}, f32[4,1,256,8,64]{2,4,3,1,0:T(8,128)S(1)}, f32[4,1,8,64,128]{4,3,2,1,0:T(8,128)}, f32[4,1,25...) while((s32[]{:T(128)}, f32[1,8,64,128]{3,2,1,0:T(8,128)S(1)}, ...), condition=%wide.region_4.5_spmd.clone.clone, body=%wide.region_1.4_spmd.clone.clone.sunk | while | flops 909844480 | bytes 5731749 | solution.py:60
  141.6 3.8 fusion.270
  154.1 3.8 fusion.270
  166.6 3.8 fusion.270
  179.2 3.8 fusion.270
  189.1 5.1 reshape.1025
  194.3 5.5 multiply_reduce_fusion.10
  199.8 5.9 psum.91
  205.7 5.2 multiply_reduce_fusion.8
  210.9 5.6 psum.92
  216.5 4.7 fusion.146
  221.2 4.4 reshape.1023
  225.6 3.8 copy.119
  233.3 99.5 %while.45 = (s32[]{:T(128)}, f32[8]{0:T(128)}, f32[8]{0:T(128)}, f32[1,8,64,128]{3,2,1,0:T(8,128)S(1)}, f32[4,1,256,8,64]{2,4,3,1,0:T(8,128)}, /*index=5*/f32[4,...) while((s32[]{:T(128)}, f32[8]{0:T(128)}, f32[8]{0:T(128)}, ...), condition=%wide.region_24.25_spmd.clone, body=%wide.region_10.24_spmd.clone.sunk | while | flops 2127077376 | bytes 17477732 | solution.py:60
  252.8 3.8 fusion.254
  277.7 3.9 fusion.254
  302.6 3.8 fusion.254
  327.4 3.8 fusion.254
  338.1 4.9 reshape.1026
  349.9 22.9 %all-reduce.22.cloned.1.call-done = f32[1,1024,256]{2,1,0:T(8,128)} async-done(((f32[1,1024,256]{2,1,0:T(8,128)}), f32[1,1024,256]{2,1,0:T(8,128)}) %all-reduce.22.cloned.1.call-update) | async-done | bytes 1048592 | tf_op jit(solution)/shard_map/psum | solution.py:180
  376.5 4.2 concatenate.13
  380.7 7.3 %fusion.175 = f32[1024,1024]{1,0:T(8,128)} fusion(bf16[1024,1096]{1,0:T(8,128)(2,1)} %concatenate.13, bf16[1024,1096]{1,0:T(8,128)(2,1)} %concatenate.14), kind=kOutput, calls=%fused_computation.264 | convolution fusion | flops 2298478592 | bytes 8683520 | tf_op jit(solution)/shard_map/dot_general | solution.py:73
  403.9 29.2 %reduce-scatter.6.cloned.1.call-done = f32[1024,256]{1,0:T(8,128)} async-done(((f32[1024,1024]{1,0:T(8,128)}), f32[1024,256]{1,0:T(8,128)}) %reduce-scatter.6.cloned.1.call-update) | async-done | bytes 1048592 | tf_op jit(solution)/shard_map/reduce_scatter | solution.py:200
  435.0 37.7 %all-reduce.19 = (f32[256]{0:T(256)}, f32[512]{0:T(512)}, f32[4,512]{1,0:T(4,128)}, f32[512]{0:T(512)}, f32[4,256]{1,0:T(4,128)}, /*index=5*/f32[256]{0:T(256)}, f32[8]{0:T(128)}, f32[8]{0:T(128)}, f32[8]{0:T(128)}) all-reduce(f32[256]{0:T(256)S(1)} %get-tuple-element.752, ...), channel_id=1, replica_groups=mesh['shard'=8,'heads'=4] {'shard'}, use_global_device_ids=true, to_apply=%region_31.32 | all-reduce | flops 4632 | bytes 37056 | tf_op jit(solution)/shard_map/psum | solution.py:226
  472.6 6.1 psum.94
  482.9 124.4 %reduce-scatter.8.cloned.1.call-done = f32[128,1608]{0,1:T(8,128)} async-done(((f32[1024,1608]{0,1:T(8,128)}), f32[128,1608]{0,1:T(8,128)}) %reduce-scatter.8.cloned.1.call-update) | async-done | bytes 823312 | tf_op jit(solution)/shard_map/reduce_scatter | solution.py:210
  (452 shorter events, 186.1 us)
Async XLA Ops:
  7.2 37.0 %copy-start.48 = (f32[4,256]{1,0:T(4,128)S(1)}, f32[4,256]{1,0:T(4,128)}, u32[]{:S(2)}) copy-start(f32[4,256]{1,0:T(4,128)} %param.30) | copy-start | bytes 12292
  7.2 37.0 %copy-start.47 = (f32[4,512]{1,0:T(4,128)S(1)}, f32[4,512]{1,0:T(4,128)}, u32[]{:S(2)}) copy-start(f32[4,512]{1,0:T(4,128)} %param.28) | copy-start | bytes 24580
  7.2 37.1 %copy-start.50 = (bf16[128,8]{0,1:T(8,128)(2,1)S(1)}, bf16[128,8]{0,1:T(8,128)(2,1)}, u32[]{:S(2)}) copy-start(bf16[128,8]{0,1:T(8,128)(2,1)} %param.24) | copy-start | bytes 6148
  7.2 63.2 %copy-start.56 = (f32[8]{0:T(128)S(1)}, f32[8]{0:T(128)}, u32[]{:S(2)}) copy-start(f32[8]{0:T(128)} %param.33) | copy-start | bytes 100
  7.2 63.5 %all-gather.8.cloned.1.call-start = ((), (), s32[]{:S(2)}) async-start(), calls=%async_computation.4 | async-start | bytes 1179648 | tf_op jit(solution)/shard_map/all_gather | solution.py:123
  8.0 87.5 %all-gather.10.cloned.1.call-start = ((), (), s32[]{:S(2)}) async-start(), calls=%async_computation.5 | async-start | bytes 1179648 | tf_op jit(solution)/shard_map/all_gather | solution.py:122
  8.7 109.9 %all-gather.6.cloned.1.call-start = ((), (), s32[]{:S(2)}) async-start(), calls=%async_computation.3 | async-start | bytes 2621440 | tf_op jit(solution)/shard_map/all_gather | solution.py:103
  9.4 196.2 %all-gather.12.cloned.1.call-start = ((), (), s32[]{:S(2)}) async-start(), calls=%async_computation.6 | async-start | bytes 1179648 | tf_op jit(solution)/shard_map/all_gather | solution.py:126
  10.0 195.6 %all-gather.14.cloned.1.call-start = ((), (), s32[]{:S(2)}) async-start(), calls=%async_computation.8 | async-start | bytes 2621440 | tf_op jit(solution)/shard_map/all_gather | solution.py:104
  10.6 362.2 %all-reduce.22.cloned.1.call-start = ((), (), s32[]{:S(2)}) async-start(), calls=%async_computation.9 | async-start | bytes 2097152 | tf_op jit(solution)/shard_map/psum | solution.py:180
  44.2 77.4 %copy-start.39 = (f32[1,256]{1,0:T(1,128)}, f32[1,256]{1,0:T(1,128)S(1)}, u32[]{:S(2)}) copy-start(f32[1,256]{1,0:T(1,128)S(1)} %get-tuple-element.862) | copy-start | bytes 3076
  44.2 77.4 %copy-start.41 = (f32[1,256]{1,0:T(1,128)}, f32[1,256]{1,0:T(1,128)S(1)}, u32[]{:S(2)}) copy-start(f32[1,256]{1,0:T(1,128)S(1)} %get-tuple-element.863) | copy-start | bytes 3076
  44.3 77.4 %copy-start.43 = (f32[1,256]{1,0:T(1,128)}, f32[1,256]{1,0:T(1,128)S(1)}, u32[]{:S(2)}) copy-start(f32[1,256]{1,0:T(1,128)S(1)} %get-tuple-element.864) | copy-start | bytes 3076
  44.3 77.4 %copy-start.45 = (f32[1,256]{1,0:T(1,128)}, f32[1,256]{1,0:T(1,128)S(1)}, u32[]{:S(2)}) copy-start(f32[1,256]{1,0:T(1,128)S(1)} %get-tuple-element.865) | copy-start | bytes 3076
  44.3 81.4 %copy-start.23 = (f32[1,512]{1,0:T(1,128)}, f32[1,512]{1,0:T(1,128)S(1)}, u32[]{:S(2)}) copy-start(f32[1,512]{1,0:T(1,128)S(1)} %get-tuple-element.858) | copy-start | bytes 6148
  44.3 81.4 %copy-start.25 = (f32[1,512]{1,0:T(1,128)}, f32[1,512]{1,0:T(1,128)S(1)}, u32[]{:S(2)}) copy-start(f32[1,512]{1,0:T(1,128)S(1)} %get-tuple-element.859) | copy-start | bytes 6148
  44.3 81.4 %copy-start.27 = (f32[1,512]{1,0:T(1,128)}, f32[1,512]{1,0:T(1,128)S(1)}, u32[]{:S(2)}) copy-start(f32[1,512]{1,0:T(1,128)S(1)} %get-tuple-element.860) | copy-start | bytes 6148
  44.3 81.4 %copy-start.29 = (f32[1,512]{1,0:T(1,128)}, f32[1,512]{1,0:T(1,128)S(1)}, u32[]{:S(2)}) copy-start(f32[1,512]{1,0:T(1,128)S(1)} %get-tuple-element.861) | copy-start | bytes 6148
  100.2 20.7 %copy-start.53 = (f32[1024]{0:T(1024)S(1)}, f32[1024]{0:T(1024)}, u32[]{:S(2)}) copy-start(f32[1024]{0:T(1024)} %param.26) | copy-start | bytes 12292
  120.9 73.4 %copy-start.20 = (f32[1024]{0:T(1024)}, f32[1024]{0:T(1024)S(1)}, u32[]{:S(2)}) copy-start(f32[1024]{0:T(1024)S(1)} %add_rsqrt_fusion.1) | copy-start | bytes 12292
  194.3 11.4 %copy-start.34 = (f32[512]{0:T(512)S(1)}, f32[512]{0:T(512)}, u32[]{:S(2)}) copy-start(f32[512]{0:T(512)} %param.27) | copy-start | bytes 6148
  199.7 16.8 %copy-start.2 = (f32[1024,512]{1,0:T(8,128)}, f32[1024,512]{1,0:T(8,128)S(1)}, u32[]{:S(2)}) copy-start(f32[1024,512]{1,0:T(8,128)S(1)} %get-tuple-element.826) | copy-start | bytes 6291460
  335.2 97.9 %reduce-scatter.6.cloned.1.call-start = ((), (), s32[]{:S(2)}) async-start(), calls=%async_computation.10 | async-start | bytes 5242880 | tf_op jit(solution)/shard_map/reduce_scatter | solution.py:200
  338.1 5.9 copy-start.1
  348.7 24.0 %copy-start.7 = (f32[1,1024,256]{2,1,0:T(8,128)S(1)}, f32[1,1024,256]{2,1,0:T(8,128)}, u32[]{:S(2)}) copy-start(f32[1,1024,256]{2,1,0:T(8,128)} %get-tuple-element.828) | copy-start | bytes 3145732
  388.1 92.2 %reduce-scatter.4.cloned.1.call-start = ((), (), s32[]{:S(2)}) async-start(), calls=%async_computation.7 | async-start | bytes 5242880 | tf_op jit(solution)/shard_map/reduce_scatter | solution.py:162
  393.3 214.0 %reduce-scatter.8.cloned.1.call-start = ((), (), s32[]{:S(2)}) async-start(), calls=%async_computation.11 | async-start | bytes 7409664 | tf_op jit(solution)/shard_map/reduce_scatter | solution.py:210
  403.2 29.9 %copy-start.6 = (bf16[1024,256]{1,0:T(8,128)(2,1)S(1)}, bf16[1024,256]{1,0:T(8,128)(2,1)}, u32[]{:S(2)}) copy-start(bf16[1024,256]{1,0:T(8,128)(2,1)} %param.20) | copy-start | bytes 1572868
  403.2 31.8 %copy-start.33 = (f32[8]{0:T(128)S(1)}, f32[8]{0:T(128)}, u32[]{:S(2)}) copy-start(f32[8]{0:T(128)} %get-tuple-element.483) | copy-start | bytes 100
  403.2 31.8 %copy-start.51 = (f32[512]{0:T(512)S(1)}, f32[512]{0:T(512)}, u32[]{:S(2)}) copy-start(f32[512]{0:T(512)} %get-tuple-element.742) | copy-start | bytes 6148
  403.2 77.1 %copy-start.11 = (bf16[1024,256]{1,0:T(8,128)(2,1)S(1)}, bf16[1024,256]{1,0:T(8,128)(2,1)}, u32[]{:S(2)}) copy-start(bf16[1024,256]{1,0:T(8,128)(2,1)} %param.35) | copy-start | bytes 1572868
  433.1 47.2 %copy-start.8 = (f32[1024,256]{1,0:T(8,128)S(1)}, f32[1024,256]{1,0:T(8,128)}, u32[]{:S(2)}) copy-start(f32[1024,256]{1,0:T(8,128)} %reduce-scatter.6.cloned.1.call-done) | copy-start | bytes 3145732
  (53 other events, 117.2 us)
Sparse Core Ops, SparseCore 0:
  10.2 43.7 all-gather.7
  56.1 39.2 all-gather.9
  97.0 21.5 all-gather.5
  120.5 40.1 all-gather.11
  162.1 21.4 all-gather.13
  335.3 37.4 all-reduce.21
  388.2 44.8 reduce-scatter.5
  435.6 44.6 reduce-scatter.3
  484.4 122.8 reduce-scatter.7
where the time goes:
time: 632 us; the launch traced here: 620 us
  waiting for transfers between devices  224 us (35%)
  matrix products  117 us (19%)
  blocking collectives  115 us (18%)
  local copies, waits for them, and re-layouts  82.5 us (13%)
  other arithmetic  65.2 us (10%)
  between operations  14.8 us (2%)
    reduce_scatter x1, waiting for transfers between devices, body(): lax.psum_scatter(jnp.concatenate([contract_first(normed, grad_joined), co...  124 us
    dot_general x12, matrix products, scan_step(): within = jnp.einsum('shtu,suhp->sthp', mixing, block_x, precision=highest)  44.5 us
    psum x1, blocking collectives, body(): lax.psum((norm_gain_grad, gate_gain_grad, x_conv_weight_grad, x_conv_bias...  37.7 us
    all_gather x1, blocking collectives, body(): lax.all_gather(bc_weight, 'shard', axis=0, tiled=True)  33.5 us
    reduce_scatter x1, waiting for transfers between devices, body(): lax.psum_scatter(grad_normed, 'heads', scatter_dimension=1, tiled=True)  29.2 us
    all_gather x1, blocking collectives, body(): lax.all_gather(dt_weight, 'shard', axis=0, tiled=True)  26 us
    all_gather x1, waiting for transfers between devices, body(): lax.all_gather(z_weight, 'shard', axis=0, tiled=True)  24.6 us
    another operation x52, other arithmetic  23.1 us
  transfers between devices with their start and end apart: 9, of which 6 were waited for; matrix products, arithmetic and copies ran while one was open for 19% of the time, Pallas kernels for 0%

commit v1 on v0

v1 whole, which is shorter than its diff:
```python
import functools

import jax
import jax.numpy as jnp
from jax import lax
from jax.experimental import pallas as pl
from jax.experimental.pallas import tpu as pltpu
from jax.sharding import PartitionSpec as P

CONV_WIDTH = 4
LEN = 1024
BLOCK = 256
LANES = 128

epsilon = 1e-05
highest = lax.Precision.HIGHEST
f32 = jnp.float32
bf16 = jnp.bfloat16
VMEM_LIMIT = 50 * 1024 * 1024


def dot(left, right, left_dim=1, right_dim=0, precision=None):
    return lax.dot_general(
        left,
        right,
        (((left_dim,), (right_dim,)), ((), ())),
        precision=precision,
        preferred_element_type=f32,
    )


def spreader(head_share, head_size):
    row = lax.broadcasted_iota(jnp.int32, (LANES, head_share * head_size), 0)
    head = lax.broadcasted_iota(jnp.int32, (LANES, head_share * head_size), 1) // head_size
    return (row == head).astype(f32)


def lower_mask(size):
    row = lax.broadcasted_iota(jnp.int32, (size, size), 0)
    col = lax.broadcasted_iota(jnp.int32, (size, size), 1)
    return row >= col


def forward_kernel(
    sizes,
    rows_ref,
    gain_ref,
    weight_ref,
    x_taps_ref,
    x_bias_ref,
    s_taps_ref,
    s_bias_ref,
    step_bias_ref,
    rate_ref,
    skip_ref,
    normed_ref,
    inner_ref,
    x_pre_ref,
    x_ref,
    state_in_ref,
    s_pre_ref,
    bc_ref,
    step_ref,
    cum_ref,
    start_ref,
    scanned_ref,
    x_buf,
    s_buf,
    state,
):
    head_share, head_size, blocks_per_seq = sizes
    inner = head_share * head_size
    half = s_bias_ref.shape[1] // 2

    @pl.when(pl.program_id(0) % blocks_per_seq == 0)
    def _():
        x_buf[0:8, :] = jnp.zeros((8, inner), f32)
        s_buf[0:8, :] = jnp.zeros((8, 2 * half), f32)
        state[...] = jnp.zeros(state.shape, f32)

    rows = rows_ref[...].astype(f32)
    scale = lax.rsqrt(jnp.mean(rows * rows, axis=-1, keepdims=True) + epsilon)
    normed = (rows * scale * gain_ref[...]).astype(bf16)
    normed_ref[...] = normed
    projected = dot(normed, weight_ref[...])
    inner_in = projected[:, :inner]
    state_in = projected[:, inner : inner + 2 * half]
    step_pre = projected[:, inner + 2 * half :] + step_bias_ref[...]
    inner_ref[...] = inner_in
    state_in_ref[...] = state_in
    step_ref[...] = step_pre

    def conv(buf, values, taps_ref, bias_ref):
        buf[8 : 8 + BLOCK, :] = values
        total = bias_ref[...] + taps_ref[3:4, :] * values
        for tap in range(CONV_WIDTH - 1):
            total = total + taps_ref[tap : tap + 1, :] * buf[5 + tap : 5 + tap + BLOCK, :]
        buf[0:8, :] = buf[BLOCK : BLOCK + 8, :]
        return total

    x_pre = conv(x_buf, inner_in, x_taps_ref, x_bias_ref)
    x_pre_ref[...] = x_pre
    x = (x_pre * jax.nn.sigmoid(x_pre)).astype(bf16)
    x_ref[...] = x
    s_pre = conv(s_buf, state_in, s_taps_ref, s_bias_ref)
    s_pre_ref[...] = s_pre
    bc = (s_pre * jax.nn.sigmoid(s_pre)).astype(bf16)
    bc_ref[...] = bc
    b, c = bc[:, :half], bc[:, half:]

    steps = jax.nn.softplus(step_pre)
    lower = lower_mask(BLOCK)
    cum = dot(lower.astype(f32), steps * rate_ref[...], precision=highest)
    cum_ref[...] = cum
    cum_t = cum.T
    spread = spreader(head_share, head_size)
    cum_x = dot(cum, spread, precision=highest)
    steps_x = dot(steps, spread, precision=highest)
    last = cum_x[BLOCK - 1 :, :]
    x_f32 = x.astype(f32)
    stepped = x_f32 * steps_x
    stepped_low = stepped.astype(bf16)

    old = state[...]
    old_low = old.astype(bf16)
    start_ref[0] = old
    out = dot(c, old_low) * jnp.exp(cum_x) + skip_ref[...] * x_f32
    weighted = (stepped * jnp.exp(last - cum_x)).astype(bf16)
    state[...] = old * jnp.exp(last) + dot(b, weighted, 0, 0)

    scores = dot(c, b, 1, 1)
    pair = LANES // head_size
    lane_head = lax.broadcasted_iota(jnp.int32, (BLOCK, LANES), 1) // head_size
    for first in range(0, head_share, pair):
        at = first * head_size
        values = stepped_low[:, at : at + LANES]
        total = None
        for k in range(pair):
            head = first + k
            decays = jnp.exp(
                jnp.where(lower, cum[:, head : head + 1] - cum_t[head : head + 1, :], -1e30)
            )
            term = dot((decays * scores).astype(bf16), values)
            total = term if k == 0 else jnp.where(lane_head == k, term, total)
        scanned_ref[:, at : at + LANES] = out[:, at : at + LANES] + total


def forward_scan(rows, gain, weight, x_taps, x_bias, s_taps, s_bias, step_bias, rate, skip, head_share, head_size):
    count, features = rows.shape
    inner = head_share * head_size
    state2 = s_bias.shape[1]
    blocks = count // BLOCK
    whole = lambda a: pl.BlockSpec(a.shape, lambda i: (0,) * a.ndim)
    per = lambda width: pl.BlockSpec((BLOCK, width), lambda i: (i, 0))
    shape = lambda width, kind: jax.ShapeDtypeStruct((count, width), kind)
    outs = [
        (features, bf16),
        (inner, f32),
        (inner, f32),
        (inner, bf16),
        (state2, f32),
        (state2, f32),
        (state2, bf16),
        (LANES, f32),
        (LANES, f32),
    ]
    consts = (gain, weight, x_taps, x_bias, s_taps, s_bias, step_bias, rate, skip)
    return pl.pallas_call(
        functools.partial(forward_kernel, (head_share, head_size, LEN // BLOCK)),
        grid=(blocks,),
        in_specs=[per(features)] + [whole(a) for a in consts],
        out_specs=[per(w) for w, _ in outs]
        + [pl.BlockSpec((1, state2 // 2, inner), lambda i: (i, 0, 0)), per(inner)],
        out_shape=[shape(w, k) for w, k in outs]
        + [jax.ShapeDtypeStruct((blocks, state2 // 2, inner), f32), shape(inner, f32)],
        scratch_shapes=[
            pltpu.VMEM((BLOCK + 8, inner), f32),
            pltpu.VMEM((BLOCK + 8, state2), f32),
            pltpu.VMEM((state2 // 2, inner), f32),
        ],
        compiler_params=pltpu.CompilerParams(vmem_limit_bytes=VMEM_LIMIT),
    )(rows, *consts)


def backward_kernel(
    sizes,
    grad_ref,
    inner_ref,
    x_pre_ref,
    x_ref,
    bc_ref,
    step_ref,
    cum_ref,
    start_ref,
    x_taps_ref,
    rate_ref,
    skip_ref,
    grad_inner_ref,
    grad_bc_ref,
    grad_step_ref,
    sums_ref,
    small_ref,
    pre_buf,
    state,
):
    head_share, head_size, blocks_per_seq = sizes
    inner = head_share * head_size
    half = bc_ref.shape[1] // 2
    at_block = pl.num_programs(0) - 1 - pl.program_id(0)

    @pl.when(pl.program_id(0) == 0)
    def _():
        sums_ref[...] = jnp.zeros(sums_ref.shape, f32)
        small_ref[...] = jnp.zeros(small_ref.shape, f32)

    @pl.when(at_block % blocks_per_seq == blocks_per_seq - 1)
    def _():
        pre_buf[BLOCK:, :] = jnp.zeros((8, inner), f32)
        state[...] = jnp.zeros(state.shape, f32)

    grad = grad_ref[...]
    grad_low = grad.astype(bf16)
    x = x_ref[...].astype(f32)
    bc = bc_ref[...]
    b, c = bc[:, :half], bc[:, half:]
    step_pre = step_ref[...]
    steps = jax.nn.softplus(step_pre)
    cum = cum_ref[...]
    cum_t = cum.T
    lower = lower_mask(BLOCK)
    upper_low = jnp.logical_not(lower).astype(bf16)
    row = lax.broadcasted_iota(jnp.int32, (BLOCK, BLOCK), 0)
    col = lax.broadcasted_iota(jnp.int32, (BLOCK, BLOCK), 1)
    upper_incl = (row <= col).astype(bf16)
    strict = row > col
    spread = spreader(head_share, head_size)
    cum_x = dot(cum, spread, precision=highest)
    steps_x = dot(steps, spread, precision=highest)
    last = cum_x[BLOCK - 1 :, :]
    decay_in = jnp.exp(cum_x)
    decay_out = jnp.exp(last - cum_x)
    stepped = x * steps_x
    stepped_low = stepped.astype(bf16)

    old = start_ref[0]
    later = state[...]
    later_low = later.astype(bf16)
    grad_decayed = grad * decay_in
    grad_decayed_low = grad_decayed.astype(bf16)
    from_later = dot(b, later_low) * decay_out
    carried = dot(c, old.astype(bf16))
    grad_c = dot(grad_decayed_low, old.astype(bf16), 1, 1)
    grad_b = dot((stepped * decay_out).astype(bf16), later_low, 1, 1)
    state[...] = later * jnp.exp(last) + dot(c, grad_decayed_low, 0, 0)

    scores = dot(c, b, 1, 1)
    pair = LANES // head_size
    lane_head = lax.broadcasted_iota(jnp.int32, (BLOCK, LANES), 1) // head_size
    lane = lax.broadcasted_iota(jnp.int32, (BLOCK, LANES), 1)
    crossing = jnp.zeros((BLOCK, LANES), f32)
    gathered = jnp.zeros((BLOCK, BLOCK), f32)
    within = []
    for first in range(0, head_share, pair):
        at = first * head_size
        grads = grad_low[:, at : at + LANES]
        values = stepped_low[:, at : at + LANES]
        total = None
        for k in range(pair):
            head = first + k
            decays = jnp.exp(
                jnp.where(lower, cum[:, head : head + 1] - cum_t[head : head + 1, :], -1e30)
            )
            own = jnp.where(lane_head == k, grads, jnp.zeros_like(grads))
            products = dot(own, values, 1, 1) * decays
            gathered = gathered + products
            term = dot((decays * scores).astype(bf16), grads, 0, 0)
            total = term if k == 0 else jnp.where(lane_head == k, term, total)
            pairs = dot(upper_incl, (products * scores).astype(bf16))
            crossed = jnp.sum(jnp.where(strict, pairs, 0.0), axis=1, keepdims=True)
            crossing = jnp.where(lane == head, crossed, crossing)
        within.append(total)
    gathered_low = gathered.astype(bf16)
    grad_bc_ref[:, :half] = grad_b + dot(gathered_low, c, 0, 0)
    grad_bc_ref[:, half:] = grad_c + dot(gathered_low, b)

    by_x = jnp.concatenate(within, axis=1) + from_later
    fold = lambda values: dot(values, spread, 1, 1, precision=highest)
    direct = fold(by_x * x)
    into = fold(grad_decayed * carried)
    onward = steps * fold(from_later * x)
    tops = jnp.sum(later * old, axis=0, keepdims=True) * jnp.exp(last)
    spanning = fold(jnp.broadcast_to(tops, (8, inner)))[0:1, :]
    suffix = dot(upper_incl.astype(f32), into, precision=highest)
    prefix = dot(strict.astype(f32), onward, precision=highest)
    by_decay = crossing + suffix + prefix + spanning
    by_step = direct + rate_ref[...] * by_decay
    grad_step = by_step * jax.nn.sigmoid(step_pre)
    grad_step_ref[...] = grad_step.astype(bf16)
    small_ref[0:1, :] += jnp.sum(grad_step, axis=0, keepdims=True)
    small_ref[1:2, :] += jnp.sum(steps * by_decay, axis=0, keepdims=True)
    skips = jnp.sum(grad * x, axis=0, keepdims=True)
    small_ref[2:3, :] += fold(jnp.broadcast_to(skips, (8, inner)))[0:1, :]

    by_conv = steps_x * by_x + skip_ref[...] * grad
    x_pre = x_pre_ref[...]
    sig = jax.nn.sigmoid(x_pre)
    by_pre = by_conv * (sig * (1.0 + x_pre * (1.0 - sig)))
    pre_buf[0:BLOCK, :] = by_pre
    inner_in = inner_ref[...]
    grad_inner = x_taps_ref[3:4, :] * by_pre
    sums_ref[3:4, :] += jnp.sum(by_pre * inner_in, axis=0, keepdims=True)
    sums_ref[4:5, :] += jnp.sum(by_pre, axis=0, keepdims=True)
    for tap in range(CONV_WIDTH - 1):
        ahead = CONV_WIDTH - 1 - tap
        moved = pre_buf[ahead : ahead + BLOCK, :]
        grad_inner = grad_inner + x_taps_ref[tap : tap + 1, :] * moved
        sums_ref[tap : tap + 1, :] += jnp.sum(moved * inner_in, axis=0, keepdims=True)
    pre_buf[BLOCK:, :] = by_pre[0:8, :]
    grad_inner_ref[...] = grad_inner.astype(bf16)


def backward_scan(grad, inner_in, x_pre, x, bc, step_pre, cum, starts, x_taps, rate, skip, head_share, head_size):
    count, inner = grad.shape
    state2 = bc.shape[1]
    blocks = count // BLOCK
    whole = lambda a: pl.BlockSpec(a.shape, lambda i: (0,) * a.ndim)
    per = lambda width: pl.BlockSpec((BLOCK, width), lambda i: (blocks - 1 - i, 0))
    rows = (grad, inner_in, x_pre, x, bc, step_pre, cum)
    consts = (x_taps, rate, skip)
    fixed = lambda width: pl.BlockSpec((8, width), lambda i: (0, 0))
    return pl.pallas_call(
        functools.partial(backward_kernel, (head_share, head_size, LEN // BLOCK)),
        grid=(blocks,),
        in_specs=[per(a.shape[1]) for a in rows]
        + [pl.BlockSpec((1, state2 // 2, inner), lambda i: (blocks - 1 - i, 0, 0))]
        + [whole(a) for a in consts],
        out_specs=[per(inner), per(state2), per(LANES), fixed(inner), fixed(LANES)],
        out_shape=[
            jax.ShapeDtypeStruct((count, inner), bf16),
            jax.ShapeDtypeStruct((count, state2), f32),
            jax.ShapeDtypeStruct((count, LANES), bf16),
            jax.ShapeDtypeStruct((8, inner), f32),
            jax.ShapeDtypeStruct((8, LANES), f32),
        ],
        scratch_shapes=[
            pltpu.VMEM((BLOCK + 8, inner), f32),
            pltpu.VMEM((state2 // 2, inner), f32),
        ],
        compiler_params=pltpu.CompilerParams(vmem_limit_bytes=VMEM_LIMIT),
    )(*rows, starts, *consts)


def swap(value, axis, step):
    count = lax.axis_size(axis)
    return lax.ppermute(value, axis, [(i, i ^ step) for i in range(count)])


def steps_of(axis):
    count = lax.axis_size(axis)
    found = []
    while count > 1:
        count //= 2
        found.append(count)
    return found


def gather(value, axis, order):
    me = lax.axis_index(axis)
    held, done = value, []
    for step in order:
        got = swap(held, axis, step)
        bit = (me // step) % 2
        place = sum(1 for d in done if d > step)
        low = jnp.stack([held, got], axis=place)
        high = jnp.stack([got, held], axis=place)
        held = jnp.where(bit == 0, low, high)
        done.append(step)
    return held.reshape((-1,) + value.shape)


def reduce_scatter(value, axis, order):
    me = lax.axis_index(axis)
    left = sorted(order, reverse=True)
    held = value.reshape((2,) * len(left) + value.shape[1:])
    for step in order:
        place = left.index(step)
        bit = (me // step) % 2
        keep = lax.dynamic_index_in_dim(held, bit, place, keepdims=False)
        send = lax.dynamic_index_in_dim(held, 1 - bit, place, keepdims=False)
        got = swap(send.astype(bf16), axis, step)
        held = keep.astype(f32) + got.astype(f32)
        left.pop(place)
    return held


def all_sum(value, axis, order):
    for step in order:
        value = value + swap(value, axis, step)
    return value


def body(
    tokens,
    z_weight,
    x_weight,
    bc_weight,
    dt_weight,
    out_weight,
    norm_gain,
    gate_gain,
    x_conv_weight,
    x_conv_bias,
    bc_conv_weight,
    bc_conv_bias,
    step_bias,
    decay_log,
    skip_gain,
    cotangent,
):
    head_index = lax.axis_index("heads")
    head_groups = lax.axis_size("heads")
    shards = lax.axis_size("shard")
    row_count, feature_share = tokens.shape
    feature_total = feature_share * head_groups
    weight_rows, inner_share = z_weight.shape
    inner_total = inner_share * head_groups
    head_share = dt_weight.shape[1]
    head_size = inner_share // head_share
    state_width = bc_weight.shape[1]
    state_share = state_width // head_groups
    seq_count = row_count // LEN
    far = steps_of("shard")
    near = far[::-1]
    heads_far = steps_of("heads")
    heads_near = heads_far[::-1]

    step_pad = LANES - head_share
    scan_weight = jnp.concatenate(
        [x_weight, bc_weight, jnp.pad(dt_weight, ((0, 0), (0, step_pad)))], axis=1
    )
    rows_parts = gather(tokens, "heads", heads_far)
    full_rows = jnp.swapaxes(rows_parts, 0, 1).reshape(row_count, feature_total)
    whole_scan = gather(scan_weight, "shard", far).reshape(feature_total, -1)
    whole_z = gather(z_weight, "shard", far).reshape(feature_total, inner_share)
    whole_out = gather(out_weight.T, "shard", far).reshape(feature_total, inner_share)
    cot_parts = gather(cotangent, "heads", heads_far)
    full_cot = jnp.swapaxes(cot_parts, 0, 1).reshape(row_count, feature_total)

    pad_lanes = lambda v: jnp.pad(v, (0, step_pad))[None]
    rate = pad_lanes(-jnp.exp(decay_log))
    skip_x = jnp.repeat(skip_gain, head_size)[None]
    normed, inner_in, x_pre, x, state_in, s_pre, bc, step_pre, cum, starts, scanned = forward_scan(
        full_rows,
        norm_gain[None],
        whole_scan,
        x_conv_weight,
        x_conv_bias[None],
        bc_conv_weight,
        bc_conv_bias[None],
        pad_lanes(step_bias),
        rate,
        skip_x,
        head_share,
        head_size,
    )

    gate_in = dot(normed, whole_z)
    gate_sig = jax.nn.sigmoid(gate_in)
    gate_act = gate_in * gate_sig
    mixed_in = scanned * gate_act
    grad_mid = dot(full_cot, whole_out)
    grad_hat = grad_mid * gate_gain
    stats = all_sum(
        jnp.stack([jnp.sum(mixed_in * mixed_in, axis=-1), jnp.sum(grad_hat * mixed_in, axis=-1)]),
        "heads",
        heads_near,
    )
    scale_mid = lax.rsqrt(stats[0] / inner_total + epsilon)[:, None]
    mid_stat = scale_mid * stats[1][:, None]
    mid_hat = mixed_in * scale_mid
    normed_mid = (mid_hat * gate_gain).astype(bf16)
    gate_gain_grad = jnp.sum(mid_hat * grad_mid, axis=0)
    grad_mixed = scale_mid * (grad_hat - mid_hat * (mid_stat / inner_total))
    grad_scanned = grad_mixed * gate_act
    grad_gate = (grad_mixed * scanned * gate_sig * (1.0 + gate_in * (1.0 - gate_sig))).astype(bf16)

    early = jnp.concatenate([dot(normed, grad_gate, 0, 0), dot(full_cot, normed_mid, 0, 0)], axis=1)
    early_sum = reduce_scatter(
        early.astype(bf16).reshape(shards, weight_rows, 2 * inner_share), "shard", near
    )
    out_parts = dot(normed_mid, whole_out, 1, 1).astype(bf16)
    out_parts = jnp.swapaxes(out_parts.reshape(row_count, head_groups, feature_share), 0, 1)
    out_share = reduce_scatter(out_parts, "heads", heads_near)
    mixed = (tokens.astype(f32) + out_share).astype(bf16)

    grad_inner, grad_bc, grad_step, sums, small = backward_scan(
        grad_scanned,
        inner_in,
        x_pre,
        x,
        bc,
        step_pre,
        cum,
        starts,
        x_conv_weight,
        rate,
        skip_x,
        head_share,
        head_size,
    )

    state_start = head_index * state_share
    cut = lambda v: lax.dynamic_slice_in_dim(v, state_start, state_share, 1)
    bc_parts = jnp.swapaxes(grad_bc.astype(bf16).reshape(row_count, head_groups, state_share), 0, 1)
    bc_total = reduce_scatter(bc_parts, "heads", heads_near)
    own_pre = cut(s_pre)
    own_sig = jax.nn.sigmoid(own_pre)
    by_pre = bc_total * (own_sig * (1.0 + own_pre * (1.0 - own_sig)))
    by_seq = by_pre.reshape(seq_count, LEN, state_share)
    own_in = cut(state_in).reshape(seq_count, LEN, state_share)
    taps = cut(bc_conv_weight)
    ahead = jnp.pad(by_seq, ((0, 0), (0, CONV_WIDTH - 1), (0, 0)))
    grad_state = 0.0
    tap_grads = []
    for tap in range(CONV_WIDTH):
        at = CONV_WIDTH - 1 - tap
        moved = ahead[:, at : at + LEN]
        grad_state = grad_state + taps[tap] * moved
        tap_grads.append(jnp.sum(moved * own_in, axis=(0, 1)))
    tap_grads.append(jnp.sum(by_seq, axis=(0, 1)))
    grad_state = grad_state.reshape(row_count, state_share).astype(bf16)
    own_taps = lax.dynamic_update_slice(
        jnp.zeros((CONV_WIDTH + 1, state_width), f32), jnp.stack(tap_grads), (0, state_start)
    )

    grad_late = jnp.concatenate([grad_inner, grad_state, grad_step[:, :head_share]], axis=1)
    weight_late = jnp.concatenate(
        [
            whole_scan[:, :inner_share],
            lax.dynamic_slice_in_dim(whole_scan, inner_share + state_start, state_share, 1),
            whole_scan[:, inner_share + state_width : inner_share + state_width + head_share],
        ],
        axis=1,
    )
    late_sum = reduce_scatter(
        dot(normed, grad_late, 0, 0).astype(bf16).reshape(shards, weight_rows, -1), "shard", near
    )
    grad_normed = dot(grad_gate, whole_z, 1, 1) + dot(grad_late, weight_late, 1, 1)
    rows_f32 = full_rows.astype(f32)
    scale_in = lax.rsqrt(jnp.mean(rows_f32 * rows_f32, axis=-1, keepdims=True) + epsilon)
    rows_product = rows_f32 * scale_in * grad_normed
    gain_partial = jnp.sum(rows_product, axis=0)
    stat_partial = jnp.sum(rows_product * norm_gain, axis=-1)
    heads_small = all_sum(
        jnp.concatenate([gain_partial, stat_partial, own_taps.reshape(-1)]), "heads", heads_near
    )
    normed_parts = jnp.swapaxes(
        grad_normed.astype(bf16).reshape(row_count, head_groups, feature_share), 0, 1
    )
    grad_share = reduce_scatter(normed_parts, "heads", heads_near)
    gain_share = lax.dynamic_slice_in_dim(norm_gain, head_index * feature_share, feature_share, 0)
    norm_stat = heads_small[feature_total : feature_total + row_count]
    tokens_hat = tokens.astype(f32) * scale_in
    tokens_grad = (
        cotangent.astype(f32)
        + scale_in * (grad_share * gain_share - tokens_hat * (norm_stat / feature_total)[:, None])
    ).astype(bf16)

    pieces = [
        lax.dynamic_slice_in_dim(heads_small, head_index * feature_share, feature_share, 0),
        gate_gain_grad,
        sums[:CONV_WIDTH].reshape(-1),
        sums[CONV_WIDTH],
        heads_small[feature_total + row_count :],
        small[0, :head_share],
        small[1, :head_share],
        small[2, :head_share],
    ]
    summed = all_sum(jnp.concatenate(pieces), "shard", near)
    cuts, at = [], 0
    for piece in pieces:
        cuts.append(summed[at : at + piece.shape[0]])
        at += piece.shape[0]
    bc_taps = cuts[4].reshape(CONV_WIDTH + 1, state_width)
    offset_bc = inner_share + state_share
    return (
        mixed,
        tokens_grad,
        early_sum[:, :inner_share],
        late_sum[:, :inner_share],
        late_sum[:, inner_share:offset_bc],
        late_sum[:, offset_bc:],
        early_sum[:, inner_share:].T,
        cuts[0],
        cuts[1],
        cuts[2].reshape(CONV_WIDTH, inner_share),
        cuts[3],
        bc_taps[:CONV_WIDTH],
        bc_taps[CONV_WIDTH],
        cuts[5].astype(f32),
        cuts[6] * rate[0, :head_share],
        cuts[7],
    )


def solution(mesh):
    placed = (
        P("shard", "heads"),
        P("shard", "heads"),
        P("shard", "heads"),
        P("shard", None),
        P("shard", "heads"),
        P("heads", "shard"),
        P(),
        P("heads"),
        P(None, "heads"),
        P("heads"),
        P(),
        P(),
        P("heads"),
        P("heads"),
        P("heads"),
        P("shard", "heads"),
    )
    return jax.shard_map(
        body,
        mesh=mesh,
        in_specs=placed,
        out_specs=(
            P("shard", "heads"),
            P("shard", "heads"),
            P("shard", "heads"),
            P("shard", "heads"),
            P("shard", "heads"),
            P("shard", "heads"),
            P("heads", "shard"),
            P("heads"),
            P("heads"),
            P(None, "heads"),
            P("heads"),
            P(),
            P(),
            P("heads"),
            P("heads"),
            P("heads"),
        ),
        check_vma=False,
    )
```

time: 632 us -> 249 us (0.39); the launches traced: 620 us -> 245 us
  waiting for transfers between devices: 224 us -> 74.4 us
  blocking collectives: 115 us -> 0 us
  matrix products: 117 us -> 19.4 us
  Pallas kernels: 0 us -> 41.1 us
  local copies, waits for them, and re-layouts: 82.5 us -> 42.3 us
  other arithmetic: 65.2 us -> 27.7 us
  starting transfers between devices: 0.56 us -> 37.9 us
  between operations: 14.8 us -> 1.99 us
    reduce_scatter x3 -> x0, waiting for transfers between devices: 155 us -> none  [the longest x1 124 us: body(): lax.psum_scatter(jnp.concatenate([contract_first(normed, grad_joined), co...]
    dot_general x65 -> x8, matrix products: 117 us -> 19.4 us  [dot(): lax.dot_general(left, right, (((left_dim,), (right_dim,)), ((), ())), pre...]
    ppermute x0 -> x32, waiting for transfers between devices: none -> 74.4 us  [swap(): return lax.ppermute(value, axis, [(i, i ^ step) for i in range(count)])]
    all_gather x2 -> x0, blocking collectives: 59.5 us -> none  [the longest x1 33.5 us: body(): lax.all_gather(bc_weight, 'shard', axis=0, tiled=True)]
    psum x4 -> x0, blocking collectives: 55.3 us -> none  [the longest x1 37.7 us: body(): lax.psum((norm_gain_grad, gate_gain_grad, x_conv_weight_grad, x_conv_bias...]
    all_gather x5 -> x0, waiting for transfers between devices: 43.1 us -> none  [the longest x1 24.6 us: body(): lax.all_gather(z_weight, 'shard', axis=0, tiled=True)]
    pallas_call x0 -> x2, Pallas kernels: none -> 41.1 us  [the longest x1 25 us: backward_scan(): pl.pallas_call(functools.partial(backward_kernel, (head_share, head_size,...]
    ppermute x0 -> x32, starting transfers between devices: none -> 37.9 us  [swap(): return lax.ppermute(value, axis, [(i, i ^ step) for i in range(count)])]
  transfers between devices with their start and end apart: 9 -> 32, of which waited for: 6 -> 18; matrix products, arithmetic and copies ran while one was open for 19% -> 29% of each run, Pallas kernels for 0% -> 0%
where the time goes in v1:
time: 249 us; the launch traced here: 245 us
  waiting for transfers between devices  74.4 us (30%)
  local copies, waits for them, and re-layouts  42.3 us (17%)
  Pallas kernels  41.1 us (17%)
  starting transfers between devices  37.9 us (15%)
  other arithmetic  27.7 us (11%)
  matrix products  19.4 us (8%)
    ppermute x32, waiting for transfers between devices, swap(): return lax.ppermute(value, axis, [(i, i ^ step) for i in range(count)])  74.4 us
    ppermute x32, starting transfers between devices, swap(): return lax.ppermute(value, axis, [(i, i ^ step) for i in range(count)])  37.9 us
    pallas_call x1, Pallas kernels, backward_scan(): pl.pallas_call(functools.partial(backward_kernel, (head_share, head_size,...  25 us
    dot_general x8, matrix products, dot(): lax.dot_general(left, right, (((left_dim,), (right_dim,)), ((), ())), pre...  19.4 us
    pallas_call x1, Pallas kernels, forward_scan(): pl.pallas_call(functools.partial(forward_kernel, (head_share, head_size,...  16.1 us
    add x9, other arithmetic, reduce_scatter(): held = keep.astype(f32) + got.astype(f32)  8.52 us
    select_n x21, other arithmetic, gather(): held = jnp.where(bit == 0, low, high)  7.21 us
    unnamed x87, local copies, waits for them, and re-layouts  5.97 us
  transfers between devices with their start and end apart: 32, of which 18 were waited for; matrix products, arithmetic and copies ran while one was open for 29% of the time, Pallas kernels for 0%

profile of v1, /device:TPU:0, one launch (start us, length us, event | category | flops | bytes accessed | tf_op | source)
XLA Modules:
  0.0 244.6 jit_solution(14351541473210772396)
XLA Ops:
  0.7 3.0 %collective-permute-start = (bf16[1024,256]{1,0:T(8,128)(2,1)}, bf16[1024,256]{1,0:T(8,128)(2,1)S(1)}, u32[]{:S(2)}, u32[]{:S(2)}) collective-permute-start(bf16[1024,256]{1,0:T(8,128)(2,1)} %param.16), channel_id=1, source_target_pairs={{0,2},{1,3},{2,0},{3,1},{4,6},{5,7},{6,4},{7,5},{8,10},{9,11},{10,... | collective-permute-start | bytes 1572872 | tf_op jit(solution)/shard_map/ppermute | solution.py:355
  5.5 2.7 %collective-permute-start.2 = (bf16[128,896]{1,0:T(8,128)(2,1)S(1)}, bf16[128,896]{1,0:T(8,128)(2,1)S(1)}, u32[]{:S(2)}, u32[]{:S(2)}) collective-permute-start(bf16[128,896]{1,0:T(8,128)(2,1)S(1)} %get-tuple-element.124), channel_id=1, source_target_pairs={{0,16},{4,20},{8,24},{12,28},{16,0},{20,4},{24,8},{28,12},{1,17},{... | collective-permute-start | bytes 688136 | tf_op jit(solution)/shard_map/ppermute | solution.py:355
  9.7 2.9 %collective-permute-start.10 = (bf16[128,512]{1,0:T(8,128)(2,1)S(1)}, bf16[128,512]{1,0:T(8,128)(2,1)S(1)}, u32[]{:S(2)}, u32[]{:S(2)}) collective-permute-start(bf16[128,512]{1,0:T(8,128)(2,1)S(1)} %bitcast.254), channel_id=1, source_target_pairs={{0,16},{4,20},{8,24},{12,28},{16,0},{20,4},{24,8},{28,12},{1,17},{... | collective-permute-start | bytes 393224 | tf_op jit(solution)/shard_map/ppermute | solution.py:355
  16.3 11.7 %collective-permute-done.5 = bf16[128,512]{1,0:T(8,128)(2,1)S(1)} collective-permute-done((bf16[128,512]{1,0:T(8,128)(2,1)}, bf16[128,512]{1,0:T(8,128)(2,1)S(1)}, u32[]{:S(2)}, u32[]{:S(2)}) %collective-permute-start.5) | collective-permute-done | bytes 131104 | tf_op jit(solution)/shard_map/ppermute | solution.py:355
  32.2 6.2 %collective-permute-done.6 = bf16[2,128,512]{2,1,0:T(8,128)(2,1)S(1)} collective-permute-done((bf16[2,128,512]{2,1,0:T(8,128)(2,1)S(1)}, bf16[2,128,512]{2,1,0:T(8,128)(2,1)S(1)}, u32[]{:S(2)}, u32[]{:S(2)}) %collective-permute-start.6) | collective-permute-done | bytes 262176 | tf_op jit(solution)/shard_map/ppermute | solution.py:355
  40.0 4.0 %collective-permute-done.11 = bf16[2,128,512]{2,1,0:T(8,128)(2,1)S(1)} collective-permute-done((bf16[2,128,512]{2,1,0:T(8,128)(2,1)S(1)}, bf16[2,128,512]{2,1,0:T(8,128)(2,1)S(1)}, u32[]{:S(2)}, u32[]{:S(2)}) %collective-permute-start.11) | collective-permute-done | bytes 262176 | tf_op jit(solution)/shard_map/ppermute | solution.py:355
  47.5 3.3 %collective-permute-done.3 = bf16[2,128,896]{2,1,0:T(8,128)(2,1)S(1)} collective-permute-done((bf16[2,128,896]{2,1,0:T(8,128)(2,1)S(1)}, bf16[2,128,896]{2,1,0:T(8,128)(2,1)S(1)}, u32[]{:S(2)}, u32[]{:S(2)}) %collective-permute-start.3) | collective-permute-done | bytes 458784 | tf_op jit(solution)/shard_map/ppermute | solution.py:355
  53.5 10.7 %collective-permute-done.12 = bf16[2,2,128,512]{3,2,0,1:T(8,128)(2,1)S(1)} collective-permute-done((bf16[2,2,128,512]{3,2,0,1:T(8,128)(2,1)S(1)}, bf16[2,2,128,512]{3,2,0,1:T(8,128)(2,1)S(1)}, u32[]{:S(2)}, u32[]{:S(2)}) %collective-permute-start.12) | collective-permute-done | bytes 524320 | tf_op jit(solution)/shard_map/ppermute | solution.py:355
  70.4 4.1 %copy.93 = bf16[1024,4,256]{0,2,1:T(8,128)(2,1)} copy(bf16[1024,4,256]{2,0,1:T(8,128)(2,1)} %bitcast.242) | data formatting | bytes 4194304 | tf_op jit(solution)/shard_map/transpose | solution.py:447
  75.1 3.1 %collective-permute-done.4 = bf16[2,2,128,896]{3,2,0,1:T(8,128)(2,1)} collective-permute-done((bf16[2,2,128,896]{3,2,0,1:T(8,128)(2,1)}, bf16[2,2,128,896]{3,2,0,1:T(8,128)(2,1)}, u32[]{:S(2)}, u32[]{:S(2)}) %collective-permute-start.4) | collective-permute-done | bytes 917536 | tf_op jit(solution)/shard_map/ppermute | solution.py:355
  81.5 16.1 %shard_map.279 = (bf16[1024,1024]{1,0:T(8,128)(2,1)}, f32[1024,512]{1,0:T(8,128)}, f32[1024,512]{1,0:T(8,128)}, bf16[1024,512]{1,0:T(8,128)(2,1)S(1)}, f32[1024,...) custom-call(bf16[1024,1024]{1,0:T(8,128)(2,1)} %bitcast.240, ...), custom_call_target="tpu_custom_call" | custom-call | tf_op jit(solution)/shard_map/pallas_call | solution.py:168
  97.6 3.2 %fusion.52 = f32[1024,512]{1,0:T(8,128)S(1)} fusion(bf16[1024,1024]{1,0:T(8,128)(2,1)} %get-tuple-element.33, bf16[1024,512]{1,0:T(8,128)(2,1)S(1)} %bitcast.279), kind=kOutput, calls=%fused_computation.150 | convolution fusion | flops 1073741824 | bytes 5242880 | tf_op jit(solution)/shard_map/dot_general | solution.py:23
  101.0 1.8 multiply_reduce_fusion.4
  107.9 2.7 %convolution_convert_fusion = bf16[1024,1024]{0,1:T(8,128)(2,1)} fusion(bf16[1024,512]{1,0:T(8,128)(2,1)S(1)} %bitcast.282, f32[1024,512]{1,0:T(8,128)S(1)} %get-tuple-element.106, f32[1024]{0:T(1024)S(1)} %bitcast.291, f32[512]{0:T(512)S(1)} %copy-done.37), kind=kOutput, calls=%fused_computation.24 | convolution fusion | flops 1076363264 | bytes 5249024 | tf_op jit(solution)/shard_map/dot_general | solution.py:23
  110.7 2.9 %multiply_convert_fusion = (bf16[1024,512]{1,0:T(8,128)(2,1)}, f32[1024,512]{1,0:T(8,128)}, f32[512]{0:T(512)S(1)}) fusion(f32[1024,512]{1,0:T(8,128)S(1)} %fusion.52, f32[1024,512]{1,0:T(8,128)S(1)} %copy-done.26, f32[1024]{0:T(1024)S(1)} %multiply_multiply_fusion.1, f32[1024,512]{1,0:T(8,128)S(1)} %get-tuple-element.106, ...), kind=kLoop, calls=%fused_computation.16 | loop fusion | flops 9960960 | bytes 11546624 | tf_op jit(solution)/shard_map/convert_element_type | solution.py:485
  113.5 25.0 %shard_map.280 = (bf16[1024,512]{1,0:T(8,128)(2,1)S(1)}, f32[1024,256]{1,0:T(8,128)S(1)}, bf16[1024,128]{1,0:T(8,128)(2,1)S(1)}, f32[8,512]{1,0:T(8,128)S(1)}, f32[8,128]{1,0:T(8,128)S(1)}) custom-call(f32[1024,512]{1,0:T(8,128)} %get-tuple-element.108.grad_ref, f32[1024,512]{1,0:T(8,128)} %get-tuple-element.34.inner_ref, ...), custom_call_target="tpu_custom_call" | custom-call | tf_op jit(solution)/shard_map/pallas_call | solution.py:331
  141.2 3.9 %copy.96 = bf16[1024,4,256]{2,0,1:T(8,128)(2,1)} copy(bf16[1024,4,256]{0,2,1:T(8,128)(2,1)} %bitcast.261) | data formatting | bytes 4194304 | tf_op jit(solution)/shard_map/reshape | solution.py:492
  145.1 2.5 %dynamic-slice_bitcast_fusion.1 = bf16[2,1024,256]{2,1,0:T(8,128)(2,1)} fusion(bf16[2,2,1024,256]{3,2,1,0:T(8,128)(2,1)} %bitcast.236, s32[]{:T(128)S(6)} %select_n.432), kind=kLoop, calls=%fused_computation.65 | loop fusion | bytes 2097156 | tf_op jit(solution)/shard_map/jit(dynamic_index_in_dim)/squeeze | solution.py:389
  148.1 3.1 %convolution_convert_fusion.2 = bf16[2,2,2,128,512]{4,3,2,1,0:T(8,128)(2,1)S(1)} fusion(bf16[2,2,2,128,1024]{4,3,2,1,0:T(8,128)(2,1)S(1)} %bitcast.260, f32[1024,512]{1,0:T(8,128)} %copy-done.25, f32[1024]{0:T(1024)S(1)} %bitcast.293, f32[512]{0:T(512)S(1)} %copy-done.37), kind=kOutput, calls=%fused_computation.27 | convolution fusion | flops 1075838976 | bytes 5249024 | tf_op jit(solution)/shard_map/dot_general | solution.py:23
  157.6 7.0 %collective-permute-done.18 = bf16[1024,64]{1,0:T(8,128)(2,1)S(1)} collective-permute-done((bf16[1024,64]{1,0:T(8,128)(2,1)S(1)}, bf16[1024,64]{1,0:T(8,128)(2,1)S(1)}, u32[]{:S(2)}, u32[]{:S(2)}) %collective-permute-start.18) | collective-permute-done | bytes 131104 | tf_op jit(solution)/shard_map/ppermute | solution.py:355
  166.8 3.1 %fusion.2 = f32[1024,1024]{1,0:T(8,128)S(1)} fusion(bf16[1024,8]{1,0:T(8,128)(2,1)} %slice.150, bf16[1024,64]{1,0:T(8,128)(2,1)} %constant_dynamic-slice_fusion.2, bf16[1024,512]{1,0:T(8,128)(2,1)S(1)} %copy-done.33, bf16[1024,8]{1,0:T(8,128)(2,1)S(1)} %bitcast.229, bf16[1024,64]{1,0:T(8,128)(2,1)} %get-tuple-element.117, ...), kind=kOutput, calls=%fused_computation.32 | convolution fusion | flops 1231912960 | bytes 6586368 | tf_op jit(solution)/shard_map/dot_general | solution.py:23
  173.8 2.5 %convolution_convert_fusion.1 = bf16[1024,584]{0,1:T(8,128)(2,1)} fusion(bf16[1024,1024]{1,0:T(8,128)(2,1)S(1)} %copy-done.39, bf16[1024,8]{1,0:T(8,128)(2,1)S(1)} %bitcast.230, bf16[1024,64]{1,0:T(8,128)(2,1)S(1)} %copy-done.35, bf16[1024,512]{1,0:T(8,128)(2,1)S(1)} %get-tuple-element.41), kind=kOutput, calls=%fused_computation.26 | convolution fusion | flops 1228922880 | bytes 4489216 | tf_op jit(solution)/shard_map/dot_general | solution.py:23
  180.5 2.5 %collective-permute-start.30 = (f32[4632]{0:T(1024)S(1)}, f32[4632]{0:T(1024)S(1)}, u32[]{:S(2)}, u32[]{:S(2)}) collective-permute-start(f32[4632]{0:T(1024)S(1)} %add.286), channel_id=1, source_target_pairs={{0,8},{4,12},{8,0},{12,4},{16,24},{20,28},{24,16},{28,20},{1,9},{5... | collective-permute-start | bytes 55592 | tf_op jit(solution)/shard_map/ppermute | solution.py:355
  183.0 2.5 %constant_dynamic-slice_fusion.1 = (bf16[2,2,1,128,584]{3,2,1,0,4:T(2,128)(2,1)S(1)}, bf16[2,2,1,128,584]{3,2,1,0,4:T(2,128)(2,1)S(1)}) fusion(bf16[2,2,2,128,584]{3,2,1,0,4:T(2,128)(2,1)S(1)} %reshape_reshape.2, s32[]{:T(128)S(6)} %select_n.438, s32[]{:T(128)S(6)} %select_n.439), kind=kLoop, calls=%fused_computation.117 | loop fusion | bytes 2392072 | tf_op jit(solution)/shard_map/jit(dynamic_index_in_dim)/dynamic_slice | solution.py:388
  187.0 3.7 %collective-permute-start.31 = (f32[4632]{0:T(1024)S(1)}, f32[4632]{0:T(1024)S(1)}, u32[]{:S(2)}, u32[]{:S(2)}) collective-permute-start(f32[4632]{0:T(1024)S(1)} %add.287), channel_id=1, source_target_pairs={{0,16},{4,20},{8,24},{12,28},{16,0},{20,4},{24,8},{28,12},{1,17},{... | collective-permute-start | bytes 55592 | tf_op jit(solution)/shard_map/ppermute | solution.py:355
  190.7 2.0 collective-permute-done.31
  195.6 5.5 %collective-permute-done.26 = bf16[2,2,128,584]{2,3,0,1:T(8,128)(2,1)} collective-permute-done((bf16[2,2,128,584]{2,3,0,1:T(8,128)(2,1)}, bf16[2,2,128,584]{2,3,0,1:T(8,128)(2,1)}, u32[]{:S(2)}, u32[]{:S(2)}) %collective-permute-start.26) | collective-permute-done | bytes 598048 | tf_op jit(solution)/shard_map/ppermute | solution.py:355
  210.6 3.6 %collective-permute-start.28 = (bf16[128,584]{0,1:T(8,128)(2,1)S(1)}, bf16[128,584]{0,1:T(8,128)(2,1)S(1)}, u32[]{:S(2)}, u32[]{:S(2)}) collective-permute-start(bf16[128,584]{0,1:T(8,128)(2,1)S(1)} %fusion.36), channel_id=1, source_target_pairs={{0,16},{4,20},{8,24},{12,28},{16,0},{20,4},{24,8},{28,12},{1,17},{... | collective-permute-start | bytes 448520 | tf_op jit(solution)/shard_map/ppermute | solution.py:355
  215.8 8.2 %collective-permute-done.24 = bf16[2,128,1024]{2,1,0:T(8,128)(2,1)S(1)} collective-permute-done((bf16[2,128,1024]{2,1,0:T(8,128)(2,1)S(1)}, bf16[2,128,1024]{2,1,0:T(8,128)(2,1)S(1)}, u32[]{:S(2)}, u32[]{:S(2)}) %collective-permute-start.24) | collective-permute-done | bytes 524320 | tf_op jit(solution)/shard_map/ppermute | solution.py:355
  225.0 2.0 collective-permute-start.25
  231.0 7.4 %collective-permute-done.25 = bf16[128,1024]{1,0:T(8,128)(2,1)} collective-permute-done((bf16[128,1024]{1,0:T(8,128)(2,1)}, bf16[128,1024]{1,0:T(8,128)(2,1)}, u32[]{:S(2)}, u32[]{:S(2)}) %collective-permute-start.25) | collective-permute-done | bytes 262176 | tf_op jit(solution)/shard_map/ppermute | solution.py:355
  241.2 3.0 %fusion.13 = (bf16[1024,256]{1,0:T(8,128)(2,1)}, bf16[1024,256]{1,0:T(8,128)(2,1)}) fusion(bf16[1024,256]{1,0:T(8,128)(2,1)S(1)} %copy-done.15, bf16[1024,256]{1,0:T(8,128)(2,1)} %collective-permute-done.20, f32[2,1024,256]{2,1,0:T(8,128)} %copy-done.13, s32[]{:T(128)S(6)} %select_n.433, bf16[1024,256]{1,0:T(8,128)(2,1)S(1)} %copy-done.17, ...), kind=kLoop, calls=%fused_computation.44 | loop fusion | flops 3932160 | bytes 5252100 | tf_op jit(solution)/shard_map/convert_element_type | solution.py:567
  (236 shorter events, 76.7 us)
Async XLA Ops:
  0.7 45.1 %collective-permute-start = (bf16[1024,256]{1,0:T(8,128)(2,1)}, bf16[1024,256]{1,0:T(8,128)(2,1)S(1)}, u32[]{:S(2)}, u32[]{:S(2)}) collective-permute-start(bf16[1024,256]{1,0:T(8,128)(2,1)} %param.16), channel_id=1, source_target_pairs={{0,2},{1,3},{2,0},{3,1},{4,6},{5,7},{6,4},{7,5},{8,10},{9,11},{10,... | collective-permute-start | bytes 1572872 | tf_op jit(solution)/shard_map/ppermute | solution.py:355
  5.5 25.9 %collective-permute-start.2 = (bf16[128,896]{1,0:T(8,128)(2,1)S(1)}, bf16[128,896]{1,0:T(8,128)(2,1)S(1)}, u32[]{:S(2)}, u32[]{:S(2)}) collective-permute-start(bf16[128,896]{1,0:T(8,128)(2,1)S(1)} %get-tuple-element.124), channel_id=1, source_target_pairs={{0,16},{4,20},{8,24},{12,28},{16,0},{20,4},{24,8},{28,12},{1,17},{... | collective-permute-start | bytes 688136 | tf_op jit(solution)/shard_map/ppermute | solution.py:355
  8.1 19.9 %collective-permute-start.5 = (bf16[128,512]{1,0:T(8,128)(2,1)}, bf16[128,512]{1,0:T(8,128)(2,1)S(1)}, u32[]{:S(2)}, u32[]{:S(2)}) collective-permute-start(bf16[128,512]{1,0:T(8,128)(2,1)} %param.17), channel_id=1, source_target_pairs={{0,16},{4,20},{8,24},{12,28},{16,0},{20,4},{24,8},{28,12},{1,17},{... | collective-permute-start | bytes 393224 | tf_op jit(solution)/shard_map/ppermute | solution.py:355
  8.5 37.6 %collective-permute-start.8 = (bf16[1024,256]{1,0:T(8,128)(2,1)}, bf16[1024,256]{1,0:T(8,128)(2,1)S(1)}, u32[]{:S(2)}, u32[]{:S(2)}) collective-permute-start(bf16[1024,256]{1,0:T(8,128)(2,1)} %param.31), channel_id=1, source_target_pairs={{0,2},{1,3},{2,0},{3,1},{4,6},{5,7},{6,4},{7,5},{8,10},{9,11},{10,... | collective-permute-start | bytes 1572872 | tf_op jit(solution)/shard_map/ppermute | solution.py:355
  9.7 19.9 %collective-permute-start.10 = (bf16[128,512]{1,0:T(8,128)(2,1)S(1)}, bf16[128,512]{1,0:T(8,128)(2,1)S(1)}, u32[]{:S(2)}, u32[]{:S(2)}) collective-permute-start(bf16[128,512]{1,0:T(8,128)(2,1)S(1)} %bitcast.254), channel_id=1, source_target_pairs={{0,16},{4,20},{8,24},{12,28},{16,0},{20,4},{24,8},{28,12},{1,17},{... | collective-permute-start | bytes 393224 | tf_op jit(solution)/shard_map/ppermute | solution.py:355
  29.0 9.3 %collective-permute-start.6 = (bf16[2,128,512]{2,1,0:T(8,128)(2,1)S(1)}, bf16[2,128,512]{2,1,0:T(8,128)(2,1)S(1)}, u32[]{:S(2)}, u32[]{:S(2)}) collective-permute-start(bf16[2,128,512]{2,1,0:T(8,128)(2,1)S(1)} %maximum_select_fusion.15), channel_id=1, source_target_pairs={{0,8},{4,12},{8,0},{12,4},{16,24},{20,28},{24,16},{28,20},{1,9},{5... | collective-permute-start | bytes 786440 | tf_op jit(solution)/shard_map/ppermute | solution.py:355
  29.7 14.3 %collective-permute-start.11 = (bf16[2,128,512]{2,1,0:T(8,128)(2,1)S(1)}, bf16[2,128,512]{2,1,0:T(8,128)(2,1)S(1)}, u32[]{:S(2)}, u32[]{:S(2)}) collective-permute-start(bf16[2,128,512]{2,1,0:T(8,128)(2,1)S(1)} %maximum_select_fusion.17), channel_id=1, source_target_pairs={{0,8},{4,12},{8,0},{12,4},{16,24},{20,28},{24,16},{28,20},{1,9},{5... | collective-permute-start | bytes 786440 | tf_op jit(solution)/shard_map/ppermute | solution.py:355
  31.5 19.3 %collective-permute-start.3 = (bf16[2,128,896]{2,1,0:T(8,128)(2,1)S(1)}, bf16[2,128,896]{2,1,0:T(8,128)(2,1)S(1)}, u32[]{:S(2)}, u32[]{:S(2)}) collective-permute-start(bf16[2,128,896]{2,1,0:T(8,128)(2,1)S(1)} %maximum_select_fusion.14), channel_id=1, source_target_pairs={{0,8},{4,12},{8,0},{12,4},{16,24},{20,28},{24,16},{28,20},{1,9},{5... | collective-permute-start | bytes 1376264 | tf_op jit(solution)/shard_map/ppermute | solution.py:355
  38.4 27.1 %collective-permute-start.7 = (bf16[2,2,128,512]{3,2,1,0:T(8,128)(2,1)S(1)}, bf16[2,2,128,512]{3,2,1,0:T(8,128)(2,1)S(1)}, u32[]{:S(2)}, u32[]{:S(2)}) collective-permute-start(bf16[2,2,128,512]{3,2,1,0:T(8,128)(2,1)S(1)} %maximum_select_fusion.10), channel_id=1, source_target_pairs={{0,4},{4,0},{8,12},{12,8},{16,20},{20,16},{24,28},{28,24},{1,5},{5... | collective-permute-start | bytes 1572872 | tf_op jit(solution)/shard_map/ppermute | solution.py:355
  44.1 20.2 %collective-permute-start.12 = (bf16[2,2,128,512]{3,2,0,1:T(8,128)(2,1)S(1)}, bf16[2,2,128,512]{3,2,0,1:T(8,128)(2,1)S(1)}, u32[]{:S(2)}, u32[]{:S(2)}) collective-permute-start(bf16[2,2,128,512]{3,2,0,1:T(8,128)(2,1)S(1)} %maximum_select_fusion.12), channel_id=1, source_target_pairs={{0,4},{4,0},{8,12},{12,8},{16,20},{20,16},{24,28},{28,24},{1,5},{5... | collective-permute-start | bytes 1572872 | tf_op jit(solution)/shard_map/ppermute | solution.py:355
  46.0 20.6 %collective-permute-start.1 = (bf16[2,1024,256]{2,1,0:T(8,128)(2,1)S(1)}, bf16[2,1024,256]{2,1,0:T(8,128)(2,1)S(1)}, u32[]{:S(2)}, u32[]{:S(2)}) collective-permute-start(bf16[2,1024,256]{2,1,0:T(8,128)(2,1)S(1)} %maximum_select_fusion.3), channel_id=1, source_target_pairs={{0,1},{1,0},{2,3},{3,2},{4,5},{5,4},{6,7},{7,6},{8,9},{9,8},{10,11... | collective-permute-start | bytes 3145736 | tf_op jit(solution)/shard_map/ppermute | solution.py:355
  46.9 21.7 %collective-permute-start.9 = (bf16[2,1024,256]{2,1,0:T(8,128)(2,1)S(1)}, bf16[2,1024,256]{2,1,0:T(8,128)(2,1)S(1)}, u32[]{:S(2)}, u32[]{:S(2)}) collective-permute-start(bf16[2,1024,256]{2,1,0:T(8,128)(2,1)S(1)} %maximum_select_fusion.6), channel_id=1, source_target_pairs={{0,1},{1,0},{2,3},{3,2},{4,5},{5,4},{6,7},{7,6},{8,9},{9,8},{10,11... | collective-permute-start | bytes 3145736 | tf_op jit(solution)/shard_map/ppermute | solution.py:355
  51.8 26.3 %collective-permute-start.4 = (bf16[2,2,128,896]{3,2,0,1:T(8,128)(2,1)}, bf16[2,2,128,896]{3,2,0,1:T(8,128)(2,1)}, u32[]{:S(2)}, u32[]{:S(2)}) collective-permute-start(bf16[2,2,128,896]{3,2,0,1:T(8,128)(2,1)} %maximum_select_fusion.9), channel_id=1, source_target_pairs={{0,4},{4,0},{8,12},{12,8},{16,20},{20,16},{24,28},{28,24},{1,5},{5... | collective-permute-start | bytes 2752520 | tf_op jit(solution)/shard_map/ppermute | solution.py:355
  102.9 1.2 collective-permute-start.13
  104.2 3.7 %collective-permute-start.14 = (f32[2,1024]{1,0:T(2,128)S(1)}, f32[2,1024]{1,0:T(2,128)S(1)}, u32[]{:S(2)}, u32[]{:S(2)}) collective-permute-start(f32[2,1024]{1,0:T(2,128)S(1)} %fusion.42), channel_id=1, source_target_pairs={{0,2},{1,3},{2,0},{3,1},{4,6},{5,7},{6,4},{7,5},{8,10},{9,11},{10,... | collective-permute-start | bytes 24584 | tf_op jit(solution)/shard_map/ppermute | solution.py:355
  139.9 15.4 %collective-permute-start.17 = (bf16[2,1024,64]{2,1,0:T(8,128)(2,1)S(1)}, bf16[2,1024,64]{2,1,0:T(8,128)(2,1)}, u32[]{:S(2)}, u32[]{:S(2)}) collective-permute-start(bf16[2,1024,64]{2,1,0:T(8,128)(2,1)S(1)} %bitcast.289), channel_id=1, source_target_pairs={{0,1},{1,0},{2,3},{3,2},{4,5},{5,4},{6,7},{7,6},{8,9},{9,8},{10,11... | collective-permute-start | bytes 786440 | tf_op jit(solution)/shard_map/ppermute | solution.py:355
  147.6 55.2 %collective-permute-start.15 = (bf16[2,1024,256]{2,1,0:T(8,128)(2,1)}, bf16[2,1024,256]{2,1,0:T(8,128)(2,1)}, u32[]{:S(2)}, u32[]{:S(2)}) collective-permute-start(bf16[2,1024,256]{2,1,0:T(8,128)(2,1)} %dynamic-slice_bitcast_fusion.1), channel_id=1, source_target_pairs={{0,1},{1,0},{2,3},{3,2},{4,5},{5,4},{6,7},{7,6},{8,9},{9,8},{10,11... | collective-permute-start | bytes 3145736 | tf_op jit(solution)/shard_map/ppermute | solution.py:355
  153.8 52.6 %collective-permute-start.23 = (bf16[2,2,128,1024]{3,2,1,0:T(8,128)(2,1)}, bf16[2,2,128,1024]{3,2,1,0:T(8,128)(2,1)}, u32[]{:S(2)}, u32[]{:S(2)}) collective-permute-start(bf16[2,2,128,1024]{3,2,1,0:T(8,128)(2,1)} %fusion.15), channel_id=1, source_target_pairs={{0,4},{4,0},{8,12},{12,8},{16,20},{20,16},{24,28},{28,24},{1,5},{5... | collective-permute-start | bytes 3145736 | tf_op jit(solution)/shard_map/ppermute | solution.py:355
  156.5 8.0 %collective-permute-start.18 = (bf16[1024,64]{1,0:T(8,128)(2,1)S(1)}, bf16[1024,64]{1,0:T(8,128)(2,1)S(1)}, u32[]{:S(2)}, u32[]{:S(2)}) collective-permute-start(bf16[1024,64]{1,0:T(8,128)(2,1)S(1)} %fusion.32), channel_id=1, source_target_pairs={{0,2},{1,3},{2,0},{3,1},{4,6},{5,7},{6,4},{7,5},{8,10},{9,11},{10,... | collective-permute-start | bytes 393224 | tf_op jit(solution)/shard_map/ppermute | solution.py:355
  171.6 1.2 collective-permute-start.21
  172.8 3.7 %collective-permute-start.22 = (f32[3328]{0:T(1024)S(1)}, f32[3328]{0:T(1024)S(1)}, u32[]{:S(2)}, u32[]{:S(2)}) collective-permute-start(f32[3328]{0:T(1024)S(1)} %fusion.41), channel_id=1, source_target_pairs={{0,2},{1,3},{2,0},{3,1},{4,6},{5,7},{6,4},{7,5},{8,10},{9,11},{10,... | collective-permute-start | bytes 39944 | tf_op jit(solution)/shard_map/ppermute | solution.py:355
  176.8 3.8 %collective-permute-start.29 = (f32[4632]{0:T(1024)S(1)}, f32[4632]{0:T(1024)S(1)}, u32[]{:S(2)}, u32[]{:S(2)}) collective-permute-start(f32[4632]{0:T(1024)S(1)} %concatenate.194), channel_id=1, source_target_pairs={{0,4},{4,0},{8,12},{12,8},{16,20},{20,16},{24,28},{28,24},{1,5},{5... | collective-permute-start | bytes 55592 | tf_op jit(solution)/shard_map/ppermute | solution.py:355
  178.4 35.9 %collective-permute-start.19 = (bf16[2,1024,256]{2,1,0:T(8,128)(2,1)}, bf16[2,1024,256]{2,1,0:T(8,128)(2,1)}, u32[]{:S(2)}, u32[]{:S(2)}) collective-permute-start(bf16[2,1024,256]{2,1,0:T(8,128)(2,1)} %dynamic-slice_bitcast_fusion), channel_id=1, source_target_pairs={{0,1},{1,0},{2,3},{3,2},{4,5},{5,4},{6,7},{7,6},{8,9},{9,8},{10,11... | collective-permute-start | bytes 3145736 | tf_op jit(solution)/shard_map/ppermute | solution.py:355
  180.5 6.4 %collective-permute-start.30 = (f32[4632]{0:T(1024)S(1)}, f32[4632]{0:T(1024)S(1)}, u32[]{:S(2)}, u32[]{:S(2)}) collective-permute-start(f32[4632]{0:T(1024)S(1)} %add.286), channel_id=1, source_target_pairs={{0,8},{4,12},{8,0},{12,4},{16,24},{20,28},{24,16},{28,20},{1,9},{5... | collective-permute-start | bytes 55592 | tf_op jit(solution)/shard_map/ppermute | solution.py:355
  186.4 14.7 %collective-permute-start.26 = (bf16[2,2,128,584]{2,3,0,1:T(8,128)(2,1)}, bf16[2,2,128,584]{2,3,0,1:T(8,128)(2,1)}, u32[]{:S(2)}, u32[]{:S(2)}) collective-permute-start(bf16[2,2,128,584]{2,3,0,1:T(8,128)(2,1)} %bitcast.224), channel_id=1, source_target_pairs={{0,4},{4,0},{8,12},{12,8},{16,20},{20,16},{24,28},{28,24},{1,5},{5... | collective-permute-start | bytes 1794056 | tf_op jit(solution)/shard_map/ppermute | solution.py:355
  187.0 5.7 %collective-permute-start.31 = (f32[4632]{0:T(1024)S(1)}, f32[4632]{0:T(1024)S(1)}, u32[]{:S(2)}, u32[]{:S(2)}) collective-permute-start(f32[4632]{0:T(1024)S(1)} %add.287), channel_id=1, source_target_pairs={{0,16},{4,20},{8,24},{12,28},{16,0},{20,4},{24,8},{28,12},{1,17},{... | collective-permute-start | bytes 55592 | tf_op jit(solution)/shard_map/ppermute | solution.py:355
  202.4 8.1 %collective-permute-start.27 = (bf16[2,128,584]{1,2,0:T(8,128)(2,1)S(1)}, bf16[2,128,584]{1,2,0:T(8,128)(2,1)S(1)}, u32[]{:S(2)}, u32[]{:S(2)}) collective-permute-start(bf16[2,128,584]{1,2,0:T(8,128)(2,1)S(1)} %fusion.31), channel_id=1, source_target_pairs={{0,8},{4,12},{8,0},{12,4},{16,24},{20,28},{24,16},{28,20},{1,9},{5... | collective-permute-start | bytes 897032 | tf_op jit(solution)/shard_map/ppermute | solution.py:355
  205.4 35.8 %collective-permute-start.16 = (bf16[1024,256]{1,0:T(8,128)(2,1)}, bf16[1024,256]{1,0:T(8,128)(2,1)}, u32[]{:S(2)}, u32[]{:S(2)}) collective-permute-start(bf16[1024,256]{1,0:T(8,128)(2,1)} %fusion.21), channel_id=1, source_target_pairs={{0,2},{1,3},{2,0},{3,1},{4,6},{5,7},{6,4},{7,5},{8,10},{9,11},{10,... | collective-permute-start | bytes 1572872 | tf_op jit(solution)/shard_map/ppermute | solution.py:355
  208.0 16.0 %collective-permute-start.24 = (bf16[2,128,1024]{2,1,0:T(8,128)(2,1)S(1)}, bf16[2,128,1024]{2,1,0:T(8,128)(2,1)S(1)}, u32[]{:S(2)}, u32[]{:S(2)}) collective-permute-start(bf16[2,128,1024]{2,1,0:T(8,128)(2,1)S(1)} %fusion.23), channel_id=1, source_target_pairs={{0,8},{4,12},{8,0},{12,4},{16,24},{20,28},{24,16},{28,20},{1,9},{5... | collective-permute-start | bytes 1572872 | tf_op jit(solution)/shard_map/ppermute | solution.py:355
  210.6 18.2 %collective-permute-start.28 = (bf16[128,584]{0,1:T(8,128)(2,1)S(1)}, bf16[128,584]{0,1:T(8,128)(2,1)S(1)}, u32[]{:S(2)}, u32[]{:S(2)}) collective-permute-start(bf16[128,584]{0,1:T(8,128)(2,1)S(1)} %fusion.36), channel_id=1, source_target_pairs={{0,16},{4,20},{8,24},{12,28},{16,0},{20,4},{24,8},{28,12},{1,17},{... | collective-permute-start | bytes 448520 | tf_op jit(solution)/shard_map/ppermute | solution.py:355
  225.0 13.3 %collective-permute-start.25 = (bf16[128,1024]{1,0:T(8,128)(2,1)}, bf16[128,1024]{1,0:T(8,128)(2,1)}, u32[]{:S(2)}, u32[]{:S(2)}) collective-permute-start(bf16[128,1024]{1,0:T(8,128)(2,1)} %fusion.33), channel_id=1, source_target_pairs={{0,16},{4,20},{8,24},{12,28},{16,0},{20,4},{24,8},{28,12},{1,17},{... | collective-permute-start | bytes 786440 | tf_op jit(solution)/shard_map/ppermute | solution.py:355
  227.9 13.3 %collective-permute-start.20 = (bf16[1024,256]{1,0:T(8,128)(2,1)}, bf16[1024,256]{1,0:T(8,128)(2,1)}, u32[]{:S(2)}, u32[]{:S(2)}) collective-permute-start(bf16[1024,256]{1,0:T(8,128)(2,1)} %fusion.22), channel_id=1, source_target_pairs={{0,2},{1,3},{2,0},{3,1},{4,6},{5,7},{6,4},{7,5},{8,10},{9,11},{10,... | collective-permute-start | bytes 1572872 | tf_op jit(solution)/shard_map/ppermute | solution.py:355
  (40 other events, 218.0 us)

commit v2 on v1

v2 whole, which is shorter than its diff:
```python
import functools

import jax
import jax.numpy as jnp
from jax import lax
from jax.experimental import pallas as pl
from jax.experimental.pallas import tpu as pltpu
from jax.sharding import PartitionSpec as P

CONV_WIDTH = 4
LEN = 1024
BLOCK = 256
LANES = 128

epsilon = 1e-05
highest = lax.Precision.HIGHEST
f32 = jnp.float32
bf16 = jnp.bfloat16
VMEM_LIMIT = 50 * 1024 * 1024


def dot(left, right, left_dim=1, right_dim=0, precision=None):
    return lax.dot_general(
        left,
        right,
        (((left_dim,), (right_dim,)), ((), ())),
        precision=precision,
        preferred_element_type=f32,
    )


def spreader(head_share, head_size):
    row = lax.broadcasted_iota(jnp.int32, (LANES, head_share * head_size), 0)
    head = lax.broadcasted_iota(jnp.int32, (LANES, head_share * head_size), 1) // head_size
    return (row == head).astype(bf16)


def lower_mask(size):
    row = lax.broadcasted_iota(jnp.int32, (size, size), 0)
    col = lax.broadcasted_iota(jnp.int32, (size, size), 1)
    return row >= col


def const_spec(array):
    return pl.BlockSpec(array.shape, lambda i: (0,) * array.ndim)


def scalar_spec():
    return pl.BlockSpec(memory_space=pltpu.SMEM)


def cost(micros):
    return pl.CostEstimate(flops=int(micros * 1e9), bytes_accessed=0, transcendentals=0)


def params():
    return pltpu.CompilerParams(vmem_limit_bytes=VMEM_LIMIT)


def out(shape, kind):
    return jax.ShapeDtypeStruct(shape, kind)


def row_of(index, size):
    return pl.ds(pl.multiple_of(index * size, size), size)


def silu_slope(values):
    sig = jax.nn.sigmoid(values)
    return sig * (1.0 + values * (1.0 - sig))


def row_sums(values):
    return dot(jnp.ones((8, values.shape[1]), bf16), values.astype(bf16), 1, 1)


def split(values, count):
    terms = []
    for _ in range(count):
        terms.append(values.astype(bf16))
        values = values - terms[-1].astype(f32)
    return terms


def select_rows(ones, values, count=3):
    return sum(dot(ones, term) for term in split(values, count))


def spread_lanes(values, spread, count):
    return sum(dot(term, spread) for term in split(values, count))


def decay_strips(cum, cum_t, head):
    mid = BLOCK // 2
    row = cum_t[head : head + 1, :]
    top = jnp.exp(jnp.minimum(cum[:mid, head : head + 1] - row[:, :mid], 0.0))
    low = jnp.exp(jnp.minimum(cum[mid:, head : head + 1] - row, 0.0))
    return top, low


def forward_kernel(
    sizes,
    me_ref,
    *refs,
):
    head_share, head_size, blocks_per_seq, rels, groups = sizes
    piece_refs, refs = refs[:groups], refs[groups:]
    (
        first_ref,
        second_ref,
        other_first,
        other_second,
        gain_ref,
        x_taps_ref,
        x_bias_ref,
        s_taps_ref,
        s_bias_ref,
        step_bias_ref,
        rate_ref,
        skip_ref,
        normed_ref,
        scale_ref,
        inner_ref,
        x_pre_ref,
        x_ref,
        state_in_ref,
        s_pre_ref,
        bc_ref,
        step_ref,
        cum_ref,
        start_ref,
        scanned_ref,
        weight_ref,
        x_buf,
        s_buf,
        state,
    ) = refs
    inner = head_share * head_size
    half = s_bias_ref.shape[1] // 2
    share = piece_refs[0].shape[1]

    @pl.when(pl.program_id(0) == 0)
    def _():
        own_first = me_ref[2] == 0
        for i, rel in enumerate(rels):
            rows = row_of(me_ref[0] ^ rel, first_ref.shape[1])
            held = len(rels) // 2
            part = first_ref[i] if i < held else second_ref[i - held]
            mine = part[:, inner : inner + half]
            others = other_first[i] if i < held else other_second[i - held]
            weight_ref[rows, :inner] = part[:, :inner]
            weight_ref[rows, inner : inner + half] = jnp.where(own_first, mine, others)
            weight_ref[rows, inner + half : inner + 2 * half] = jnp.where(own_first, others, mine)
            weight_ref[rows, inner + 2 * half :] = part[:, inner + half :]

    @pl.when(pl.program_id(0) % blocks_per_seq == 0)
    def _():
        x_buf[0:8, :] = jnp.zeros((8, inner), f32)
        s_buf[0:8, :] = jnp.zeros((8, 2 * half), f32)
        state[...] = jnp.zeros(state.shape, f32)

    pieces = [ref[...].astype(f32) for ref in piece_refs]
    squares = pieces[0] * pieces[0]
    for piece in pieces[1:]:
        squares = squares + piece * piece
    mean = jnp.sum(squares, axis=-1, keepdims=True) / (share * groups)
    scale = lax.rsqrt(mean + epsilon)
    scale_ref[...] = jnp.broadcast_to(scale, scale_ref.shape)
    for rel, piece in enumerate(pieces):
        at = row_of(me_ref[1] ^ rel, share)
        normed_ref[:, at] = (piece * scale * gain_ref[:, at]).astype(bf16)
    projected = dot(normed_ref[...], weight_ref[...])
    inner_in = projected[:, :inner]
    state_in = projected[:, inner : inner + 2 * half]
    step_pre = projected[:, inner + 2 * half :] + step_bias_ref[...]
    inner_ref[...] = inner_in.astype(bf16)
    state_in_ref[...] = state_in.astype(bf16)
    step_ref[...] = step_pre

    def conv(buf, values, taps_ref, bias_ref):
        buf[8 : 8 + BLOCK, :] = values
        total = bias_ref[...] + taps_ref[3:4, :] * values
        for tap in range(CONV_WIDTH - 1):
            total = total + taps_ref[tap : tap + 1, :] * buf[5 + tap : 5 + tap + BLOCK, :]
        buf[0:8, :] = buf[BLOCK : BLOCK + 8, :]
        return total

    x_pre = conv(x_buf, inner_in, x_taps_ref, x_bias_ref)
    x_pre_ref[...] = x_pre.astype(bf16)
    x = (x_pre * jax.nn.sigmoid(x_pre)).astype(bf16)
    x_ref[...] = x
    s_pre = conv(s_buf, state_in, s_taps_ref, s_bias_ref)
    s_pre_ref[...] = s_pre.astype(bf16)
    bc = (s_pre * jax.nn.sigmoid(s_pre)).astype(bf16)
    bc_ref[...] = bc
    b, c = bc[:, :half], bc[:, half:]

    steps = jax.nn.softplus(step_pre)
    lower = lower_mask(BLOCK)
    cum = select_rows(lower.astype(bf16), steps * rate_ref[...])
    cum_ref[...] = cum
    cum_t = cum.T
    spread = spreader(head_share, head_size)
    cum_x = spread_lanes(cum, spread, 3)
    steps_x = spread_lanes(steps, spread, 2)
    last = cum_x[BLOCK - 1 :, :]
    x_f32 = x.astype(f32)
    stepped = x_f32 * steps_x
    stepped_low = stepped.astype(bf16)

    old = state[...]
    old_low = old.astype(bf16)
    start_ref[0] = old_low
    base = dot(c, old_low) * jnp.exp(cum_x) + skip_ref[...] * x_f32
    weighted = (stepped * jnp.exp(last - cum_x)).astype(bf16)
    state[...] = old * jnp.exp(last) + dot(b, weighted, 0, 0)

    scores = jnp.where(lower, dot(c, b, 1, 1), 0.0)
    mid = BLOCK // 2
    top_scores, low_scores = scores[:mid, :mid], scores[mid:, :]
    pair = LANES // head_size
    lane_head = lax.broadcasted_iota(jnp.int32, (mid, LANES), 1) // head_size
    for first in range(0, head_share, pair):
        at = first * head_size
        values = stepped_low[:, at : at + LANES]
        for k in range(pair):
            top, low = decay_strips(cum, cum_t, first + k)
            top_term = dot((top * top_scores).astype(bf16), values[:mid])
            low_term = dot((low * low_scores).astype(bf16), values)
            if k == 0:
                top_total, low_total = top_term, low_term
            else:
                top_total = jnp.where(lane_head == k, top_term, top_total)
                low_total = jnp.where(lane_head == k, low_term, low_total)
        scanned_ref[:mid, at : at + LANES] = base[:mid, at : at + LANES] + top_total
        scanned_ref[mid:, at : at + LANES] = base[mid:, at : at + LANES] + low_total


def forward_scan(me, pieces, weights, consts, head_share, head_size, rels):
    count, share = pieces[0].shape
    groups = len(pieces)
    features = share * groups
    inner = head_share * head_size
    state2 = consts[3].shape[1]
    blocks = count // BLOCK
    per = lambda width: pl.BlockSpec((BLOCK, width), lambda i: (i, 0))
    outs = [
        (features, bf16),
        (LANES, f32),
        (inner, bf16),
        (inner, bf16),
        (inner, bf16),
        (state2, bf16),
        (state2, bf16),
        (state2, bf16),
        (LANES, f32),
        (LANES, f32),
    ]
    wide = inner + state2 + LANES
    return pl.pallas_call(
        functools.partial(
            forward_kernel, (head_share, head_size, LEN // BLOCK, rels, groups)
        ),
        grid=(blocks,),
        in_specs=[scalar_spec()]
        + [per(share)] * groups
        + [const_spec(a) for a in (*weights, *consts)],
        out_specs=[per(w) for w, _ in outs]
        + [
            pl.BlockSpec((1, state2 // 2, inner), lambda i: (i, 0, 0)),
            per(inner),
            pl.BlockSpec((features, wide), lambda i: (0, 0)),
        ],
        out_shape=[out((count, w), k) for w, k in outs]
        + [
            out((blocks, state2 // 2, inner), bf16),
            out((count, inner), f32),
            out((features, wide), bf16),
        ],
        scratch_shapes=[
            pltpu.VMEM((BLOCK + 8, inner), f32),
            pltpu.VMEM((BLOCK + 8, state2), f32),
            pltpu.VMEM((state2 // 2, inner), f32),
        ],
        compiler_params=params(),
        cost_estimate=cost(16),
    )(me, *pieces, *weights, *consts)


def gate_kernel(sizes, me_ref, *refs):
    z_rels, o_rels, groups = sizes
    cot_refs, refs = refs[:groups], refs[groups:]
    z_first, z_second, o_first, o_second, normed_ref, scanned_ref, gain_ref = refs[:7]
    gate_ref, grad_mid_ref, stats_ref, z_ref, o_ref = refs[7:]
    share = cot_refs[0].shape[1]

    @pl.when(pl.program_id(0) == 0)
    def _():
        held = len(z_rels) // 2
        for i in range(len(z_rels)):
            rows = row_of(me_ref[0] ^ z_rels[i], z_first.shape[1])
            z_ref[rows, :] = z_first[i] if i < held else z_second[i - held]
            rows = row_of(me_ref[0] ^ o_rels[i], z_first.shape[1])
            o_ref[rows, :] = o_first[i] if i < held else o_second[i - held]

    gate_in = dot(normed_ref[...], z_ref[...])
    grad_mid = sum(
        dot(ref[...], o_ref[row_of(me_ref[1] ^ rel, share), :])
        for rel, ref in enumerate(cot_refs)
    )
    gate_ref[...] = gate_in.astype(gate_ref.dtype)
    grad_mid_ref[...] = grad_mid.astype(grad_mid_ref.dtype)
    mixed_in = scanned_ref[...] * (gate_in * jax.nn.sigmoid(gate_in))
    squares = row_sums(mixed_in * mixed_in)
    products = row_sums(grad_mid * gain_ref[...] * mixed_in)
    row = lax.broadcasted_iota(jnp.int32, squares.shape, 0)
    stats_ref[...] = jnp.where(row == 0, squares, products)


def gate(me, cots, weights, normed, scanned, gain, z_rels, o_rels):
    count, share = cots[0].shape
    groups = len(cots)
    features = share * groups
    inner = scanned.shape[1]
    per = lambda width: pl.BlockSpec((BLOCK, width), lambda i: (i, 0))
    whole = pl.BlockSpec((features, inner), lambda i: (0, 0))
    return pl.pallas_call(
        functools.partial(gate_kernel, (z_rels, o_rels, groups)),
        grid=(count // BLOCK,),
        in_specs=[scalar_spec()]
        + [per(share)] * groups
        + [const_spec(a) for a in weights]
        + [per(features), per(inner), const_spec(gain)],
        out_specs=[
            per(inner),
            per(inner),
            pl.BlockSpec((8, BLOCK), lambda i: (0, i)),
            whole,
            whole,
        ],
        out_shape=[
            out((count, inner), f32),
            out((count, inner), bf16),
            out((8, count), f32),
            out((features, inner), bf16),
            out((features, inner), bf16),
        ],
        compiler_params=params(),
        cost_estimate=cost(8),
    )(me, *cots, *weights, normed, scanned, gain)


def mix_kernel(sizes, me_ref, *refs):
    z_rels, o_rels, groups = sizes
    cot_refs, refs = refs[:groups], refs[groups:]
    stats_ref, normed_ref, gate_ref, grad_mid_ref, scanned_ref, o_ref, gain_ref = refs[:7]
    (
        grad_scanned_ref,
        grad_gate_ref,
        out_send,
        out_keep,
        z_send,
        z_keep,
        o_send,
        o_keep,
        gain_grad_ref,
        z_sum,
        o_sum,
    ) = refs[7:]
    inner = gain_ref.shape[1]
    share = out_send.shape[2]

    @pl.when(pl.program_id(0) == 0)
    def _():
        z_sum[...] = jnp.zeros(z_sum.shape, f32)
        o_sum[...] = jnp.zeros(o_sum.shape, f32)
        gain_grad_ref[...] = jnp.zeros(gain_grad_ref.shape, f32)

    stats = stats_ref[...].T
    total = inner * groups
    scale = lax.rsqrt(stats[:, 0:1] / total + epsilon)
    mean = scale * stats[:, 1:2] / total
    gate_in = gate_ref[...]
    sig = jax.nn.sigmoid(gate_in)
    act = gate_in * sig
    scanned = scanned_ref[...]
    mid_hat = scanned * act * scale
    grad_mid = grad_mid_ref[...].astype(f32)
    normed_mid = (mid_hat * gain_ref[...]).astype(bf16)
    gain_grad_ref[0:1, :] += jnp.sum(mid_hat * grad_mid, axis=0, keepdims=True)
    grad_mixed = scale * (grad_mid * gain_ref[...] - mid_hat * mean)
    grad_scanned_ref[...] = (grad_mixed * act).astype(bf16)
    grad_gate = (grad_mixed * scanned * sig * (1.0 + gate_in * (1.0 - sig))).astype(bf16)
    grad_gate_ref[...] = grad_gate
    z_sum[...] += dot(normed_ref[...], grad_gate, 0, 0)
    for rel in range(groups):
        rows = row_of(me_ref[1] ^ rel, share)
        o_sum[rows, :] += dot(cot_refs[rel][...], normed_mid, 0, 0)
        part = dot(normed_mid, o_ref[rows, :], 1, 1).astype(bf16)
        if rel % 2:
            out_send[rel // 2] = part
        else:
            out_keep[rel // 2] = part

    @pl.when(pl.program_id(0) == pl.num_programs(0) - 1)
    def _():
        size = z_send.shape[1]
        for refs_of, total, rels in ((z_send, z_sum, z_rels[0]), (z_keep, z_sum, z_rels[1]), (o_send, o_sum, o_rels[0]), (o_keep, o_sum, o_rels[1])):
            for i, rel in enumerate(rels):
                refs_of[i] = total[row_of(me_ref[0] ^ rel, size), :].astype(bf16)


def mix(me, cots, stats, normed, gate_in, grad_mid, scanned, o_weight, gain, shards, z_rels, o_rels):
    groups = len(cots)
    count, inner = scanned.shape
    features = normed.shape[1]
    share = features // groups
    size = features // shards
    per = lambda width: pl.BlockSpec((BLOCK, width), lambda i: (i, 0))
    parts = pl.BlockSpec((groups // 2, BLOCK, share), lambda i: (0, i, 0))
    early = (shards // 2, size, inner)
    fixed = pl.BlockSpec(early, lambda i: (0, 0, 0))
    return pl.pallas_call(
        functools.partial(mix_kernel, (z_rels, o_rels, groups)),
        grid=(count // BLOCK,),
        in_specs=[scalar_spec()]
        + [per(share)] * groups
        + [
            pl.BlockSpec((8, BLOCK), lambda i: (0, i)),
            per(features),
            per(inner),
            per(inner),
            per(inner),
            const_spec(o_weight),
            const_spec(gain),
        ],
        out_specs=[
            per(inner),
            per(inner),
            parts,
            parts,
            fixed,
            fixed,
            fixed,
            fixed,
            pl.BlockSpec((8, inner), lambda i: (0, 0)),
        ],
        out_shape=[
            out((count, inner), bf16),
            out((count, inner), bf16),
            out((groups // 2, count, share), bf16),
            out((groups // 2, count, share), bf16),
            out(early, bf16),
            out(early, bf16),
            out(early, bf16),
            out(early, bf16),
            out((8, inner), f32),
        ],
        scratch_shapes=[pltpu.VMEM((features, inner), f32)] * 2,
        compiler_params=params(),
        cost_estimate=cost(10),
    )(me, *cots, stats, normed, gate_in, grad_mid, scanned, o_weight, gain)


def backward_kernel(sizes, *refs):
    me_ref = refs[0]
    head_share, head_size, blocks_per_seq, top_block, joined = sizes
    inputs, upper_parts, refs = refs[1:21], refs[21] if joined else None, refs[21 + joined :]
    (
        grad_ref,
        inner_ref,
        x_pre_ref,
        x_ref,
        state_in_ref,
        s_pre_ref,
        bc_ref,
        step_ref,
        cum_ref,
        start_ref,
        x_taps_ref,
        s_taps_ref,
        rate_ref,
        skip_ref,
    ) = inputs[:14]
    given = inputs[14:]
    late_ref, s_parts, *carried_refs = refs
    x_sums, s_sums, small_ref, x_tail, s_tail, state, x_buf, s_buf = carried_refs
    inner = head_share * head_size
    half = bc_ref.shape[1] // 2
    at_block = top_block - pl.program_id(0)

    @pl.when(pl.program_id(0) == 0)
    def _():
        for ref, value in zip((x_sums, s_sums, small_ref, x_tail, s_tail, state), given):
            ref[...] = value[...]

    @pl.when(at_block % blocks_per_seq == blocks_per_seq - 1)
    def _():
        x_tail[...] = jnp.zeros(x_tail.shape, f32)
        s_tail[...] = jnp.zeros(s_tail.shape, f32)
        state[...] = jnp.zeros(state.shape, f32)

    grad_low = grad_ref[...]
    grad = grad_low.astype(f32)
    x = x_ref[...].astype(f32)
    bc = bc_ref[...]
    b, c = bc[:, :half], bc[:, half:]
    step_pre = step_ref[...]
    steps = jax.nn.softplus(step_pre)
    cum = cum_ref[...]
    cum_t = cum.T
    lower = lower_mask(BLOCK)
    row = lax.broadcasted_iota(jnp.int32, (BLOCK, BLOCK), 0)
    col = lax.broadcasted_iota(jnp.int32, (BLOCK, BLOCK), 1)
    spread = spreader(head_share, head_size)
    cum_x = spread_lanes(cum, spread, 3)
    steps_x = spread_lanes(steps, spread, 2)
    last = cum_x[BLOCK - 1 :, :]
    decay_in = jnp.exp(cum_x)
    decay_out = jnp.exp(last - cum_x)
    stepped = x * steps_x
    stepped_low = stepped.astype(bf16)

    old_low = start_ref[0]
    old = old_low.astype(f32)
    later = state[...]
    later_low = later.astype(bf16)
    grad_decayed = grad * decay_in
    grad_decayed_low = grad_decayed.astype(bf16)
    from_later = dot(b, later_low) * decay_out
    carried = dot(c, old_low)
    grad_c = dot(grad_decayed_low, old_low, 1, 1)
    grad_b = dot((stepped * decay_out).astype(bf16), later_low, 1, 1)
    state[...] = later * jnp.exp(last) + dot(c, grad_decayed_low, 0, 0)

    scores = jnp.where(lower, dot(c, b, 1, 1), 0.0)
    mid = BLOCK // 2
    top_scores, low_scores = scores[:mid, :mid], scores[mid:, :]
    pair = LANES // head_size
    lane_head = lax.broadcasted_iota(jnp.int32, (BLOCK, LANES), 1) // head_size
    pick_lane = lax.broadcasted_iota(jnp.int32, (BLOCK, LANES), 1)
    top_sum = jnp.zeros((mid, mid), f32)
    low_sum = jnp.zeros((mid, BLOCK), f32)
    top_cross = jnp.zeros((mid, LANES), f32)
    low_cross = jnp.zeros((mid, LANES), f32)
    all_cross = jnp.zeros((BLOCK, LANES), f32)
    within = []
    for first in range(0, head_share, pair):
        at = first * head_size
        grads = grad_low[:, at : at + LANES]
        values = stepped_low[:, at : at + LANES]
        total = None
        for k in range(pair):
            top, low = decay_strips(cum, cum_t, first + k)
            own = jnp.where(lane_head == k, grads, jnp.zeros_like(grads))
            pick = (pick_lane == first + k).astype(bf16)
            top_products = dot(own[:mid], values[:mid], 1, 1) * top
            low_products = dot(own[mid:], values, 1, 1) * low
            top_sum = top_sum + top_products
            low_sum = low_sum + low_products
            low_term = dot((low * low_scores).astype(bf16), grads[mid:], 0, 0)
            top_term = dot((top * top_scores).astype(bf16), grads[:mid], 0, 0)
            term = low_term + jnp.concatenate([top_term, jnp.zeros_like(top_term)], axis=0)
            total = term if k == 0 else jnp.where(lane_head == k, term, total)
            top_pairs = (top_products * top_scores).astype(bf16)
            low_pairs = (low_products * low_scores).astype(bf16)
            top_cross = top_cross + dot(top_pairs, pick[:mid]) - dot(top_pairs, pick[:mid], 0, 0)
            low_cross = low_cross + dot(low_pairs, pick)
            all_cross = all_cross + dot(low_pairs, pick[mid:], 0, 0)
        within.append(total)
    zeros = jnp.zeros((mid, mid), f32)
    gathered = jnp.concatenate([jnp.concatenate([top_sum, zeros], axis=1), low_sum], axis=0)
    gathered_low = jnp.where(lower, gathered, 0.0).astype(bf16)
    grad_b = grad_b + dot(gathered_low, c, 0, 0)
    grad_c = grad_c + dot(gathered_low, b)
    crossing = jnp.concatenate([top_cross, low_cross], axis=0) - all_cross

    by_x = jnp.concatenate(within, axis=1) + from_later
    fold = lambda values: dot(values.astype(bf16), spread, 1, 1)
    direct = fold(by_x * x)
    into = fold(grad_decayed * carried)
    onward = steps * fold(from_later * x)
    tops = jnp.sum(later * old, axis=0, keepdims=True) * jnp.exp(last)
    spanning = fold(jnp.broadcast_to(tops, (8, inner)))[0:1, :]
    upper = (row <= col).astype(bf16)
    strict = (row > col).astype(bf16)
    by_decay = select_rows(upper, into + crossing, 3) + select_rows(strict, onward, 2) + spanning
    by_step = direct + rate_ref[...] * by_decay
    grad_step = by_step * jax.nn.sigmoid(step_pre)
    small_ref[0:1, :] += jnp.sum(grad_step, axis=0, keepdims=True)
    small_ref[1:2, :] += jnp.sum(steps * by_decay, axis=0, keepdims=True)
    skips = jnp.sum(grad * x, axis=0, keepdims=True)
    small_ref[2:3, :] += sum(
        dot(term, spread, 1, 1) for term in split(jnp.broadcast_to(skips, (8, inner)), 2)
    )[0:1, :]

    def conv_back(buf, tail, by_pre, values, taps_ref, sums):
        buf[0:BLOCK, :] = by_pre
        buf[BLOCK:, :] = tail[...]
        tail[...] = by_pre[0:8, :]
        total = taps_ref[3:4, :] * by_pre
        sums[3:4, :] += jnp.sum(by_pre * values, axis=0, keepdims=True)
        sums[4:5, :] += jnp.sum(by_pre, axis=0, keepdims=True)
        for tap in range(CONV_WIDTH - 1):
            ahead = CONV_WIDTH - 1 - tap
            moved = buf[ahead : ahead + BLOCK, :]
            total = total + taps_ref[tap : tap + 1, :] * moved
            sums[tap : tap + 1, :] += jnp.sum(moved * values, axis=0, keepdims=True)
        return total.astype(bf16)

    by_conv = steps_x * by_x + skip_ref[...] * grad
    by_pre = by_conv * silu_slope(x_pre_ref[...].astype(f32))
    late_ref[:, :inner] = conv_back(
        x_buf, x_tail, by_pre, inner_ref[...].astype(f32), x_taps_ref, x_sums
    )
    by_state = jnp.concatenate([grad_b, grad_c], axis=1) * silu_slope(s_pre_ref[...].astype(f32))
    grad_state = conv_back(
        s_buf, s_tail, by_state, state_in_ref[...].astype(f32), s_taps_ref, s_sums
    )
    late_ref[:, inner : inner + 2 * half] = grad_state
    width = half // 2
    first = lax.broadcasted_iota(jnp.int32, (BLOCK, half), 1) < width
    left, right = grad_state[:, :half], grad_state[:, half:]
    turn = lambda v: jnp.concatenate([v[:, width:], v[:, :width]], axis=1)
    even, odd = jnp.where(first, left, turn(right)), jnp.where(first, turn(left), right)
    own_first, low_side = me_ref[2] == 0, me_ref[1] < 2
    for core, (one, other) in enumerate(((even, odd), (odd, even))):
        half_of = jnp.where(own_first, one, other)
        turned = turn(half_of)
        for side, part in enumerate((jnp.where(low_side, half_of, turned), jnp.where(low_side, turned, half_of))):
            if joined:
                part = jnp.where(first, part, turn(upper_parts[core + 2 * side]))
            s_parts[core + 2 * side] = part
    late_ref[:, inner + 2 * half :] = grad_step.astype(bf16)


def backward_scan(me, part, rows, starts, consts, carry, upper, head_share, head_size):
    first, stop = part
    count, inner = rows[0].shape
    state2 = rows[6].shape[1]
    wide = inner + state2 + LANES
    per = lambda width: pl.BlockSpec((BLOCK, width), lambda i: (stop - 1 - i, 0))
    joined = [] if upper is None else list(upper)[::-1]
    sizes = (head_share, head_size, LEN // BLOCK, stop - 1, len(joined))
    state_parts = pl.BlockSpec((4, BLOCK, state2 // 2), lambda i: (0, stop - first - 1 - i, 0))
    results = pl.pallas_call(
        functools.partial(backward_kernel, sizes),
        grid=(stop - first,),
        in_specs=[scalar_spec()]
        + [per(a.shape[1]) for a in rows]
        + [pl.BlockSpec((1, state2 // 2, inner), lambda i: (stop - 1 - i, 0, 0))]
        + [const_spec(a) for a in (*consts, *carry)]
        + ([state_parts, pl.BlockSpec(memory_space=pl.ANY)] if joined else []),
        out_specs=[per(wide)]
        + [state_parts]
        + [const_spec(a) for a in carry],
        out_shape=[out((count, wide), bf16)]
        + [out((4, (stop - first) * BLOCK, state2 // 2), bf16)]
        + [out(a.shape, f32) for a in carry],
        input_output_aliases={len(rows) + 3 + len(consts) + len(carry): 0} if joined else {},
        scratch_shapes=[
            pltpu.VMEM((BLOCK + 8, inner), f32),
            pltpu.VMEM((BLOCK + 8, state2), f32),
        ],
        compiler_params=params(),
        cost_estimate=cost(12),
    )(me, *rows, starts, *consts, *carry, *joined)
    return results[0], results[1], tuple(results[2:])


def late_kernel(sizes, me_ref, *refs):
    a_rels, b_rels, inner, half = sizes
    late_ref, state_ref, normed_ref, a_send, a_keep, b_send, b_keep, total = refs

    @pl.when(pl.program_id(0) == 0)
    def _():
        total[...] = jnp.zeros(total.shape, f32)

    rest = inner + 2 * half
    width = LANES // 2
    turn = lambda v: jnp.concatenate([v[:, width:], v[:, :width]], axis=1)
    steps = turn(late_ref[:, rest:])
    state = state_ref[...]
    state = jnp.where(pl.program_id(0) < pl.num_programs(0) // 2, state, turn(state))
    first = lax.broadcasted_iota(jnp.int32, (BLOCK, LANES), 1) < width
    both = jnp.concatenate([late_ref[:, :inner], jnp.where(first, state, steps)], axis=1)
    total[...] += dot(normed_ref[...], both, 0, 0)

    @pl.when(pl.program_id(0) == pl.num_programs(0) - 1)
    def _():
        size, cut = a_send.shape[1:]
        for rels, send, keep, columns in (
            (a_rels, a_send, a_keep, slice(0, cut)),
            (b_rels, b_send, b_keep, slice(cut, None)),
        ):
            for to, found in zip((send, keep), rels):
                for i, rel in enumerate(found):
                    to[i] = total[row_of(me_ref[0] ^ rel, size), columns].astype(bf16)


def late_grads(me, late, state, normed, inner, half, shards, a_rels, b_rels):
    count, wide = late.shape
    features = normed.shape[1]
    size = features // shards
    cut = inner // 2
    per = lambda width: pl.BlockSpec((BLOCK, width), lambda i: (i, 0))
    packed = pl.BlockSpec((BLOCK, LANES), lambda i: (i % (count // BLOCK // 2), 0))
    a_part, b_part = (shards // 2, size, cut), (shards // 2, size, inner + LANES - cut)
    outs = [a_part, a_part, b_part, b_part]
    return pl.pallas_call(
        functools.partial(late_kernel, (a_rels, b_rels, inner, half)),
        grid=(count // BLOCK,),
        in_specs=[scalar_spec(), per(wide), packed, per(features)],
        out_specs=[pl.BlockSpec(dims, lambda i: (0, 0, 0)) for dims in outs],
        out_shape=[out(dims, bf16) for dims in outs],
        scratch_shapes=[pltpu.VMEM((features, inner + LANES), f32)],
        compiler_params=params(),
        cost_estimate=cost(5),
    )(me, late, state, normed)


def rows_kernel(groups, me_ref, *refs):
    piece_refs, refs = refs[:groups], refs[groups:]
    late_ref, gate_grad_ref, scale_ref, z_ref, weight_ref, gain_ref = refs[:6]
    rows_send, rows_keep, gain_grad_ref, stat_ref = refs[6:]
    share = piece_refs[0].shape[1]

    @pl.when(pl.program_id(0) == 0)
    def _():
        gain_grad_ref[...] = jnp.zeros(gain_grad_ref.shape, f32)

    grad_gate = gate_grad_ref[...]
    late = late_ref[...]
    scale = scale_ref[:, 0:1]
    stat = jnp.zeros((BLOCK, share), f32)
    for rel in range(groups):
        rows = row_of(me_ref[0 + 1] ^ rel, share)
        part = dot(grad_gate, z_ref[rows, :], 1, 1) + dot(late, weight_ref[rows, :], 1, 1)
        to = rows_send if rel % 2 else rows_keep
        to[rel // 2] = part.astype(bf16)
        product = piece_refs[rel][...].astype(f32) * scale * part
        gain_grad_ref[0:1, rows] += jnp.sum(product, axis=0, keepdims=True)
        stat = stat + product * gain_ref[:, rows]
    stat_ref[...] = row_sums(stat)


def row_grads(me, pieces, late, grad_gate, scale, z_all, weight, gain):
    count, share = pieces[0].shape
    groups = len(pieces)
    features = share * groups
    per = lambda width: pl.BlockSpec((BLOCK, width), lambda i: (i, 0))
    parts = pl.BlockSpec((groups // 2, BLOCK, share), lambda i: (0, i, 0))
    return pl.pallas_call(
        functools.partial(rows_kernel, groups),
        grid=(count // BLOCK,),
        in_specs=[scalar_spec()]
        + [per(a.shape[1]) for a in (*pieces, late, grad_gate, scale)]
        + [const_spec(a) for a in (z_all, weight, gain)],
        out_specs=[
            parts,
            parts,
            pl.BlockSpec((8, features), lambda i: (0, 0)),
            pl.BlockSpec((8, BLOCK), lambda i: (0, i)),
        ],
        out_shape=[
            out((groups // 2, count, share), bf16),
            out((groups // 2, count, share), bf16),
            out((8, features), f32),
            out((8, count), f32),
        ],
        compiler_params=params(),
        cost_estimate=cost(6),
    )(me, *pieces, late, grad_gate, scale, z_all, weight, gain)


def swap(value, axis, step):
    count = lax.axis_size(axis)
    return lax.ppermute(value, axis, [(i, i ^ step) for i in range(count)])


def steps_of(axis):
    found = []
    while 2 ** len(found) < lax.axis_size(axis):
        found.append(2 ** len(found))
    return found


def rels_of(order):
    rels = [0]
    for step in order:
        rels = rels + [rel ^ step for rel in rels]
    return rels


def halves_of(order):
    rels = rels_of(order[:0:-1])
    return [rel ^ order[0] for rel in rels], rels


def gather_steps(value, axis, order):
    held = value[None]
    for i, step in enumerate(order):
        held, got = yield held, swap(held, axis, step)
        if i < len(order) - 1:
            held = jnp.concatenate([held, got], axis=0)


def reduce_steps(send, keep, axis, order):
    for i, step in enumerate(order):
        keep, got = yield keep, swap(send, axis, step)
        if i < len(order) - 1:
            total = keep.astype(f32) + got.astype(f32)
            mid = total.shape[0] // 2
            keep, send = total[:mid], total[mid:].astype(bf16)


def pair_steps(send, keep, axis, order):
    keep, got = yield keep, swap(send, axis, order[0])
    send = (keep[1:].astype(f32) + got[1:].astype(f32)).astype(bf16)
    yield (keep, got), swap(send, axis, order[1])


def sum_steps(value, axis, order):
    for step in order:
        value, got = yield value, swap(value, axis, step)
        value = value + got


class Exchange:
    def __init__(self, steps, left=0):
        self.steps, self.value, self.ended, self.left = steps, None, False, left

    def advance(self):
        self.left -= 1
        try:
            self.value = self.steps.send(self.value)
        except StopIteration:
            self.ended = True

    def total(self):
        keep, got = self.value
        return keep.astype(f32) + got.astype(f32)


def phase(exchanges, beside=()):
    values, beside = lax.optimization_barrier(([e.value for e in exchanges], beside))
    for exchange, value in zip(exchanges, values):
        exchange.value = value
    return beside


def finish(exchanges, jobs):
    moving, results = exchanges, [None] * len(jobs)
    while moving:
        for exchange in moving:
            exchange.advance()
        moving = [exchange for exchange in moving if not exchange.ended]
        new = [i for i, job in enumerate(jobs) if job[0].ended and results[i] is None]
        made = [jobs[i][1]() for i in new]
        if any(exchange.left > 0 for exchange in moving):
            made = phase(moving, made)
        for i, result in zip(new, made):
            results[i] = result
    return results


def body(
    tokens,
    z_weight,
    x_weight,
    bc_weight,
    dt_weight,
    out_weight,
    norm_gain,
    gate_gain,
    x_conv_weight,
    x_conv_bias,
    bc_conv_weight,
    bc_conv_bias,
    step_bias,
    decay_log,
    skip_gain,
    cotangent,
):
    head_index = lax.axis_index("heads")
    shard_index = lax.axis_index("shard")
    groups = lax.axis_size("heads")
    shards = lax.axis_size("shard")
    row_count, feature_share = tokens.shape
    feature_total = feature_share * groups
    size, inner_share = z_weight.shape
    head_share = dt_weight.shape[1]
    head_size = inner_share // head_share
    state_width = bc_weight.shape[1]
    half = state_width // 2
    near = steps_of("shard")
    far = near[::-1]
    rels = rels_of(far)
    core = head_index % 2
    me = jnp.stack([shard_index, head_index, core]).astype(jnp.int32)
    step_pad = LANES - head_share

    own_half = lax.dynamic_slice_in_dim(bc_weight, core * half, half, 1)
    scan_weight = jnp.concatenate(
        [x_weight, own_half, jnp.pad(dt_weight, ((0, 0), (0, step_pad)))], axis=1
    )
    o_order = near[:1] + far[:-1]
    scan_x = Exchange(gather_steps(scan_weight, "shard", far))
    z_x = Exchange(gather_steps(z_weight, "shard", far))
    o_x = Exchange(gather_steps(out_weight.T, "shard", o_order), len(far))
    last = len(far) - 1
    cut = lambda v: v[:, :, inner_share : inner_share + half]
    for i in range(len(far)):
        scan_x.advance()
        moving = [scan_x]
        if i > 0:
            z_x.advance()
            moving.append(z_x)
        if i != 1:
            o_x.advance()
            moving.append(o_x)
        if i == 0:
            beside = (swap(tokens, "heads", 2), swap(tokens, "heads", 1))
            tokens_across, tokens_near, z_from, cot_from = phase(
                moving, (*beside, z_weight, cotangent)
            )
            z_x = Exchange(gather_steps(z_from, "shard", far), len(far))
        elif i == last:
            beside = (
                swap(tokens_across, "heads", 1),
                swap(cot_from, "heads", 2),
                swap(cut(scan_x.value[0]), "heads", 1),
            )
            tokens_last, cot_across, other_held = phase(moving, beside)
        else:
            (cot_from,) = phase(moving, (cot_from,))
    scan_held, scan_got = scan_x.value
    token_parts = [tokens, tokens_near, tokens_across, tokens_last]
    other_got = swap(cut(scan_got), "heads", 1)

    pad_lanes = lambda v: jnp.pad(v, (0, step_pad))[None]
    rate = pad_lanes(-jnp.exp(decay_log))
    skip_x = jnp.repeat(skip_gain, head_size)[None]
    z_x.advance()
    o_x.advance()
    cot_near, cot_last = swap(cot_from, "heads", 1), swap(cot_across, "heads", 1)
    scan = forward_scan(
        me,
        token_parts,
        (scan_held, scan_got, other_held, other_got),
        (
            norm_gain[None],
            x_conv_weight,
            x_conv_bias[None],
            bc_conv_weight,
            bc_conv_bias[None],
            pad_lanes(step_bias),
            rate,
            skip_x,
        ),
        head_share,
        head_size,
        rels,
    )

    (
        normed,
        scale_in,
        inner_in,
        x_pre,
        x,
        state_in,
        s_pre,
        bc,
        step_pre,
        cum,
        starts,
        scanned,
        scan_weight_all,
    ), (cot_near, cot_last) = phase([z_x, o_x], (scan, (cot_near, cot_last)))
    finish([z_x, o_x], [])
    cot_parts = [cotangent, cot_near, cot_across, cot_last]

    gain_row = gate_gain[None]
    gate_in, grad_mid, stats, z_all, o_all = gate(
        me, cot_parts, (*z_x.value, *o_x.value), normed, scanned, gain_row, rels, rels_of(o_order)
    )
    for step in (1, 2):
        stats = stats + swap(stats, "heads", step)

    send_rels, keep_rels = halves_of(near)
    o_sums = near[1:] + near[:1]
    (
        grad_scanned,
        grad_gate,
        out_send,
        out_keep,
        z_send,
        z_keep,
        o_send,
        o_keep,
        gate_gain_grad,
    ) = mix(
        me, cot_parts, stats, normed, gate_in, grad_mid, scanned, o_all, gain_row,
        shards, (send_rels, keep_rels), halves_of(o_sums),
    )
    z_x = Exchange(reduce_steps(z_send, z_keep, "shard", near), len(near))
    o_x = Exchange(reduce_steps(o_send, o_keep, "shard", o_sums), len(near))
    out_x = Exchange(reduce_steps(out_send, out_keep, "heads", [1, 2]))

    blocks = row_count // BLOCK
    carry = tuple(
        jnp.zeros(dims, f32)
        for dims in (
            (8, inner_share),
            (8, state_width),
            (8, LANES),
            (8, inner_share),
            (8, state_width),
            (half, inner_share),
        )
    )
    scan_rows = (grad_scanned, inner_in, x_pre, x, state_in, s_pre, bc, step_pre, cum)
    scan_consts = (x_conv_weight, bc_conv_weight, rate, skip_x)
    sizes = (head_share, head_size)
    quarter = half // 2
    for exchange in (z_x, o_x, out_x):
        exchange.advance()
    late, s_upper, carry = phase(
        [z_x, o_x, out_x],
        backward_scan(me, (blocks // 2, blocks), scan_rows, starts, scan_consts, carry, None, *sizes),
    )
    for exchange in (z_x, o_x, out_x):
        exchange.advance()
    late, state_parts, carry = phase(
        [z_x, o_x, out_x],
        backward_scan(
            me, (0, blocks // 2), scan_rows, starts, scan_consts, carry, (late, s_upper), *sizes
        ),
    )
    x_sums, s_sums, small = carry[:3]
    (rows_send, rows_keep, gain_grad, stat), state_got = phase(
        [],
        (
            row_grads(
                me, token_parts, late, grad_gate, scale_in, z_all, scan_weight_all, norm_gain[None]
            ),
            [swap(state_parts[step], "heads", step) for step in (1, 2, 3)],
        ),
    )

    state_total = sum((part.astype(f32) for part in state_got), state_parts[0].astype(f32)).astype(bf16)
    b_sums = near[1:] + near[:1]
    rows_x = Exchange(pair_steps(rows_send, rows_keep, "heads", [1, 2]))
    by_heads = jnp.concatenate([gain_grad[0], stat[0], s_sums[: CONV_WIDTH + 1].reshape(-1)])
    rows_x.advance()
    (a_send, a_keep, b_send, b_keep), by_heads, got = phase(
        [rows_x, z_x, o_x],
        (
            late_grads(
                me, late, state_total, normed, inner_share, half, shards, halves_of(near), halves_of(b_sums)
            ),
            by_heads,
            [swap(by_heads, "heads", step) for step in (1, 2, 3)],
        ),
    )
    a_x = Exchange(reduce_steps(a_send, a_keep, "shard", near), len(near))
    b_x = Exchange(reduce_steps(b_send, b_keep, "shard", b_sums), len(near))
    by_heads = (by_heads + got[0]) + (got[1] + got[2])
    local = jnp.concatenate(
        [
            gate_gain_grad[0],
            x_sums[: CONV_WIDTH + 1].reshape(-1),
            small[0, :head_share],
            small[1, :head_share],
            small[2, :head_share],
        ]
    )
    summed = jnp.concatenate(
        [
            lax.dynamic_slice_in_dim(by_heads, head_index * feature_share, feature_share, 0),
            by_heads[feature_total + row_count :],
            local,
        ]
    )
    small_x = Exchange(sum_steps(summed, "shard", near), len(near))
    for exchange in (a_x, b_x, rows_x, small_x, z_x):
        exchange.advance()
    mixed = (tokens.astype(f32) + out_x.total()[0]).astype(bf16)
    norm_stat = by_heads[feature_total : feature_total + row_count]
    mixed, norm_stat = phase([a_x, b_x, rows_x, small_x, z_x], (mixed, norm_stat))
    scale = scale_in[:, :1]
    gain_share = lax.dynamic_slice_in_dim(norm_gain, head_index * feature_share, feature_share, 0)

    def token_grads():
        tokens_hat = tokens.astype(f32) * scale
        (first, second), third = rows_x.value
        total = first[0].astype(f32) + second[0].astype(f32) + third[0].astype(f32)
        scaled = total * gain_share - tokens_hat * (norm_stat / feature_total)[:, None]
        return (cotangent.astype(f32) + scale * scaled).astype(bf16)

    tokens_grad, z_sum, o_sum, a_sum, b_sum, summed = finish(
        [o_x, a_x, b_x, rows_x, small_x, z_x],
        [
            (rows_x, token_grads),
            (z_x, lambda: z_x.total()[0]),
            (o_x, lambda: o_x.total()[0].T),
            (a_x, lambda: a_x.total()[0]),
            (b_x, lambda: b_x.total()[0]),
            (small_x, small_x.total),
        ],
    )
    steps_at = inner_share - a_sum.shape[1]

    cuts, at = [], 0
    taps = CONV_WIDTH + 1
    for count in (feature_share, taps * state_width, inner_share, taps * inner_share) + (head_share,) * 3:
        cuts.append(summed[at : at + count])
        at += count
    bc_taps = cuts[1].reshape(taps, state_width)
    x_taps = cuts[3].reshape(taps, inner_share)
    return (
        mixed,
        tokens_grad,
        z_sum,
        jnp.concatenate([a_sum, b_sum[:, :steps_at]], axis=1),
        b_sum[:, steps_at : steps_at + quarter],
        b_sum[:, steps_at + LANES // 2 : steps_at + LANES // 2 + head_share],
        o_sum,
        cuts[0],
        cuts[2],
        x_taps[:CONV_WIDTH],
        x_taps[CONV_WIDTH],
        bc_taps[:CONV_WIDTH],
        bc_taps[CONV_WIDTH],
        cuts[4],
        cuts[5] * rate[0, :head_share],
        cuts[6],
    )


def solution(mesh):
    placed = (
        P("shard", "heads"),
        P("shard", "heads"),
        P("shard", "heads"),
        P("shard", None),
        P("shard", "heads"),
        P("heads", "shard"),
        P(),
        P("heads"),
        P(None, "heads"),
        P("heads"),
        P(),
        P(),
        P("heads"),
        P("heads"),
        P("heads"),
        P("shard", "heads"),
    )
    return jax.shard_map(
        body,
        mesh=mesh,
        in_specs=placed,
        out_specs=(
            P("shard", "heads"),
            P("shard", "heads"),
            P("shard", "heads"),
            P("shard", "heads"),
            P("shard", "heads"),
            P("shard", "heads"),
            P("heads", "shard"),
            P("heads"),
            P("heads"),
            P(None, "heads"),
            P("heads"),
            P(),
            P(),
            P("heads"),
            P("heads"),
            P("heads"),
        ),
        check_vma=False,
    )
```

time: 249 us -> 194 us (0.78); the launches traced: 245 us -> 193 us
  waiting for transfers between devices: 74.4 us -> 43.1 us
  Pallas kernels: 41.1 us -> 67.2 us
  local copies, waits for them, and re-layouts: 42.3 us -> 19.5 us
  matrix products: 19.4 us -> 0 us
  other arithmetic: 27.7 us -> 12.8 us
  starting transfers between devices: 37.9 us -> 48.7 us
    ppermute x32 -> x44, waiting for transfers between devices: 74.4 us -> 43.1 us  [swap(): return lax.ppermute(value, axis, [(i, i ^ step) for i in range(count)])]
    pallas_call x1 -> x6, Pallas kernels: 25 us -> 54.1 us  [the longest x2 23.6 us: backward_scan(): pl.pallas_call(functools.partial(backward_kernel, sizes), grid=(stop - fi...]
    dot_general x8 -> x0, matrix products: 19.4 us -> none  [dot(): lax.dot_general(left, right, (((left_dim,), (right_dim,)), ((), ())), pre...]
    ppermute x32 -> x44, starting transfers between devices: 37.9 us -> 48.7 us  [swap(): return lax.ppermute(value, axis, [(i, i ^ step) for i in range(count)])]
    select_n x21 -> x0, other arithmetic: 7.21 us -> none  [gather(): held = jnp.where(bit == 0, low, high)]
    reshape x5 -> x2, local copies, waits for them, and re-layouts: 6.33 us -> 0.01 us  [the longest x1 0.01 us: body(): x_sums[:CONV_WIDTH + 1].reshape(-1)]
    dynamic_slice x7 -> x2, local copies, waits for them, and re-layouts: 6.09 us -> 0.09 us  [the longest x1 0.08 us: body(): lax.dynamic_slice_in_dim(by_heads, head_index * feature_share, feature_sh...]
    add x16 -> x15, other arithmetic: 8.57 us -> 3.07 us  [the longest x9 3.04 us: reduce_steps(): total = keep.astype(f32) + got.astype(f32)]
  transfers between devices with their start and end apart: 32 -> 44, of which waited for: 18 -> 17; matrix products, arithmetic and copies ran while one was open for 29% -> 11% of each run, Pallas kernels for 0% -> 26%
where the time goes in v2:
time: 194 us; the launch traced here: 193 us
  Pallas kernels  67.2 us (35%)
  starting transfers between devices  48.7 us (25%)
  waiting for transfers between devices  43.1 us (22%)
  local copies, waits for them, and re-layouts  19.5 us (10%)
  other arithmetic  12.8 us (7%)
    ppermute x44, starting transfers between devices, swap(): return lax.ppermute(value, axis, [(i, i ^ step) for i in range(count)])  48.7 us
    ppermute x44, waiting for transfers between devices, swap(): return lax.ppermute(value, axis, [(i, i ^ step) for i in range(count)])  43.1 us
    pallas_call x2, Pallas kernels, backward_scan(): pl.pallas_call(functools.partial(backward_kernel, sizes), grid=(stop - fi...  23.6 us
    pallas_call x1, Pallas kernels, forward_scan(): pl.pallas_call(functools.partial(forward_kernel, (head_share, head_size,...  13 us
    pallas_call x1, Pallas kernels, mix(): pl.pallas_call(functools.partial(mix_kernel, (z_rels, o_rels, groups)), g...  10.6 us
    unnamed x109, local copies, waits for them, and re-layouts  10 us
    pallas_call x1, Pallas kernels, row_grads(): pl.pallas_call(functools.partial(rows_kernel, groups), grid=(count // BLO...  7.59 us
    pallas_call x1, Pallas kernels, gate(): pl.pallas_call(functools.partial(gate_kernel, (z_rels, o_rels, groups)),...  7.06 us
  transfers between devices with their start and end apart: 44, of which 17 were waited for; matrix products, arithmetic and copies ran while one was open for 11% of the time, Pallas kernels for 26%

profile of v2, /device:TPU:0, one launch (start us, length us, event | category | flops | bytes accessed | tf_op | source)
XLA Modules:
  0.0 192.9 jit_solution(9278875142236950210)
XLA Ops:
  0.7 3.0 %collective-permute-start.2 = (bf16[1024,256]{1,0:T(8,128)(2,1)}, bf16[1024,256]{1,0:T(8,128)(2,1)S(1)}, u32[]{:S(2)}, u32[]{:S(2)}) collective-permute-start(bf16[1024,256]{1,0:T(8,128)(2,1)} %refs_0_.7), channel_id=1, source_target_pairs={{0,2},{1,3},{2,0},{3,1},{4,6},{5,7},{6,4},{7,5},{8,10},{9,11},{10,... | collective-permute-start | bytes 1572872 | tf_op jit(solution)/shard_map/ppermute | solution.py:778
  5.5 2.7 %collective-permute-start = (bf16[1,128,768]{2,1,0:T(8,128)(2,1)S(1)}, bf16[1,128,768]{2,1,0:T(8,128)(2,1)S(1)}, u32[]{:S(2)}, u32[]{:S(2)}) collective-permute-start(bf16[1,128,768]{2,1,0:T(8,128)(2,1)S(1)} %fusion.11), channel_id=1, source_target_pairs={{0,16},{4,20},{8,24},{12,28},{16,0},{20,4},{24,8},{28,12},{1,17},{... | collective-permute-start | bytes 589832 | tf_op jit(solution)/shard_map/ppermute | solution.py:778
  9.2 1.6 collective-permute-start.1
  10.7 4.1 %collective-permute-done.1 = bf16[1,128,512]{2,1,0:T(8,128)(2,1)S(1)} collective-permute-done((bf16[1,128,512]{2,1,0:T(8,128)(2,1)S(1)}, bf16[1,128,512]{2,1,0:T(8,128)(2,1)S(1)}, u32[]{:S(2)}, u32[]{:S(2)}) %collective-permute-start.1) | collective-permute-done | bytes 131104 | tf_op jit(solution)/shard_map/ppermute | solution.py:778
  14.9 3.1 %collective-permute-done = bf16[1,128,768]{2,1,0:T(8,128)(2,1)S(1)} collective-permute-done((bf16[1,128,768]{2,1,0:T(8,128)(2,1)S(1)}, bf16[1,128,768]{2,1,0:T(8,128)(2,1)S(1)}, u32[]{:S(2)}, u32[]{:S(2)}) %collective-permute-start) | collective-permute-done | bytes 196640 | tf_op jit(solution)/shard_map/ppermute | solution.py:778
  18.8 3.4 %collective-permute-start.5 = (bf16[1,128,512]{2,1,0:T(8,128)(2,1)}, bf16[1,128,512]{2,1,0:T(8,128)(2,1)S(1)}, u32[]{:S(2)}, u32[]{:S(2)}) collective-permute-start(bf16[1,128,512]{2,1,0:T(8,128)(2,1)} %bitcast.65), channel_id=1, source_target_pairs={{0,16},{4,20},{8,24},{12,28},{16,0},{20,4},{24,8},{28,12},{1,17},{... | collective-permute-start | bytes 393224 | tf_op jit(solution)/shard_map/ppermute | solution.py:778
  22.2 8.1 %collective-permute-done.5 = bf16[1,128,512]{2,1,0:T(8,128)(2,1)S(1)} collective-permute-done((bf16[1,128,512]{2,1,0:T(8,128)(2,1)}, bf16[1,128,512]{2,1,0:T(8,128)(2,1)S(1)}, u32[]{:S(2)}, u32[]{:S(2)}) %collective-permute-start.5) | collective-permute-done | bytes 131104 | tf_op jit(solution)/shard_map/ppermute | solution.py:778
  34.8 2.0 %collective-permute-start.8 = (bf16[2,128,512]{2,1,0:T(8,128)(2,1)S(1)}, bf16[2,128,512]{2,1,0:T(8,128)(2,1)S(1)}, u32[]{:S(2)}, u32[]{:S(2)}) collective-permute-start(bf16[2,128,512]{2,1,0:T(8,128)(2,1)S(1)} %constant_dynamic-update-slice_fusion.6), channel_id=1, source_target_pairs={{0,16},{4,20},{8,24},{12,28},{16,0},{20,4},{24,8},{28,12},{1,17},{... | collective-permute-start | bytes 786440 | tf_op jit(solution)/shard_map/ppermute | solution.py:778
  37.3 2.5 %collective-permute-start.7 = (bf16[2,128,512]{2,1,0:T(8,128)(2,1)S(1)}, bf16[2,128,512]{2,1,0:T(8,128)(2,1)S(1)}, u32[]{:S(2)}, u32[]{:S(2)}) collective-permute-start(bf16[2,128,512]{2,1,0:T(8,128)(2,1)S(1)} %constant_dynamic-update-slice_fusion.4), channel_id=1, source_target_pairs={{0,8},{4,12},{8,0},{12,4},{16,24},{20,28},{24,16},{28,20},{1,9},{5... | collective-permute-start | bytes 786440 | tf_op jit(solution)/shard_map/ppermute | solution.py:778
  39.9 1.6 slice.237
  41.4 6.8 %collective-permute-done.8 = bf16[2,128,512]{2,1,0:T(8,128)(2,1)S(1)} collective-permute-done((bf16[2,128,512]{2,1,0:T(8,128)(2,1)S(1)}, bf16[2,128,512]{2,1,0:T(8,128)(2,1)S(1)}, u32[]{:S(2)}, u32[]{:S(2)}) %collective-permute-start.8) | collective-permute-done | bytes 262176 | tf_op jit(solution)/shard_map/ppermute | solution.py:778
  53.0 3.4 %collective-permute-start.13 = (bf16[4,128,512]{2,1,0:T(8,128)(2,1)S(1)}, bf16[4,128,512]{2,1,0:T(8,128)(2,1)S(1)}, u32[]{:S(2)}, u32[]{:S(2)}) collective-permute-start(bf16[4,128,512]{2,1,0:T(8,128)(2,1)S(1)} %constant_dynamic-update-slice_fusion.10.refs_6_), channel_id=1, source_target_pairs={{0,8},{4,12},{8,0},{12,4},{16,24},{20,28},{24,16},{28,20},{1,9},{5... | collective-permute-start | bytes 1572872 | tf_op jit(solution)/shard_map/ppermute | solution.py:778
  56.4 1.6 collective-permute-start.12
  58.1 13.0 %shard_map.279 = (bf16[1024,1024]{1,0:T(8,128)(2,1)}, f32[1024,128]{1,0:T(8,128)S(1)}, bf16[1024,512]{1,0:T(8,128)(2,1)}, bf16[1024,512]{1,0:T(8,128)(2,1)}, bf1...) custom-call(s32[3]{0:T(128)S(1)} %pad_add_fusion.me_ref.refs_0_, ...), custom_call_target="tpu_custom_call" | custom-call | flops 16000000000 | tf_op jit(solution)/shard_map/pallas_call | solution.py:260
  73.6 7.1 %shard_map.280 = (f32[1024,512]{1,0:T(8,128)}, bf16[1024,512]{1,0:T(8,128)(2,1)}, f32[8,1024]{1,0:T(8,128)S(1)}, bf16[1024,512]{1,0:T(8,128)(2,1)}, bf16[1024,512]{1,0:T(8,128)(2,1)}) custom-call(s32[3]{0:T(128)S(1)} %pad_add_fusion.me_ref.refs_0_, bf16[1024,256]{1,0:T(8,128)(2,1)S(1)} %copy-done.2, bf16[1024,256]{1,0:T(8,128)(2,1)S(1)} %collective-permute-done.15.refs_1_, ...), custom_call_target="tpu_custom_call" | custom-call | flops 8000000000 | tf_op jit(solution)/shard_map/pallas_call | solution.py:327
  82.9 3.2 %collective-permute-done.18 = f32[8,1024]{1,0:T(8,128)S(1)} collective-permute-done((f32[8,1024]{1,0:T(8,128)S(1)}, f32[8,1024]{1,0:T(8,128)S(1)}, u32[]{:S(2)}, u32[]{:S(2)}) %collective-permute-start.18) | collective-permute-done | bytes 32800 | tf_op jit(solution)/shard_map/ppermute | solution.py:778
  87.1 10.6 %shard_map.281 = (bf16[1024,512]{1,0:T(8,128)(2,1)}, bf16[1024,512]{1,0:T(8,128)(2,1)}, bf16[2,1024,256]{2,1,0:T(8,128)(2,1)}, bf16[2,1024,256]{2,1,0:T(8,128)(2...) custom-call(s32[3]{0:T(128)S(1)} %pad_add_fusion.me_ref.refs_0_, ...), custom_call_target="tpu_custom_call" | custom-call | flops 10000000000 | tf_op jit(solution)/shard_map/pallas_call | solution.py:423
  98.8 11.7 %shard_map.282 = (bf16[1024,896]{1,0:T(8,128)(2,1)}, bf16[4,512,128]{2,1,0:T(8,128)(2,1)S(1)}, f32[8,512]{1,0:T(8,128)S(1)}, f32[8,256]{1,0:T(8,128)S(1)}, f32[8...) custom-call(s32[3]{0:T(128)S(1)} %pad_add_fusion.me_ref.refs_0_, ...), custom_call_target="tpu_custom_call" | custom-call | flops 12000000000 | tf_op jit(solution)/shard_map/pallas_call | solution.py:646
  115.6 11.8 %shard_map.283 = (bf16[1024,896]{1,0:T(8,128)(2,1)}, bf16[4,512,128]{2,1,0:T(8,128)(2,1)S(1)}, f32[8,512]{1,0:T(8,128)S(1)}, f32[8,256]{1,0:T(8,128)S(1)}, f32[8...) custom-call(s32[3]{0:T(128)S(1)} %pad_add_fusion.me_ref.refs_0_, ...), custom_call_target="tpu_custom_call", output_to_operand_aliasing={{0}: (22, {})} | custom-call | flops 12000000000 | tf_op jit(solution)/shard_map/pallas_call | solution.py:646
  128.5 1.6 collective-permute-start.26
  130.4 7.6 %shard_map.284 = (bf16[2,1024,256]{2,1,0:T(8,128)(2,1)S(1)}, bf16[2,1024,256]{2,1,0:T(8,128)(2,1)}, f32[8,1024]{1,0:T(8,128)S(1)}, f32[8,1024]{1,0:T(8,128)S(1)}) custom-call(s32[3]{0:T(128)S(1)} %pad_add_fusion.me_ref.refs_0_, bf16[1024,256]{1,0:T(8,128)(2,1)S(1)} %copy-done.1, bf16[1024,256]{1,0:T(8,128)(2,1)S(1)} %copy-done.7, ...), custom_call_target="tpu_custom_call" | custom-call | flops 6000000000 | tf_op jit(solution)/shard_map/pallas_call | solution.py:753
  144.5 5.3 %shard_map.285 = (bf16[4,128,256]{2,1,0:T(8,128)(2,1)}, bf16[4,128,256]{2,1,0:T(8,128)(2,1)S(1)}, bf16[4,128,384]{2,1,0:T(8,128)(2,1)S(1)}, bf16[4,128,384]{2,1,0:T(8,128)(2,1)S(1)}) custom-call(s32[3]{0:T(128)S(1)} %pad_add_fusion.me_ref.refs_0_, bf16[1024,896]{1,0:T(8,128)(2,1)S(1)} %copy-done.18, bf16[512,128]{1,0:T(8,128)(2,1)S(1)} %fusion.9.refs_1_, ...), custom_call_target="tpu_custom_call" | custom-call | flops 5000000000 | tf_op jit(solution)/shard_map/pallas_call | solution.py:710
  151.0 1.6 collective-permute-start.34
  154.9 1.6 collective-permute-start.33
  160.7 4.4 %collective-permute-done.35 = f32[4632]{0:T(1024)S(1)} collective-permute-done((f32[4632]{0:T(1024)S(1)}, f32[4632]{0:T(1024)S(1)}, u32[]{:S(2)}, u32[]{:S(2)}) %collective-permute-start.35) | collective-permute-done | bytes 18560 | tf_op jit(solution)/shard_map/ppermute | solution.py:778
  166.6 2.1 %collective-permute-done.33 = bf16[4,128,384]{2,1,0:T(8,128)(2,1)} collective-permute-done((bf16[4,128,384]{2,1,0:T(8,128)(2,1)S(1)}, bf16[4,128,384]{2,1,0:T(8,128)(2,1)}, u32[]{:S(2)}, u32[]{:S(2)}) %collective-permute-start.33) | collective-permute-done | bytes 393248 | tf_op jit(solution)/shard_map/ppermute | solution.py:778
  170.6 2.6 %collective-permute-start.39 = (bf16[2,128,384]{2,1,0:T(8,128)(2,1)S(1)}, bf16[2,128,384]{2,1,0:T(8,128)(2,1)S(1)}, u32[]{:S(2)}, u32[]{:S(2)}) collective-permute-start(bf16[2,128,384]{2,1,0:T(8,128)(2,1)S(1)} %slice.302), channel_id=1, source_target_pairs={{0,16},{4,20},{8,24},{12,28},{16,0},{20,4},{24,8},{28,12},{1,17},{... | collective-permute-start | bytes 589832 | tf_op jit(solution)/shard_map/ppermute | solution.py:778
  173.9 2.5 %fusion.5 = bf16[1024,256]{1,0:T(8,128)(2,1)} fusion(bf16[1024,256]{1,0:T(8,128)(2,1)S(1)} %copy-done.1, bf16[1,1024,256]{2,1,0:T(8,128)(2,1)} %collective-permute-done.34, bf16[1024,256]{1,0:T(8,128)(2,1)S(1)} %copy-done.2, f32[1024]{0:T(1024)S(1)} %broadcast_multiply_fusion, f32[256]{0:T(256)S(1)} %dynamic_slice.11, ...), kind=kLoop, calls=%fused_computation.8 | loop fusion | flops 3670016 | bytes 3154944 | tf_op jit(solution)/shard_map/convert_element_type | solution.py:1100
  176.4 1.6 add_bitcast_fusion.1
  179.2 2.8 %collective-permute-done.39 = bf16[2,128,384]{2,1,0:T(8,128)(2,1)S(1)} collective-permute-done((bf16[2,128,384]{2,1,0:T(8,128)(2,1)S(1)}, bf16[2,128,384]{2,1,0:T(8,128)(2,1)S(1)}, u32[]{:S(2)}, u32[]{:S(2)}) %collective-permute-start.39) | collective-permute-done | bytes 196640 | tf_op jit(solution)/shard_map/ppermute | solution.py:778
  183.3 2.6 %collective-permute-start.41 = (bf16[1,128,256]{2,1,0:T(8,128)(2,1)S(1)}, bf16[1,128,256]{2,1,0:T(8,128)(2,1)S(1)}, u32[]{:S(2)}, u32[]{:S(2)}) collective-permute-start(bf16[1,128,256]{2,1,0:T(8,128)(2,1)S(1)} %slice.307), channel_id=1, source_target_pairs={{0,16},{4,20},{8,24},{12,28},{16,0},{20,4},{24,8},{28,12},{1,17},{... | collective-permute-start | bytes 196616 | tf_op jit(solution)/shard_map/ppermute | solution.py:778
  185.9 1.6 collective-permute-start.42
  (261 shorter events, 52.1 us)
Async XLA Ops:
  0.7 17.3 %collective-permute-start.2 = (bf16[1024,256]{1,0:T(8,128)(2,1)}, bf16[1024,256]{1,0:T(8,128)(2,1)S(1)}, u32[]{:S(2)}, u32[]{:S(2)}) collective-permute-start(bf16[1024,256]{1,0:T(8,128)(2,1)} %refs_0_.7), channel_id=1, source_target_pairs={{0,2},{1,3},{2,0},{3,1},{4,6},{5,7},{6,4},{7,5},{8,10},{9,11},{10,... | collective-permute-start | bytes 1572872 | tf_op jit(solution)/shard_map/ppermute | solution.py:778
  3.7 14.3 %collective-permute-start.3 = (bf16[1024,256]{1,0:T(8,128)(2,1)}, bf16[1024,256]{1,0:T(8,128)(2,1)S(1)}, u32[]{:S(2)}, u32[]{:S(2)}) collective-permute-start(bf16[1024,256]{1,0:T(8,128)(2,1)} %refs_0_.7), channel_id=1, source_target_pairs={{0,1},{1,0},{2,3},{3,2},{4,5},{5,4},{6,7},{7,6},{8,9},{9,8},{10,11... | collective-permute-start | bytes 1572872 | tf_op jit(solution)/shard_map/ppermute | solution.py:778
  5.5 12.5 %collective-permute-start = (bf16[1,128,768]{2,1,0:T(8,128)(2,1)S(1)}, bf16[1,128,768]{2,1,0:T(8,128)(2,1)S(1)}, u32[]{:S(2)}, u32[]{:S(2)}) collective-permute-start(bf16[1,128,768]{2,1,0:T(8,128)(2,1)S(1)} %fusion.11), channel_id=1, source_target_pairs={{0,16},{4,20},{8,24},{12,28},{16,0},{20,4},{24,8},{28,12},{1,17},{... | collective-permute-start | bytes 589832 | tf_op jit(solution)/shard_map/ppermute | solution.py:778
  18.1 13.6 %collective-permute-start.4 = (bf16[2,128,768]{2,1,0:T(8,128)(2,1)S(1)}, bf16[2,128,768]{2,1,0:T(8,128)(2,1)S(1)}, u32[]{:S(2)}, u32[]{:S(2)}) collective-permute-start(bf16[2,128,768]{2,1,0:T(8,128)(2,1)S(1)} %constant_dynamic-update-slice_fusion), channel_id=1, source_target_pairs={{0,8},{4,12},{8,0},{12,4},{16,24},{20,28},{24,16},{28,20},{1,9},{5... | collective-permute-start | bytes 1179656 | tf_op jit(solution)/shard_map/ppermute | solution.py:778
  18.8 11.5 %collective-permute-start.5 = (bf16[1,128,512]{2,1,0:T(8,128)(2,1)}, bf16[1,128,512]{2,1,0:T(8,128)(2,1)S(1)}, u32[]{:S(2)}, u32[]{:S(2)}) collective-permute-start(bf16[1,128,512]{2,1,0:T(8,128)(2,1)} %bitcast.65), channel_id=1, source_target_pairs={{0,16},{4,20},{8,24},{12,28},{16,0},{20,4},{24,8},{28,12},{1,17},{... | collective-permute-start | bytes 393224 | tf_op jit(solution)/shard_map/ppermute | solution.py:778
  33.3 18.6 %collective-permute-start.6 = (bf16[4,128,768]{2,1,0:T(8,128)(2,1)}, bf16[4,128,768]{2,1,0:T(8,128)(2,1)}, u32[]{:S(2)}, u32[]{:S(2)}) collective-permute-start(bf16[4,128,768]{2,1,0:T(8,128)(2,1)} %constant_dynamic-update-slice_fusion.2.refs_4_), channel_id=1, source_target_pairs={{0,4},{4,0},{8,12},{12,8},{16,20},{20,16},{24,28},{28,24},{1,5},{5... | collective-permute-start | bytes 2359304 | tf_op jit(solution)/shard_map/ppermute | solution.py:778
  34.8 13.5 %collective-permute-start.8 = (bf16[2,128,512]{2,1,0:T(8,128)(2,1)S(1)}, bf16[2,128,512]{2,1,0:T(8,128)(2,1)S(1)}, u32[]{:S(2)}, u32[]{:S(2)}) collective-permute-start(bf16[2,128,512]{2,1,0:T(8,128)(2,1)S(1)} %constant_dynamic-update-slice_fusion.6), channel_id=1, source_target_pairs={{0,16},{4,20},{8,24},{12,28},{16,0},{20,4},{24,8},{28,12},{1,17},{... | collective-permute-start | bytes 786440 | tf_op jit(solution)/shard_map/ppermute | solution.py:778
  36.8 13.2 %collective-permute-start.9 = (bf16[1024,256]{1,0:T(8,128)(2,1)S(1)}, bf16[1024,256]{1,0:T(8,128)(2,1)S(1)}, u32[]{:S(2)}, u32[]{:S(2)}) collective-permute-start(bf16[1024,256]{1,0:T(8,128)(2,1)S(1)} %collective-permute-done.2.refs_2_), channel_id=1, source_target_pairs={{0,1},{1,0},{2,3},{3,2},{4,5},{5,4},{6,7},{7,6},{8,9},{9,8},{10,11... | collective-permute-start | bytes 1572872 | tf_op jit(solution)/shard_map/ppermute | solution.py:778
  36.8 14.4 %collective-permute-start.10 = (bf16[1024,256]{1,0:T(8,128)(2,1)S(1)}, bf16[1024,256]{1,0:T(8,128)(2,1)}, u32[]{:S(2)}, u32[]{:S(2)}) collective-permute-start(bf16[1024,256]{1,0:T(8,128)(2,1)S(1)} %copy-done.2), channel_id=1, source_target_pairs={{0,2},{1,3},{2,0},{3,1},{4,6},{5,7},{6,4},{7,5},{8,10},{9,11},{10,... | collective-permute-start | bytes 1572872 | tf_op jit(solution)/shard_map/ppermute | solution.py:778
  37.3 12.6 %collective-permute-start.7 = (bf16[2,128,512]{2,1,0:T(8,128)(2,1)S(1)}, bf16[2,128,512]{2,1,0:T(8,128)(2,1)S(1)}, u32[]{:S(2)}, u32[]{:S(2)}) collective-permute-start(bf16[2,128,512]{2,1,0:T(8,128)(2,1)S(1)} %constant_dynamic-update-slice_fusion.4), channel_id=1, source_target_pairs={{0,8},{4,12},{8,0},{12,4},{16,24},{20,28},{24,16},{28,20},{1,9},{5... | collective-permute-start | bytes 786440 | tf_op jit(solution)/shard_map/ppermute | solution.py:778
  49.8 22.9 %collective-permute-start.15 = (bf16[1024,256]{1,0:T(8,128)(2,1)S(1)}, bf16[1024,256]{1,0:T(8,128)(2,1)S(1)}, u32[]{:S(2)}, u32[]{:S(2)}) collective-permute-start(bf16[1024,256]{1,0:T(8,128)(2,1)S(1)} %copy-done.2), channel_id=1, source_target_pairs={{0,1},{1,0},{2,3},{3,2},{4,5},{5,4},{6,7},{7,6},{8,9},{9,8},{10,11... | collective-permute-start | bytes 1572872 | tf_op jit(solution)/shard_map/ppermute | solution.py:778
  53.0 19.8 %collective-permute-start.13 = (bf16[4,128,512]{2,1,0:T(8,128)(2,1)S(1)}, bf16[4,128,512]{2,1,0:T(8,128)(2,1)S(1)}, u32[]{:S(2)}, u32[]{:S(2)}) collective-permute-start(bf16[4,128,512]{2,1,0:T(8,128)(2,1)S(1)} %constant_dynamic-update-slice_fusion.10.refs_6_), channel_id=1, source_target_pairs={{0,8},{4,12},{8,0},{12,4},{16,24},{20,28},{24,16},{28,20},{1,9},{5... | collective-permute-start | bytes 1572872 | tf_op jit(solution)/shard_map/ppermute | solution.py:778
  56.4 16.3 %collective-permute-start.12 = (bf16[4,128,512]{2,1,0:T(8,128)(2,1)S(1)}, bf16[4,128,512]{2,1,0:T(8,128)(2,1)S(1)}, u32[]{:S(2)}, u32[]{:S(2)}) collective-permute-start(bf16[4,128,512]{2,1,0:T(8,128)(2,1)S(1)} %constant_dynamic-update-slice_fusion.8.refs_4_), channel_id=1, source_target_pairs={{0,4},{4,0},{8,12},{12,8},{16,20},{20,16},{24,28},{28,24},{1,5},{5... | collective-permute-start | bytes 1572872 | tf_op jit(solution)/shard_map/ppermute | solution.py:778
  58.0 14.8 %collective-permute-start.16 = (bf16[1024,256]{1,0:T(8,128)(2,1)}, bf16[1024,256]{1,0:T(8,128)(2,1)S(1)}, u32[]{:S(2)}, u32[]{:S(2)}) collective-permute-start(bf16[1024,256]{1,0:T(8,128)(2,1)} %collective-permute-done.10.refs_2_), channel_id=1, source_target_pairs={{0,1},{1,0},{2,3},{3,2},{4,5},{5,4},{6,7},{7,6},{8,9},{9,8},{10,11... | collective-permute-start | bytes 1572872 | tf_op jit(solution)/shard_map/ppermute | solution.py:778
  97.7 14.7 %collective-permute-start.21 = (bf16[2,1024,256]{2,1,0:T(8,128)(2,1)}, bf16[2,1024,256]{2,1,0:T(8,128)(2,1)S(1)}, u32[]{:S(2)}, u32[]{:S(2)}) collective-permute-start(bf16[2,1024,256]{2,1,0:T(8,128)(2,1)} %get-tuple-element.226), channel_id=1, source_target_pairs={{0,1},{1,0},{2,3},{3,2},{4,5},{5,4},{6,7},{7,6},{8,9},{9,8},{10,11... | collective-permute-start | bytes 3145736 | tf_op jit(solution)/shard_map/ppermute | solution.py:778
  97.8 14.3 %collective-permute-start.19 = (bf16[4,128,512]{2,1,0:T(8,128)(2,1)S(1)}, bf16[4,128,512]{2,1,0:T(8,128)(2,1)S(1)}, u32[]{:S(2)}, u32[]{:S(2)}) collective-permute-start(bf16[4,128,512]{2,1,0:T(8,128)(2,1)S(1)} %get-tuple-element.222), channel_id=1, source_target_pairs={{0,4},{4,0},{8,12},{12,8},{16,20},{20,16},{24,28},{28,24},{1,5},{5... | collective-permute-start | bytes 1572872 | tf_op jit(solution)/shard_map/ppermute | solution.py:778
  98.4 14.0 %collective-permute-start.20 = (bf16[4,128,512]{2,1,0:T(8,128)(2,1)S(1)}, bf16[4,128,512]{2,1,0:T(8,128)(2,1)S(1)}, u32[]{:S(2)}, u32[]{:S(2)}) collective-permute-start(bf16[4,128,512]{2,1,0:T(8,128)(2,1)S(1)} %get-tuple-element.224), channel_id=1, source_target_pairs={{0,8},{4,12},{8,0},{12,4},{16,24},{20,28},{24,16},{28,20},{1,9},{5... | collective-permute-start | bytes 1572872 | tf_op jit(solution)/shard_map/ppermute | solution.py:778
  112.8 15.6 %collective-permute-start.24 = (bf16[1,1024,256]{2,1,0:T(8,128)(2,1)S(1)}, bf16[1,1024,256]{2,1,0:T(8,128)(2,1)S(1)}, u32[]{:S(2)}, u32[]{:S(2)}) collective-permute-start(bf16[1,1024,256]{2,1,0:T(8,128)(2,1)S(1)} %slice.299), channel_id=1, source_target_pairs={{0,2},{1,3},{2,0},{3,1},{4,6},{5,7},{6,4},{7,5},{8,10},{9,11},{10,... | collective-permute-start | bytes 1572872 | tf_op jit(solution)/shard_map/ppermute | solution.py:778
  113.5 14.9 %collective-permute-start.23 = (bf16[2,128,512]{2,1,0:T(8,128)(2,1)S(1)}, bf16[2,128,512]{2,1,0:T(8,128)(2,1)S(1)}, u32[]{:S(2)}, u32[]{:S(2)}) collective-permute-start(bf16[2,128,512]{2,1,0:T(8,128)(2,1)S(1)} %slice.300), channel_id=1, source_target_pairs={{0,16},{4,20},{8,24},{12,28},{16,0},{20,4},{24,8},{28,12},{1,17},{... | collective-permute-start | bytes 786440 | tf_op jit(solution)/shard_map/ppermute | solution.py:778
  115.2 13.2 %collective-permute-start.22 = (bf16[2,128,512]{2,1,0:T(8,128)(2,1)S(1)}, bf16[2,128,512]{2,1,0:T(8,128)(2,1)S(1)}, u32[]{:S(2)}, u32[]{:S(2)}) collective-permute-start(bf16[2,128,512]{2,1,0:T(8,128)(2,1)S(1)} %slice.301), channel_id=1, source_target_pairs={{0,8},{4,12},{8,0},{12,4},{16,24},{20,28},{24,16},{28,20},{1,9},{5... | collective-permute-start | bytes 786440 | tf_op jit(solution)/shard_map/ppermute | solution.py:778
  128.4 9.6 %collective-permute-start.25 = (bf16[512,128]{1,0:T(8,128)(2,1)S(1)}, bf16[512,128]{1,0:T(8,128)(2,1)S(1)}, u32[]{:S(2)}, u32[]{:S(2)}) collective-permute-start(bf16[512,128]{1,0:T(8,128)(2,1)S(1)} %get-tuple-element.366), channel_id=1, source_target_pairs={{0,1},{1,0},{2,3},{3,2},{4,5},{5,4},{6,7},{7,6},{8,9},{9,8},{10,11... | collective-permute-start | bytes 393224 | tf_op jit(solution)/shard_map/ppermute | solution.py:778
  128.5 9.5 %collective-permute-start.26 = (bf16[512,128]{1,0:T(8,128)(2,1)S(1)}, bf16[512,128]{1,0:T(8,128)(2,1)S(1)}, u32[]{:S(2)}, u32[]{:S(2)}) collective-permute-start(bf16[512,128]{1,0:T(8,128)(2,1)S(1)} %get-tuple-element.365), channel_id=1, source_target_pairs={{0,2},{1,3},{2,0},{3,1},{4,6},{5,7},{6,4},{7,5},{8,10},{9,11},{10,... | collective-permute-start | bytes 393224 | tf_op jit(solution)/shard_map/ppermute | solution.py:778
  138.1 11.8 %collective-permute-start.28 = (bf16[2,1024,256]{2,1,0:T(8,128)(2,1)S(1)}, bf16[2,1024,256]{2,1,0:T(8,128)(2,1)}, u32[]{:S(2)}, u32[]{:S(2)}) collective-permute-start(bf16[2,1024,256]{2,1,0:T(8,128)(2,1)S(1)} %get-tuple-element.275), channel_id=1, source_target_pairs={{0,1},{1,0},{2,3},{3,2},{4,5},{5,4},{6,7},{7,6},{8,9},{9,8},{10,11... | collective-permute-start | bytes 3145736 | tf_op jit(solution)/shard_map/ppermute | solution.py:778
  140.0 9.8 %collective-permute-start.29 = (f32[3328]{0:T(1024)S(1)}, f32[3328]{0:T(1024)S(1)}, u32[]{:S(2)}, u32[]{:S(2)}) collective-permute-start(f32[3328]{0:T(1024)S(1)} %pad_maximum_fusion.1), channel_id=1, source_target_pairs={{0,1},{1,0},{2,3},{3,2},{4,5},{5,4},{6,7},{7,6},{8,9},{9,8},{10,11... | collective-permute-start | bytes 39944 | tf_op jit(solution)/shard_map/ppermute | solution.py:778
  140.2 9.6 %collective-permute-start.30 = (f32[3328]{0:T(1024)S(1)}, f32[3328]{0:T(1024)S(1)}, u32[]{:S(2)}, u32[]{:S(2)}) collective-permute-start(f32[3328]{0:T(1024)S(1)} %pad_maximum_fusion.1), channel_id=1, source_target_pairs={{0,2},{1,3},{2,0},{3,1},{4,6},{5,7},{6,4},{7,5},{8,10},{9,11},{10,... | collective-permute-start | bytes 39944 | tf_op jit(solution)/shard_map/ppermute | solution.py:778
  151.0 17.6 %collective-permute-start.34 = (bf16[1,1024,256]{2,1,0:T(8,128)(2,1)S(1)}, bf16[1,1024,256]{2,1,0:T(8,128)(2,1)}, u32[]{:S(2)}, u32[]{:S(2)}) collective-permute-start(bf16[1,1024,256]{2,1,0:T(8,128)(2,1)S(1)} %add_convert_fusion), channel_id=1, source_target_pairs={{0,2},{1,3},{2,0},{3,1},{4,6},{5,7},{6,4},{7,5},{8,10},{9,11},{10,... | collective-permute-start | bytes 1572872 | tf_op jit(solution)/shard_map/ppermute | solution.py:778
  153.4 13.1 %collective-permute-start.36 = (bf16[1,128,512]{2,1,0:T(8,128)(2,1)}, bf16[1,128,512]{2,1,0:T(8,128)(2,1)}, u32[]{:S(2)}, u32[]{:S(2)}) collective-permute-start(bf16[1,128,512]{2,1,0:T(8,128)(2,1)} %slice.305), channel_id=1, source_target_pairs={{0,16},{4,20},{8,24},{12,28},{16,0},{20,4},{24,8},{28,12},{1,17},{... | collective-permute-start | bytes 393224 | tf_op jit(solution)/shard_map/ppermute | solution.py:778
  154.9 13.7 %collective-permute-start.33 = (bf16[4,128,384]{2,1,0:T(8,128)(2,1)S(1)}, bf16[4,128,384]{2,1,0:T(8,128)(2,1)}, u32[]{:S(2)}, u32[]{:S(2)}) collective-permute-start(bf16[4,128,384]{2,1,0:T(8,128)(2,1)S(1)} %get-tuple-element.293), channel_id=1, source_target_pairs={{0,8},{4,12},{8,0},{12,4},{16,24},{20,28},{24,16},{28,20},{1,9},{5... | collective-permute-start | bytes 1179656 | tf_op jit(solution)/shard_map/ppermute | solution.py:778
  156.6 10.0 %collective-permute-start.32 = (bf16[4,128,256]{2,1,0:T(8,128)(2,1)}, bf16[4,128,256]{2,1,0:T(8,128)(2,1)S(1)}, u32[]{:S(2)}, u32[]{:S(2)}) collective-permute-start(bf16[4,128,256]{2,1,0:T(8,128)(2,1)} %get-tuple-element.291), channel_id=1, source_target_pairs={{0,4},{4,0},{8,12},{12,8},{16,20},{20,16},{24,28},{28,24},{1,5},{5... | collective-permute-start | bytes 786440 | tf_op jit(solution)/shard_map/ppermute | solution.py:778
  165.1 13.0 %collective-permute-start.37 = (bf16[1,128,512]{2,1,0:T(8,128)(2,1)S(1)}, bf16[1,128,512]{2,1,0:T(8,128)(2,1)S(1)}, u32[]{:S(2)}, u32[]{:S(2)}) collective-permute-start(bf16[1,128,512]{2,1,0:T(8,128)(2,1)S(1)} %slice.304), channel_id=1, source_target_pairs={{0,4},{4,0},{8,12},{12,8},{16,20},{20,16},{24,28},{28,24},{1,5},{5... | collective-permute-start | bytes 393224 | tf_op jit(solution)/shard_map/ppermute | solution.py:778
  168.7 9.4 %collective-permute-start.40 = (f32[4632]{0:T(1024)S(1)}, f32[4632]{0:T(1024)S(1)}, u32[]{:S(2)}, u32[]{:S(2)}) collective-permute-start(f32[4632]{0:T(1024)S(1)} %add.134), channel_id=1, source_target_pairs={{0,8},{4,12},{8,0},{12,4},{16,24},{20,28},{24,16},{28,20},{1,9},{5... | collective-permute-start | bytes 55592 | tf_op jit(solution)/shard_map/ppermute | solution.py:778
  170.6 11.4 %collective-permute-start.39 = (bf16[2,128,384]{2,1,0:T(8,128)(2,1)S(1)}, bf16[2,128,384]{2,1,0:T(8,128)(2,1)S(1)}, u32[]{:S(2)}, u32[]{:S(2)}) collective-permute-start(bf16[2,128,384]{2,1,0:T(8,128)(2,1)S(1)} %slice.302), channel_id=1, source_target_pairs={{0,16},{4,20},{8,24},{12,28},{16,0},{20,4},{24,8},{28,12},{1,17},{... | collective-permute-start | bytes 589832 | tf_op jit(solution)/shard_map/ppermute | solution.py:778
  (66 other events, 757.8 us)

commit v3 on v2

--- a/solution.py
+++ b/solution.py
@@ -16,7 +16,7 @@
 highest = lax.Precision.HIGHEST
 f32 = jnp.float32
 bf16 = jnp.bfloat16
-VMEM_LIMIT = 50 * 1024 * 1024
+VMEM_LIMIT = 53 * 1024 * 1024
 
 
 def dot(left, right, left_dim=1, right_dim=0, precision=None):
@@ -670,7 +670,7 @@
 
 def late_kernel(sizes, me_ref, *refs):
     a_rels, b_rels, inner, half = sizes
-    late_ref, state_ref, normed_ref, a_send, a_keep, b_send, b_keep, total = refs
+    late_ref, *state_refs, normed_ref, a_send, a_keep, b_send, b_keep, total = refs
 
     @pl.when(pl.program_id(0) == 0)
     def _():
@@ -680,7 +680,7 @@
     width = LANES // 2
     turn = lambda v: jnp.concatenate([v[:, width:], v[:, :width]], axis=1)
     steps = turn(late_ref[:, rest:])
-    state = state_ref[...]
+    state = sum(ref[...].astype(f32) for ref in state_refs).astype(bf16)
     state = jnp.where(pl.program_id(0) < pl.num_programs(0) // 2, state, turn(state))
     first = lax.broadcasted_iota(jnp.int32, (BLOCK, LANES), 1) < width
     both = jnp.concatenate([late_ref[:, :inner], jnp.where(first, state, steps)], axis=1)
@@ -698,7 +698,7 @@
                     to[i] = total[row_of(me_ref[0] ^ rel, size), columns].astype(bf16)
 
 
-def late_grads(me, late, state, normed, inner, half, shards, a_rels, b_rels):
+def late_grads(me, late, states, normed, inner, half, shards, a_rels, b_rels):
     count, wide = late.shape
     features = normed.shape[1]
     size = features // shards
@@ -710,13 +710,13 @@
     return pl.pallas_call(
         functools.partial(late_kernel, (a_rels, b_rels, inner, half)),
         grid=(count // BLOCK,),
-        in_specs=[scalar_spec(), per(wide), packed, per(features)],
+        in_specs=[scalar_spec(), per(wide)] + [packed] * len(states) + [per(features)],
         out_specs=[pl.BlockSpec(dims, lambda i: (0, 0, 0)) for dims in outs],
         out_shape=[out(dims, bf16) for dims in outs],
         scratch_shapes=[pltpu.VMEM((features, inner + LANES), f32)],
         compiler_params=params(),
         cost_estimate=cost(5),
-    )(me, late, state, normed)
+    )(me, late, *states, normed)
 
 
 def rows_kernel(groups, me_ref, *refs):
@@ -1049,7 +1049,6 @@
         ),
     )
 
-    state_total = sum((part.astype(f32) for part in state_got), state_parts[0].astype(f32)).astype(bf16)
     b_sums = near[1:] + near[:1]
     rows_x = Exchange(pair_steps(rows_send, rows_keep, "heads", [1, 2]))
     by_heads = jnp.concatenate([gain_grad[0], stat[0], s_sums[: CONV_WIDTH + 1].reshape(-1)])
@@ -1058,7 +1057,7 @@
         [rows_x, z_x, o_x],
         (
             late_grads(
-                me, late, state_total, normed, inner_share, half, shards, halves_of(near), halves_of(b_sums)
+                me, late, (state_parts[0], *state_got), normed, inner_share, half, shards, halves_of(near), halves_of(b_sums)
             ),
             by_heads,
             [swap(by_heads, "heads", step) for step in (1, 2, 3)],

time: 194 us -> 190 us (0.979)
  local copies, waits for them, and re-layouts: 19.5 us -> 12.2 us
  Pallas kernels: 67.2 us -> 70.9 us
  other arithmetic: 12.8 us -> 10.4 us
  waiting for transfers between devices: 43.1 us -> 45.5 us
    unnamed x109 -> x95, local copies, waits for them, and re-layouts: 10 us -> 6.52 us
    ppermute x44, waiting for transfers between devices: 43.1 us -> 45.5 us  [swap(): return lax.ppermute(value, axis, [(i, i ^ step) for i in range(count)])]
  transfers between devices with their start and end apart: 44 -> 44, of which waited for: 17 -> 17; matrix products, arithmetic and copies ran while one was open for 11% -> 9% of each run, Pallas kernels for 26% -> 27%
where the time goes in v3:
time: 190 us; the launch traced here: 189 us
  Pallas kernels  70.9 us (37%)
  starting transfers between devices  48.9 us (26%)
  waiting for transfers between devices  45.5 us (24%)
  local copies, waits for them, and re-layouts  12.2 us (6%)
  other arithmetic  10.4 us (5%)
    ppermute x44, starting transfers between devices, swap(): return lax.ppermute(value, axis, [(i, i ^ step) for i in range(count)])  48.9 us
    ppermute x44, waiting for transfers between devices, swap(): return lax.ppermute(value, axis, [(i, i ^ step) for i in range(count)])  45.5 us
    pallas_call x2, Pallas kernels, backward_scan(): pl.pallas_call(functools.partial(backward_kernel, sizes), grid=(stop - fi...  24.2 us
    pallas_call x1, Pallas kernels, forward_scan(): pl.pallas_call(functools.partial(forward_kernel, (head_share, head_size,...  13.4 us
    pallas_call x1, Pallas kernels, mix(): pl.pallas_call(functools.partial(mix_kernel, (z_rels, o_rels, groups)), g...  11.1 us
    pallas_call x1, Pallas kernels, row_grads(): pl.pallas_call(functools.partial(rows_kernel, groups), grid=(count // BLO...  8.35 us
    pallas_call x1, Pallas kernels, gate(): pl.pallas_call(functools.partial(gate_kernel, (z_rels, o_rels, groups)),...  7.78 us
    unnamed x95, local copies, waits for them, and re-layouts  6.52 us
  transfers between devices with their start and end apart: 44, of which 17 were waited for; matrix products, arithmetic and copies ran while one was open for 9% of the time, Pallas kernels for 27%

profile of v3, /device:TPU:0, one launch (start us, length us, event | category | flops | bytes accessed | tf_op | source)
XLA Modules:
  0.0 189.5 jit_solution(4501093247057228323)
XLA Ops:
  0.7 3.0 %collective-permute-start.2 = (bf16[1024,256]{1,0:T(8,128)(2,1)}, bf16[1024,256]{1,0:T(8,128)(2,1)S(1)}, u32[]{:S(2)}, u32[]{:S(2)}) collective-permute-start(bf16[1024,256]{1,0:T(8,128)(2,1)} %refs_0_.7), channel_id=1, source_target_pairs={{0,2},{1,3},{2,0},{3,1},{4,6},{5,7},{6,4},{7,5},{8,10},{9,11},{10,... | collective-permute-start | bytes 1572872 | tf_op jit(solution)/shard_map/ppermute | solution.py:778
  5.5 2.7 %collective-permute-start = (bf16[1,128,768]{2,1,0:T(8,128)(2,1)S(1)}, bf16[1,128,768]{2,1,0:T(8,128)(2,1)S(1)}, u32[]{:S(2)}, u32[]{:S(2)}) collective-permute-start(bf16[1,128,768]{2,1,0:T(8,128)(2,1)S(1)} %fusion.8), channel_id=1, source_target_pairs={{0,16},{4,20},{8,24},{12,28},{16,0},{20,4},{24,8},{28,12},{1,17},{... | collective-permute-start | bytes 589832 | tf_op jit(solution)/shard_map/ppermute | solution.py:778
  9.2 1.6 collective-permute-start.1
  10.7 4.1 %collective-permute-done.1 = bf16[1,128,512]{2,1,0:T(8,128)(2,1)S(1)} collective-permute-done((bf16[1,128,512]{2,1,0:T(8,128)(2,1)S(1)}, bf16[1,128,512]{2,1,0:T(8,128)(2,1)S(1)}, u32[]{:S(2)}, u32[]{:S(2)}) %collective-permute-start.1) | collective-permute-done | bytes 131104 | tf_op jit(solution)/shard_map/ppermute | solution.py:778
  14.9 3.1 %collective-permute-done = bf16[1,128,768]{2,1,0:T(8,128)(2,1)S(1)} collective-permute-done((bf16[1,128,768]{2,1,0:T(8,128)(2,1)S(1)}, bf16[1,128,768]{2,1,0:T(8,128)(2,1)S(1)}, u32[]{:S(2)}, u32[]{:S(2)}) %collective-permute-start) | collective-permute-done | bytes 196640 | tf_op jit(solution)/shard_map/ppermute | solution.py:778
  18.8 3.4 %collective-permute-start.5 = (bf16[1,128,512]{2,1,0:T(8,128)(2,1)}, bf16[1,128,512]{2,1,0:T(8,128)(2,1)S(1)}, u32[]{:S(2)}, u32[]{:S(2)}) collective-permute-start(bf16[1,128,512]{2,1,0:T(8,128)(2,1)} %bitcast.64), channel_id=1, source_target_pairs={{0,16},{4,20},{8,24},{12,28},{16,0},{20,4},{24,8},{28,12},{1,17},{... | collective-permute-start | bytes 393224 | tf_op jit(solution)/shard_map/ppermute | solution.py:778
  22.2 8.1 %collective-permute-done.5 = bf16[1,128,512]{2,1,0:T(8,128)(2,1)S(1)} collective-permute-done((bf16[1,128,512]{2,1,0:T(8,128)(2,1)}, bf16[1,128,512]{2,1,0:T(8,128)(2,1)S(1)}, u32[]{:S(2)}, u32[]{:S(2)}) %collective-permute-start.5) | collective-permute-done | bytes 131104 | tf_op jit(solution)/shard_map/ppermute | solution.py:778
  31.8 1.6 collective-permute-start.6
  33.4 2.0 %collective-permute-start.8 = (bf16[2,128,512]{2,1,0:T(8,128)(2,1)S(1)}, bf16[2,128,512]{2,1,0:T(8,128)(2,1)S(1)}, u32[]{:S(2)}, u32[]{:S(2)}) collective-permute-start(bf16[2,128,512]{2,1,0:T(8,128)(2,1)S(1)} %constant_dynamic-update-slice_fusion.6), channel_id=1, source_target_pairs={{0,16},{4,20},{8,24},{12,28},{16,0},{20,4},{24,8},{28,12},{1,17},{... | collective-permute-start | bytes 786440 | tf_op jit(solution)/shard_map/ppermute | solution.py:778
  35.9 2.5 %collective-permute-start.7 = (bf16[2,128,512]{2,1,0:T(8,128)(2,1)S(1)}, bf16[2,128,512]{2,1,0:T(8,128)(2,1)S(1)}, u32[]{:S(2)}, u32[]{:S(2)}) collective-permute-start(bf16[2,128,512]{2,1,0:T(8,128)(2,1)S(1)} %constant_dynamic-update-slice_fusion.4), channel_id=1, source_target_pairs={{0,8},{4,12},{8,0},{12,4},{16,24},{20,28},{24,16},{28,20},{1,9},{5... | collective-permute-start | bytes 786440 | tf_op jit(solution)/shard_map/ppermute | solution.py:778
  38.5 8.3 %collective-permute-done.8 = bf16[2,128,512]{2,1,0:T(8,128)(2,1)S(1)} collective-permute-done((bf16[2,128,512]{2,1,0:T(8,128)(2,1)S(1)}, bf16[2,128,512]{2,1,0:T(8,128)(2,1)S(1)}, u32[]{:S(2)}, u32[]{:S(2)}) %collective-permute-start.8) | collective-permute-done | bytes 262176 | tf_op jit(solution)/shard_map/ppermute | solution.py:778
  51.4 3.4 %collective-permute-start.13 = (bf16[4,128,512]{2,1,0:T(8,128)(2,1)S(1)}, bf16[4,128,512]{2,1,0:T(8,128)(2,1)S(1)}, u32[]{:S(2)}, u32[]{:S(2)}) collective-permute-start(bf16[4,128,512]{2,1,0:T(8,128)(2,1)S(1)} %constant_dynamic-update-slice_fusion.10.refs_6_), channel_id=1, source_target_pairs={{0,8},{4,12},{8,0},{12,4},{16,24},{20,28},{24,16},{28,20},{1,9},{5... | collective-permute-start | bytes 1572872 | tf_op jit(solution)/shard_map/ppermute | solution.py:778
  54.9 1.6 collective-permute-start.12
  56.5 13.4 %shard_map.279 = (bf16[1024,1024]{1,0:T(8,128)(2,1)}, f32[1024,128]{1,0:T(8,128)S(1)}, bf16[1024,512]{1,0:T(8,128)(2,1)}, bf16[1024,512]{1,0:T(8,128)(2,1)}, bf1...) custom-call(s32[3]{0:T(128)S(1)} %pad_add_fusion.me_ref.refs_0_, ...), custom_call_target="tpu_custom_call" | custom-call | flops 16000000000 | tf_op jit(solution)/shard_map/pallas_call | solution.py:260
  71.4 7.8 %shard_map.280 = (f32[1024,512]{1,0:T(8,128)}, bf16[1024,512]{1,0:T(8,128)(2,1)}, f32[8,1024]{1,0:T(8,128)S(1)}, bf16[1024,512]{1,0:T(8,128)(2,1)}, bf16[1024,512]{1,0:T(8,128)(2,1)}) custom-call(s32[3]{0:T(128)S(1)} %pad_add_fusion.me_ref.refs_0_, bf16[1024,256]{1,0:T(8,128)(2,1)S(1)} %copy-done.3, bf16[1024,256]{1,0:T(8,128)(2,1)} %copy-done.37, ...), custom_call_target="tpu_custom_call" | custom-call | flops 8000000000 | tf_op jit(solution)/shard_map/pallas_call | solution.py:327
  81.3 3.2 %collective-permute-done.18 = f32[8,1024]{1,0:T(8,128)S(1)} collective-permute-done((f32[8,1024]{1,0:T(8,128)S(1)}, f32[8,1024]{1,0:T(8,128)S(1)}, u32[]{:S(2)}, u32[]{:S(2)}) %collective-permute-start.18) | collective-permute-done | bytes 32800 | tf_op jit(solution)/shard_map/ppermute | solution.py:778
  84.5 11.1 %shard_map.281 = (bf16[1024,512]{1,0:T(8,128)(2,1)}, bf16[1024,512]{1,0:T(8,128)(2,1)}, bf16[2,1024,256]{2,1,0:T(8,128)(2,1)}, bf16[2,1024,256]{2,1,0:T(8,128)(2...) custom-call(s32[3]{0:T(128)S(1)} %pad_add_fusion.me_ref.refs_0_, ...), custom_call_target="tpu_custom_call" | custom-call | flops 10000000000 | tf_op jit(solution)/shard_map/pallas_call | solution.py:423
  96.8 12.0 %shard_map.282 = (bf16[1024,896]{1,0:T(8,128)(2,1)}, bf16[4,512,128]{2,1,0:T(8,128)(2,1)}, f32[8,512]{1,0:T(8,128)S(1)}, f32[8,256]{1,0:T(8,128)S(1)}, f32[8,128...) custom-call(s32[3]{0:T(128)S(1)} %pad_add_fusion.me_ref.refs_0_, ...), custom_call_target="tpu_custom_call" | custom-call | flops 12000000000 | tf_op jit(solution)/shard_map/pallas_call | solution.py:646
  113.9 12.2 %shard_map.283 = (bf16[1024,896]{1,0:T(8,128)(2,1)}, bf16[4,512,128]{2,1,0:T(8,128)(2,1)}, f32[8,512]{1,0:T(8,128)S(1)}, f32[8,256]{1,0:T(8,128)S(1)}, f32[8,128...) custom-call(s32[3]{0:T(128)S(1)} %pad_add_fusion.me_ref.refs_0_, ...), custom_call_target="tpu_custom_call", output_to_operand_aliasing={{0}: (22, {})} | custom-call | flops 12000000000 | tf_op jit(solution)/shard_map/pallas_call | solution.py:646
  127.3 1.5 collective-permute-start.26
  129.2 8.3 %shard_map.284 = (bf16[2,1024,256]{2,1,0:T(8,128)(2,1)}, bf16[2,1024,256]{2,1,0:T(8,128)(2,1)}, f32[8,1024]{1,0:T(8,128)S(1)}, f32[8,1024]{1,0:T(8,128)S(1)}) custom-call(s32[3]{0:T(128)S(1)} %pad_add_fusion.me_ref.refs_0_, bf16[1024,256]{1,0:T(8,128)(2,1)S(1)} %copy-done.1, bf16[1024,256]{1,0:T(8,128)(2,1)} %copy-done.36, bf16[1024,256]{1,0:T(8,128)(2,1)} %copy-done.35, ...), custom_call_target="tpu_custom_call" | custom-call | flops 6000000000 | tf_op jit(solution)/shard_map/pallas_call | solution.py:753
  141.4 5.9 %shard_map.285 = (bf16[4,128,256]{2,1,0:T(8,128)(2,1)S(1)}, bf16[4,128,256]{2,1,0:T(8,128)(2,1)}, bf16[4,128,384]{2,1,0:T(8,128)(2,1)}, bf16[4,128,384]{2,1,0:T(8,128)(2,1)}) custom-call(s32[3]{0:T(128)S(1)} %pad_add_fusion.me_ref.refs_0_, bf16[1024,896]{1,0:T(8,128)(2,1)} %get-tuple-element.264.refs_4_.refs_0_, ...), custom_call_target="tpu_custom_call" | custom-call | flops 5000000000 | tf_op jit(solution)/shard_map/pallas_call | solution.py:710
  149.9 1.6 collective-permute-start.36
  151.5 1.7 collective-permute-start.33
  153.2 1.5 collective-permute-start.32
  156.2 5.2 %collective-permute-done.35 = f32[4632]{0:T(1024)S(1)} collective-permute-done((f32[4632]{0:T(1024)S(1)}, f32[4632]{0:T(1024)S(1)}, u32[]{:S(2)}, u32[]{:S(2)}) %collective-permute-start.35) | collective-permute-done | bytes 18560 | tf_op jit(solution)/shard_map/ppermute | solution.py:778
  162.9 2.1 %collective-permute-done.33 = bf16[4,128,384]{2,1,0:T(8,128)(2,1)} collective-permute-done((bf16[4,128,384]{2,1,0:T(8,128)(2,1)}, bf16[4,128,384]{2,1,0:T(8,128)(2,1)}, u32[]{:S(2)}, u32[]{:S(2)}) %collective-permute-start.33) | collective-permute-done | bytes 393248 | tf_op jit(solution)/shard_map/ppermute | solution.py:778
  167.0 3.0 %collective-permute-start.39 = (bf16[2,128,384]{2,1,0:T(8,128)(2,1)S(1)}, bf16[2,128,384]{2,1,0:T(8,128)(2,1)S(1)}, u32[]{:S(2)}, u32[]{:S(2)}) collective-permute-start(bf16[2,128,384]{2,1,0:T(8,128)(2,1)S(1)} %slice.302), channel_id=1, source_target_pairs={{0,16},{4,20},{8,24},{12,28},{16,0},{20,4},{24,8},{28,12},{1,17},{... | collective-permute-start | bytes 589832 | tf_op jit(solution)/shard_map/ppermute | solution.py:778
  171.3 2.4 %fusion.5 = bf16[1024,256]{1,0:T(8,128)(2,1)} fusion(bf16[1024,256]{1,0:T(8,128)(2,1)S(1)} %copy-done.1, bf16[1,1024,256]{2,1,0:T(8,128)(2,1)} %collective-permute-done.34, bf16[1024,256]{1,0:T(8,128)(2,1)S(1)} %copy-done.4, f32[1024]{0:T(1024)S(1)} %broadcast_multiply_fusion, f32[256]{0:T(256)S(1)} %dynamic_slice.11, ...), kind=kLoop, calls=%fused_computation.8 | loop fusion | flops 3670016 | bytes 3154944 | tf_op jit(solution)/shard_map/convert_element_type | solution.py:1099
  174.4 4.1 %collective-permute-done.38 = bf16[2,128,256]{2,1,0:T(8,128)(2,1)S(1)} collective-permute-done((bf16[2,128,256]{2,1,0:T(8,128)(2,1)S(1)}, bf16[2,128,256]{2,1,0:T(8,128)(2,1)S(1)}, u32[]{:S(2)}, u32[]{:S(2)}) %collective-permute-start.38) | collective-permute-done | bytes 131104 | tf_op jit(solution)/shard_map/ppermute | solution.py:778
  179.5 3.0 %collective-permute-start.41 = (bf16[1,128,256]{2,1,0:T(8,128)(2,1)S(1)}, bf16[1,128,256]{2,1,0:T(8,128)(2,1)S(1)}, u32[]{:S(2)}, u32[]{:S(2)}) collective-permute-start(bf16[1,128,256]{2,1,0:T(8,128)(2,1)S(1)} %slice.307), channel_id=1, source_target_pairs={{0,16},{4,20},{8,24},{12,28},{16,0},{20,4},{24,8},{28,12},{1,17},{... | collective-permute-start | bytes 196616 | tf_op jit(solution)/shard_map/ppermute | solution.py:778
  182.6 1.6 collective-permute-start.42
  (247 shorter events, 40.8 us)
Async XLA Ops:
  0.7 17.3 %collective-permute-start.2 = (bf16[1024,256]{1,0:T(8,128)(2,1)}, bf16[1024,256]{1,0:T(8,128)(2,1)S(1)}, u32[]{:S(2)}, u32[]{:S(2)}) collective-permute-start(bf16[1024,256]{1,0:T(8,128)(2,1)} %refs_0_.7), channel_id=1, source_target_pairs={{0,2},{1,3},{2,0},{3,1},{4,6},{5,7},{6,4},{7,5},{8,10},{9,11},{10,... | collective-permute-start | bytes 1572872 | tf_op jit(solution)/shard_map/ppermute | solution.py:778
  3.7 14.3 %collective-permute-start.3 = (bf16[1024,256]{1,0:T(8,128)(2,1)}, bf16[1024,256]{1,0:T(8,128)(2,1)S(1)}, u32[]{:S(2)}, u32[]{:S(2)}) collective-permute-start(bf16[1024,256]{1,0:T(8,128)(2,1)} %refs_0_.7), channel_id=1, source_target_pairs={{0,1},{1,0},{2,3},{3,2},{4,5},{5,4},{6,7},{7,6},{8,9},{9,8},{10,11... | collective-permute-start | bytes 1572872 | tf_op jit(solution)/shard_map/ppermute | solution.py:778
  5.5 12.5 %collective-permute-start = (bf16[1,128,768]{2,1,0:T(8,128)(2,1)S(1)}, bf16[1,128,768]{2,1,0:T(8,128)(2,1)S(1)}, u32[]{:S(2)}, u32[]{:S(2)}) collective-permute-start(bf16[1,128,768]{2,1,0:T(8,128)(2,1)S(1)} %fusion.8), channel_id=1, source_target_pairs={{0,16},{4,20},{8,24},{12,28},{16,0},{20,4},{24,8},{28,12},{1,17},{... | collective-permute-start | bytes 589832 | tf_op jit(solution)/shard_map/ppermute | solution.py:778
  18.1 13.6 %collective-permute-start.4 = (bf16[2,128,768]{2,1,0:T(8,128)(2,1)S(1)}, bf16[2,128,768]{2,1,0:T(8,128)(2,1)S(1)}, u32[]{:S(2)}, u32[]{:S(2)}) collective-permute-start(bf16[2,128,768]{2,1,0:T(8,128)(2,1)S(1)} %constant_dynamic-update-slice_fusion), channel_id=1, source_target_pairs={{0,8},{4,12},{8,0},{12,4},{16,24},{20,28},{24,16},{28,20},{1,9},{5... | collective-permute-start | bytes 1179656 | tf_op jit(solution)/shard_map/ppermute | solution.py:778
  18.8 11.5 %collective-permute-start.5 = (bf16[1,128,512]{2,1,0:T(8,128)(2,1)}, bf16[1,128,512]{2,1,0:T(8,128)(2,1)S(1)}, u32[]{:S(2)}, u32[]{:S(2)}) collective-permute-start(bf16[1,128,512]{2,1,0:T(8,128)(2,1)} %bitcast.64), channel_id=1, source_target_pairs={{0,16},{4,20},{8,24},{12,28},{16,0},{20,4},{24,8},{28,12},{1,17},{... | collective-permute-start | bytes 393224 | tf_op jit(solution)/shard_map/ppermute | solution.py:778
  31.8 18.5 %collective-permute-start.6 = (bf16[4,128,768]{2,1,0:T(8,128)(2,1)S(1)}, bf16[4,128,768]{2,1,0:T(8,128)(2,1)}, u32[]{:S(2)}, u32[]{:S(2)}) collective-permute-start(bf16[4,128,768]{2,1,0:T(8,128)(2,1)S(1)} %constant_dynamic-update-slice_fusion.2.refs_4_), channel_id=1, source_target_pairs={{0,4},{4,0},{8,12},{12,8},{16,20},{20,16},{24,28},{28,24},{1,5},{5... | collective-permute-start | bytes 2359304 | tf_op jit(solution)/shard_map/ppermute | solution.py:778
  33.4 13.5 %collective-permute-start.8 = (bf16[2,128,512]{2,1,0:T(8,128)(2,1)S(1)}, bf16[2,128,512]{2,1,0:T(8,128)(2,1)S(1)}, u32[]{:S(2)}, u32[]{:S(2)}) collective-permute-start(bf16[2,128,512]{2,1,0:T(8,128)(2,1)S(1)} %constant_dynamic-update-slice_fusion.6), channel_id=1, source_target_pairs={{0,16},{4,20},{8,24},{12,28},{16,0},{20,4},{24,8},{28,12},{1,17},{... | collective-permute-start | bytes 786440 | tf_op jit(solution)/shard_map/ppermute | solution.py:778
  35.4 13.0 %collective-permute-start.9 = (bf16[1024,256]{1,0:T(8,128)(2,1)S(1)}, bf16[1024,256]{1,0:T(8,128)(2,1)}, u32[]{:S(2)}, u32[]{:S(2)}) collective-permute-start(bf16[1024,256]{1,0:T(8,128)(2,1)S(1)} %collective-permute-done.2.refs_2_), channel_id=1, source_target_pairs={{0,1},{1,0},{2,3},{3,2},{4,5},{5,4},{6,7},{7,6},{8,9},{9,8},{10,11... | collective-permute-start | bytes 1572872 | tf_op jit(solution)/shard_map/ppermute | solution.py:778
  35.4 14.4 %collective-permute-start.10 = (bf16[1024,256]{1,0:T(8,128)(2,1)S(1)}, bf16[1024,256]{1,0:T(8,128)(2,1)}, u32[]{:S(2)}, u32[]{:S(2)}) collective-permute-start(bf16[1024,256]{1,0:T(8,128)(2,1)S(1)} %copy-done.3), channel_id=1, source_target_pairs={{0,2},{1,3},{2,0},{3,1},{4,6},{5,7},{6,4},{7,5},{8,10},{9,11},{10,... | collective-permute-start | bytes 1572872 | tf_op jit(solution)/shard_map/ppermute | solution.py:778
  35.9 12.4 %collective-permute-start.7 = (bf16[2,128,512]{2,1,0:T(8,128)(2,1)S(1)}, bf16[2,128,512]{2,1,0:T(8,128)(2,1)S(1)}, u32[]{:S(2)}, u32[]{:S(2)}) collective-permute-start(bf16[2,128,512]{2,1,0:T(8,128)(2,1)S(1)} %constant_dynamic-update-slice_fusion.4), channel_id=1, source_target_pairs={{0,8},{4,12},{8,0},{12,4},{16,24},{20,28},{24,16},{28,20},{1,9},{5... | collective-permute-start | bytes 786440 | tf_op jit(solution)/shard_map/ppermute | solution.py:778
  48.2 21.8 %collective-permute-start.15 = (bf16[1024,256]{1,0:T(8,128)(2,1)S(1)}, bf16[1024,256]{1,0:T(8,128)(2,1)S(1)}, u32[]{:S(2)}, u32[]{:S(2)}) collective-permute-start(bf16[1024,256]{1,0:T(8,128)(2,1)S(1)} %copy-done.3), channel_id=1, source_target_pairs={{0,1},{1,0},{2,3},{3,2},{4,5},{5,4},{6,7},{7,6},{8,9},{9,8},{10,11... | collective-permute-start | bytes 1572872 | tf_op jit(solution)/shard_map/ppermute | solution.py:778
  51.4 18.6 %collective-permute-start.13 = (bf16[4,128,512]{2,1,0:T(8,128)(2,1)S(1)}, bf16[4,128,512]{2,1,0:T(8,128)(2,1)S(1)}, u32[]{:S(2)}, u32[]{:S(2)}) collective-permute-start(bf16[4,128,512]{2,1,0:T(8,128)(2,1)S(1)} %constant_dynamic-update-slice_fusion.10.refs_6_), channel_id=1, source_target_pairs={{0,8},{4,12},{8,0},{12,4},{16,24},{20,28},{24,16},{28,20},{1,9},{5... | collective-permute-start | bytes 1572872 | tf_op jit(solution)/shard_map/ppermute | solution.py:778
  54.9 15.2 %collective-permute-start.12 = (bf16[4,128,512]{2,1,0:T(8,128)(2,1)S(1)}, bf16[4,128,512]{2,1,0:T(8,128)(2,1)S(1)}, u32[]{:S(2)}, u32[]{:S(2)}) collective-permute-start(bf16[4,128,512]{2,1,0:T(8,128)(2,1)S(1)} %constant_dynamic-update-slice_fusion.8.refs_4_), channel_id=1, source_target_pairs={{0,4},{4,0},{8,12},{12,8},{16,20},{20,16},{24,28},{28,24},{1,5},{5... | collective-permute-start | bytes 1572872 | tf_op jit(solution)/shard_map/ppermute | solution.py:778
  56.4 13.6 %collective-permute-start.16 = (bf16[1024,256]{1,0:T(8,128)(2,1)}, bf16[1024,256]{1,0:T(8,128)(2,1)S(1)}, u32[]{:S(2)}, u32[]{:S(2)}) collective-permute-start(bf16[1024,256]{1,0:T(8,128)(2,1)} %collective-permute-done.10.refs_2_), channel_id=1, source_target_pairs={{0,1},{1,0},{2,3},{3,2},{4,5},{5,4},{6,7},{7,6},{8,9},{9,8},{10,11... | collective-permute-start | bytes 1572872 | tf_op jit(solution)/shard_map/ppermute | solution.py:778
  95.6 14.9 %collective-permute-start.21 = (bf16[2,1024,256]{2,1,0:T(8,128)(2,1)}, bf16[2,1024,256]{2,1,0:T(8,128)(2,1)S(1)}, u32[]{:S(2)}, u32[]{:S(2)}) collective-permute-start(bf16[2,1024,256]{2,1,0:T(8,128)(2,1)} %get-tuple-element.226), channel_id=1, source_target_pairs={{0,1},{1,0},{2,3},{3,2},{4,5},{5,4},{6,7},{7,6},{8,9},{9,8},{10,11... | collective-permute-start | bytes 3145736 | tf_op jit(solution)/shard_map/ppermute | solution.py:778
  95.7 14.3 %collective-permute-start.19 = (bf16[4,128,512]{2,1,0:T(8,128)(2,1)S(1)}, bf16[4,128,512]{2,1,0:T(8,128)(2,1)S(1)}, u32[]{:S(2)}, u32[]{:S(2)}) collective-permute-start(bf16[4,128,512]{2,1,0:T(8,128)(2,1)S(1)} %get-tuple-element.222), channel_id=1, source_target_pairs={{0,4},{4,0},{8,12},{12,8},{16,20},{20,16},{24,28},{28,24},{1,5},{5... | collective-permute-start | bytes 1572872 | tf_op jit(solution)/shard_map/ppermute | solution.py:778
  96.3 14.2 %collective-permute-start.20 = (bf16[4,128,512]{2,1,0:T(8,128)(2,1)}, bf16[4,128,512]{2,1,0:T(8,128)(2,1)S(1)}, u32[]{:S(2)}, u32[]{:S(2)}) collective-permute-start(bf16[4,128,512]{2,1,0:T(8,128)(2,1)} %get-tuple-element.224), channel_id=1, source_target_pairs={{0,8},{4,12},{8,0},{12,4},{16,24},{20,28},{24,16},{28,20},{1,9},{5... | collective-permute-start | bytes 1572872 | tf_op jit(solution)/shard_map/ppermute | solution.py:778
  110.9 15.5 %collective-permute-start.24 = (bf16[1,1024,256]{2,1,0:T(8,128)(2,1)S(1)}, bf16[1,1024,256]{2,1,0:T(8,128)(2,1)S(1)}, u32[]{:S(2)}, u32[]{:S(2)}) collective-permute-start(bf16[1,1024,256]{2,1,0:T(8,128)(2,1)S(1)} %slice.299), channel_id=1, source_target_pairs={{0,2},{1,3},{2,0},{3,1},{4,6},{5,7},{6,4},{7,5},{8,10},{9,11},{10,... | collective-permute-start | bytes 1572872 | tf_op jit(solution)/shard_map/ppermute | solution.py:778
  111.8 14.4 %collective-permute-start.23 = (bf16[2,128,512]{2,1,0:T(8,128)(2,1)S(1)}, bf16[2,128,512]{2,1,0:T(8,128)(2,1)S(1)}, u32[]{:S(2)}, u32[]{:S(2)}) collective-permute-start(bf16[2,128,512]{2,1,0:T(8,128)(2,1)S(1)} %slice.300), channel_id=1, source_target_pairs={{0,16},{4,20},{8,24},{12,28},{16,0},{20,4},{24,8},{28,12},{1,17},{... | collective-permute-start | bytes 786440 | tf_op jit(solution)/shard_map/ppermute | solution.py:778
  113.5 12.9 %collective-permute-start.22 = (bf16[2,128,512]{2,1,0:T(8,128)(2,1)S(1)}, bf16[2,128,512]{2,1,0:T(8,128)(2,1)S(1)}, u32[]{:S(2)}, u32[]{:S(2)}) collective-permute-start(bf16[2,128,512]{2,1,0:T(8,128)(2,1)S(1)} %slice.301), channel_id=1, source_target_pairs={{0,8},{4,12},{8,0},{12,4},{16,24},{20,28},{24,16},{28,20},{1,9},{5... | collective-permute-start | bytes 786440 | tf_op jit(solution)/shard_map/ppermute | solution.py:778
  127.2 10.3 %collective-permute-start.25 = (bf16[512,128]{1,0:T(8,128)(2,1)S(1)}, bf16[512,128]{1,0:T(8,128)(2,1)S(1)}, u32[]{:S(2)}, u32[]{:S(2)}) collective-permute-start(bf16[512,128]{1,0:T(8,128)(2,1)S(1)} %get-tuple-element.367), channel_id=1, source_target_pairs={{0,1},{1,0},{2,3},{3,2},{4,5},{5,4},{6,7},{7,6},{8,9},{9,8},{10,11... | collective-permute-start | bytes 393224 | tf_op jit(solution)/shard_map/ppermute | solution.py:778
  127.3 10.3 %collective-permute-start.26 = (bf16[512,128]{1,0:T(8,128)(2,1)S(1)}, bf16[512,128]{1,0:T(8,128)(2,1)S(1)}, u32[]{:S(2)}, u32[]{:S(2)}) collective-permute-start(bf16[512,128]{1,0:T(8,128)(2,1)S(1)} %get-tuple-element.366), channel_id=1, source_target_pairs={{0,2},{1,3},{2,0},{3,1},{4,6},{5,7},{6,4},{7,5},{8,10},{9,11},{10,... | collective-permute-start | bytes 393224 | tf_op jit(solution)/shard_map/ppermute | solution.py:778
  128.8 8.7 %collective-permute-start.27 = (bf16[512,128]{1,0:T(8,128)(2,1)S(1)}, bf16[512,128]{1,0:T(8,128)(2,1)S(1)}, u32[]{:S(2)}, u32[]{:S(2)}) collective-permute-start(bf16[512,128]{1,0:T(8,128)(2,1)S(1)} %get-tuple-element.365), channel_id=1, source_target_pairs={{0,3},{1,2},{2,1},{3,0},{4,7},{5,6},{6,5},{7,4},{8,11},{9,10},{10,... | collective-permute-start | bytes 393224 | tf_op jit(solution)/shard_map/ppermute | solution.py:778
  137.6 9.8 %collective-permute-start.28 = (bf16[2,1024,256]{2,1,0:T(8,128)(2,1)}, bf16[2,1024,256]{2,1,0:T(8,128)(2,1)S(1)}, u32[]{:S(2)}, u32[]{:S(2)}) collective-permute-start(bf16[2,1024,256]{2,1,0:T(8,128)(2,1)} %get-tuple-element.275), channel_id=1, source_target_pairs={{0,1},{1,0},{2,3},{3,2},{4,5},{5,4},{6,7},{7,6},{8,9},{9,8},{10,11... | collective-permute-start | bytes 3145736 | tf_op jit(solution)/shard_map/ppermute | solution.py:778
  139.5 7.8 %collective-permute-start.29 = (f32[3328]{0:T(1024)S(1)}, f32[3328]{0:T(1024)S(1)}, u32[]{:S(2)}, u32[]{:S(2)}) collective-permute-start(f32[3328]{0:T(1024)S(1)} %pad_maximum_fusion.1), channel_id=1, source_target_pairs={{0,1},{1,0},{2,3},{3,2},{4,5},{5,4},{6,7},{7,6},{8,9},{9,8},{10,11... | collective-permute-start | bytes 39944 | tf_op jit(solution)/shard_map/ppermute | solution.py:778
  148.3 16.7 %collective-permute-start.34 = (bf16[1,1024,256]{2,1,0:T(8,128)(2,1)}, bf16[1,1024,256]{2,1,0:T(8,128)(2,1)}, u32[]{:S(2)}, u32[]{:S(2)}) collective-permute-start(bf16[1,1024,256]{2,1,0:T(8,128)(2,1)} %add_convert_fusion), channel_id=1, source_target_pairs={{0,2},{1,3},{2,0},{3,1},{4,6},{5,7},{6,4},{7,5},{8,10},{9,11},{10,... | collective-permute-start | bytes 1572872 | tf_op jit(solution)/shard_map/ppermute | solution.py:778
  149.9 13.0 %collective-permute-start.36 = (bf16[1,128,512]{2,1,0:T(8,128)(2,1)S(1)}, bf16[1,128,512]{2,1,0:T(8,128)(2,1)S(1)}, u32[]{:S(2)}, u32[]{:S(2)}) collective-permute-start(bf16[1,128,512]{2,1,0:T(8,128)(2,1)S(1)} %slice.305), channel_id=1, source_target_pairs={{0,16},{4,20},{8,24},{12,28},{16,0},{20,4},{24,8},{28,12},{1,17},{... | collective-permute-start | bytes 393224 | tf_op jit(solution)/shard_map/ppermute | solution.py:778
  151.5 13.5 %collective-permute-start.33 = (bf16[4,128,384]{2,1,0:T(8,128)(2,1)}, bf16[4,128,384]{2,1,0:T(8,128)(2,1)}, u32[]{:S(2)}, u32[]{:S(2)}) collective-permute-start(bf16[4,128,384]{2,1,0:T(8,128)(2,1)} %get-tuple-element.293), channel_id=1, source_target_pairs={{0,8},{4,12},{8,0},{12,4},{16,24},{20,28},{24,16},{28,20},{1,9},{5... | collective-permute-start | bytes 1179656 | tf_op jit(solution)/shard_map/ppermute | solution.py:778
  153.2 9.7 %collective-permute-start.32 = (bf16[4,128,256]{2,1,0:T(8,128)(2,1)S(1)}, bf16[4,128,256]{2,1,0:T(8,128)(2,1)}, u32[]{:S(2)}, u32[]{:S(2)}) collective-permute-start(bf16[4,128,256]{2,1,0:T(8,128)(2,1)S(1)} %get-tuple-element.291), channel_id=1, source_target_pairs={{0,4},{4,0},{8,12},{12,8},{16,20},{20,16},{24,28},{28,24},{1,5},{5... | collective-permute-start | bytes 786440 | tf_op jit(solution)/shard_map/ppermute | solution.py:778
  161.4 13.0 %collective-permute-start.37 = (bf16[1,128,512]{2,1,0:T(8,128)(2,1)S(1)}, bf16[1,128,512]{2,1,0:T(8,128)(2,1)S(1)}, u32[]{:S(2)}, u32[]{:S(2)}) collective-permute-start(bf16[1,128,512]{2,1,0:T(8,128)(2,1)S(1)} %slice.304), channel_id=1, source_target_pairs={{0,4},{4,0},{8,12},{12,8},{16,20},{20,16},{24,28},{28,24},{1,5},{5... | collective-permute-start | bytes 393224 | tf_op jit(solution)/shard_map/ppermute | solution.py:778
  165.0 9.4 %collective-permute-start.40 = (f32[4632]{0:T(1024)S(1)}, f32[4632]{0:T(1024)S(1)}, u32[]{:S(2)}, u32[]{:S(2)}) collective-permute-start(f32[4632]{0:T(1024)S(1)} %add.122), channel_id=1, source_target_pairs={{0,8},{4,12},{8,0},{12,4},{16,24},{20,28},{24,16},{28,20},{1,9},{5... | collective-permute-start | bytes 55592 | tf_op jit(solution)/shard_map/ppermute | solution.py:778
  167.0 11.5 %collective-permute-start.39 = (bf16[2,128,384]{2,1,0:T(8,128)(2,1)S(1)}, bf16[2,128,384]{2,1,0:T(8,128)(2,1)S(1)}, u32[]{:S(2)}, u32[]{:S(2)}) collective-permute-start(bf16[2,128,384]{2,1,0:T(8,128)(2,1)S(1)} %slice.302), channel_id=1, source_target_pairs={{0,16},{4,20},{8,24},{12,28},{16,0},{20,4},{24,8},{28,12},{1,17},{... | collective-permute-start | bytes 589832 | tf_op jit(solution)/shard_map/ppermute | solution.py:778
  (60 other events, 752.1 us)

commit v4 on v3

--- a/solution.py
+++ b/solution.py
@@ -10,6 +10,7 @@
 CONV_WIDTH = 4
 LEN = 1024
 BLOCK = 256
+ROWS = 512
 LANES = 128
 
 epsilon = 1e-05
@@ -322,11 +323,11 @@
     groups = len(cots)
     features = share * groups
     inner = scanned.shape[1]
-    per = lambda width: pl.BlockSpec((BLOCK, width), lambda i: (i, 0))
+    per = lambda width: pl.BlockSpec((ROWS, width), lambda i: (i, 0))
     whole = pl.BlockSpec((features, inner), lambda i: (0, 0))
     return pl.pallas_call(
         functools.partial(gate_kernel, (z_rels, o_rels, groups)),
-        grid=(count // BLOCK,),
+        grid=(count // ROWS,),
         in_specs=[scalar_spec()]
         + [per(share)] * groups
         + [const_spec(a) for a in weights]
@@ -334,7 +335,7 @@
         out_specs=[
             per(inner),
             per(inner),
-            pl.BlockSpec((8, BLOCK), lambda i: (0, i)),
+            pl.BlockSpec((8, ROWS), lambda i: (0, i)),
             whole,
             whole,
         ],
@@ -682,7 +683,7 @@
     steps = turn(late_ref[:, rest:])
     state = sum(ref[...].astype(f32) for ref in state_refs).astype(bf16)
     state = jnp.where(pl.program_id(0) < pl.num_programs(0) // 2, state, turn(state))
-    first = lax.broadcasted_iota(jnp.int32, (BLOCK, LANES), 1) < width
+    first = lax.broadcasted_iota(jnp.int32, (ROWS, LANES), 1) < width
     both = jnp.concatenate([late_ref[:, :inner], jnp.where(first, state, steps)], axis=1)
     total[...] += dot(normed_ref[...], both, 0, 0)
 
@@ -703,13 +704,13 @@
     features = normed.shape[1]
     size = features // shards
     cut = inner // 2
-    per = lambda width: pl.BlockSpec((BLOCK, width), lambda i: (i, 0))
-    packed = pl.BlockSpec((BLOCK, LANES), lambda i: (i % (count // BLOCK // 2), 0))
+    per = lambda width: pl.BlockSpec((ROWS, width), lambda i: (i, 0))
+    packed = pl.BlockSpec((ROWS, LANES), lambda i: (i % (count // ROWS // 2), 0))
     a_part, b_part = (shards // 2, size, cut), (shards // 2, size, inner + LANES - cut)
     outs = [a_part, a_part, b_part, b_part]
     return pl.pallas_call(
         functools.partial(late_kernel, (a_rels, b_rels, inner, half)),
-        grid=(count // BLOCK,),
+        grid=(count // ROWS,),
         in_specs=[scalar_spec(), per(wide)] + [packed] * len(states) + [per(features)],
         out_specs=[pl.BlockSpec(dims, lambda i: (0, 0, 0)) for dims in outs],
         out_shape=[out(dims, bf16) for dims in outs],
@@ -732,7 +733,7 @@
     grad_gate = gate_grad_ref[...]
     late = late_ref[...]
     scale = scale_ref[:, 0:1]
-    stat = jnp.zeros((BLOCK, share), f32)
+    stat = jnp.zeros((ROWS, share), f32)
     for rel in range(groups):
         rows = row_of(me_ref[0 + 1] ^ rel, share)
         part = dot(grad_gate, z_ref[rows, :], 1, 1) + dot(late, weight_ref[rows, :], 1, 1)
@@ -748,11 +749,11 @@
     count, share = pieces[0].shape
     groups = len(pieces)
     features = share * groups
-    per = lambda width: pl.BlockSpec((BLOCK, width), lambda i: (i, 0))
-    parts = pl.BlockSpec((groups // 2, BLOCK, share), lambda i: (0, i, 0))
+    per = lambda width: pl.BlockSpec((ROWS, width), lambda i: (i, 0))
+    parts = pl.BlockSpec((groups // 2, ROWS, share), lambda i: (0, i, 0))
     return pl.pallas_call(
         functools.partial(rows_kernel, groups),
-        grid=(count // BLOCK,),
+        grid=(count // ROWS,),
         in_specs=[scalar_spec()]
         + [per(a.shape[1]) for a in (*pieces, late, grad_gate, scale)]
         + [const_spec(a) for a in (z_all, weight, gain)],
@@ -760,7 +761,7 @@
             parts,
             parts,
             pl.BlockSpec((8, features), lambda i: (0, 0)),
-            pl.BlockSpec((8, BLOCK), lambda i: (0, i)),
+            pl.BlockSpec((8, ROWS), lambda i: (0, i)),
         ],
         out_shape=[
             out((groups // 2, count, share), bf16),

time: 190 us -> 188 us (0.989)
  no operation moved by 1% of the time
where the time goes in v4:
time: 188 us
  Pallas kernels  69.2 us (37%)
  starting transfers between devices  48.9 us (26%)
  waiting for transfers between devices  45.7 us (24%)
  local copies, waits for them, and re-layouts  12 us (6%)
  other arithmetic  10.4 us (6%)
    ppermute x44, starting transfers between devices, swap(): return lax.ppermute(value, axis, [(i, i ^ step) for i in range(count)])  48.9 us
    ppermute x44, waiting for transfers between devices, swap(): return lax.ppermute(value, axis, [(i, i ^ step) for i in range(count)])  45.7 us
    pallas_call x2, Pallas kernels, backward_scan(): pl.pallas_call(functools.partial(backward_kernel, sizes), grid=(stop - fi...  24.1 us
    pallas_call x1, Pallas kernels, forward_scan(): pl.pallas_call(functools.partial(forward_kernel, (head_share, head_size,...  13.4 us
    pallas_call x1, Pallas kernels, mix(): pl.pallas_call(functools.partial(mix_kernel, (z_rels, o_rels, groups)), g...  11.2 us
    pallas_call x1, Pallas kernels, row_grads(): pl.pallas_call(functools.partial(rows_kernel, groups), grid=(count // ROW...  8.11 us
    pallas_call x1, Pallas kernels, gate(): pl.pallas_call(functools.partial(gate_kernel, (z_rels, o_rels, groups)),...  7.45 us
    unnamed x95, local copies, waits for them, and re-layouts  6.37 us
  transfers between devices with their start and end apart: 44, of which 17 were waited for; matrix products, arithmetic and copies ran while one was open for 9% of the time, Pallas kernels for 27%

profile of v4, /device:TPU:0, one launch (start us, length us, event | category | flops | bytes accessed | tf_op | source)
XLA Modules:
  0.0 187.9 jit_solution(7596654382748931358)
XLA Ops:
  0.7 3.0 %collective-permute-start.2 = (bf16[1024,256]{1,0:T(8,128)(2,1)}, bf16[1024,256]{1,0:T(8,128)(2,1)S(1)}, u32[]{:S(2)}, u32[]{:S(2)}) collective-permute-start(bf16[1024,256]{1,0:T(8,128)(2,1)} %refs_0_.7), channel_id=1, source_target_pairs={{0,2},{1,3},{2,0},{3,1},{4,6},{5,7},{6,4},{7,5},{8,10},{9,11},{10,... | collective-permute-start | bytes 1572872 | tf_op jit(solution)/shard_map/ppermute | solution.py:779
  5.5 2.7 %collective-permute-start = (bf16[1,128,768]{2,1,0:T(8,128)(2,1)S(1)}, bf16[1,128,768]{2,1,0:T(8,128)(2,1)S(1)}, u32[]{:S(2)}, u32[]{:S(2)}) collective-permute-start(bf16[1,128,768]{2,1,0:T(8,128)(2,1)S(1)} %fusion.8), channel_id=1, source_target_pairs={{0,16},{4,20},{8,24},{12,28},{16,0},{20,4},{24,8},{28,12},{1,17},{... | collective-permute-start | bytes 589832 | tf_op jit(solution)/shard_map/ppermute | solution.py:779
  9.2 1.6 collective-permute-start.1
  10.7 4.1 %collective-permute-done.1 = bf16[1,128,512]{2,1,0:T(8,128)(2,1)S(1)} collective-permute-done((bf16[1,128,512]{2,1,0:T(8,128)(2,1)S(1)}, bf16[1,128,512]{2,1,0:T(8,128)(2,1)S(1)}, u32[]{:S(2)}, u32[]{:S(2)}) %collective-permute-start.1) | collective-permute-done | bytes 131104 | tf_op jit(solution)/shard_map/ppermute | solution.py:779
  14.9 3.1 %collective-permute-done = bf16[1,128,768]{2,1,0:T(8,128)(2,1)S(1)} collective-permute-done((bf16[1,128,768]{2,1,0:T(8,128)(2,1)S(1)}, bf16[1,128,768]{2,1,0:T(8,128)(2,1)S(1)}, u32[]{:S(2)}, u32[]{:S(2)}) %collective-permute-start) | collective-permute-done | bytes 196640 | tf_op jit(solution)/shard_map/ppermute | solution.py:779
  18.8 3.4 %collective-permute-start.5 = (bf16[1,128,512]{2,1,0:T(8,128)(2,1)}, bf16[1,128,512]{2,1,0:T(8,128)(2,1)S(1)}, u32[]{:S(2)}, u32[]{:S(2)}) collective-permute-start(bf16[1,128,512]{2,1,0:T(8,128)(2,1)} %bitcast.64), channel_id=1, source_target_pairs={{0,16},{4,20},{8,24},{12,28},{16,0},{20,4},{24,8},{28,12},{1,17},{... | collective-permute-start | bytes 393224 | tf_op jit(solution)/shard_map/ppermute | solution.py:779
  22.2 8.1 %collective-permute-done.5 = bf16[1,128,512]{2,1,0:T(8,128)(2,1)S(1)} collective-permute-done((bf16[1,128,512]{2,1,0:T(8,128)(2,1)}, bf16[1,128,512]{2,1,0:T(8,128)(2,1)S(1)}, u32[]{:S(2)}, u32[]{:S(2)}) %collective-permute-start.5) | collective-permute-done | bytes 131104 | tf_op jit(solution)/shard_map/ppermute | solution.py:779
  31.8 1.6 collective-permute-start.6
  33.4 2.0 %collective-permute-start.8 = (bf16[2,128,512]{2,1,0:T(8,128)(2,1)S(1)}, bf16[2,128,512]{2,1,0:T(8,128)(2,1)S(1)}, u32[]{:S(2)}, u32[]{:S(2)}) collective-permute-start(bf16[2,128,512]{2,1,0:T(8,128)(2,1)S(1)} %constant_dynamic-update-slice_fusion.6), channel_id=1, source_target_pairs={{0,16},{4,20},{8,24},{12,28},{16,0},{20,4},{24,8},{28,12},{1,17},{... | collective-permute-start | bytes 786440 | tf_op jit(solution)/shard_map/ppermute | solution.py:779
  35.9 2.5 %collective-permute-start.7 = (bf16[2,128,512]{2,1,0:T(8,128)(2,1)S(1)}, bf16[2,128,512]{2,1,0:T(8,128)(2,1)S(1)}, u32[]{:S(2)}, u32[]{:S(2)}) collective-permute-start(bf16[2,128,512]{2,1,0:T(8,128)(2,1)S(1)} %constant_dynamic-update-slice_fusion.4), channel_id=1, source_target_pairs={{0,8},{4,12},{8,0},{12,4},{16,24},{20,28},{24,16},{28,20},{1,9},{5... | collective-permute-start | bytes 786440 | tf_op jit(solution)/shard_map/ppermute | solution.py:779
  38.5 8.3 %collective-permute-done.8 = bf16[2,128,512]{2,1,0:T(8,128)(2,1)S(1)} collective-permute-done((bf16[2,128,512]{2,1,0:T(8,128)(2,1)S(1)}, bf16[2,128,512]{2,1,0:T(8,128)(2,1)S(1)}, u32[]{:S(2)}, u32[]{:S(2)}) %collective-permute-start.8) | collective-permute-done | bytes 262176 | tf_op jit(solution)/shard_map/ppermute | solution.py:779
  51.4 3.4 %collective-permute-start.13 = (bf16[4,128,512]{2,1,0:T(8,128)(2,1)S(1)}, bf16[4,128,512]{2,1,0:T(8,128)(2,1)S(1)}, u32[]{:S(2)}, u32[]{:S(2)}) collective-permute-start(bf16[4,128,512]{2,1,0:T(8,128)(2,1)S(1)} %constant_dynamic-update-slice_fusion.10.refs_6_), channel_id=1, source_target_pairs={{0,8},{4,12},{8,0},{12,4},{16,24},{20,28},{24,16},{28,20},{1,9},{5... | collective-permute-start | bytes 1572872 | tf_op jit(solution)/shard_map/ppermute | solution.py:779
  54.9 1.6 collective-permute-start.12
  56.5 13.4 %shard_map.279 = (bf16[1024,1024]{1,0:T(8,128)(2,1)}, f32[1024,128]{1,0:T(8,128)S(1)}, bf16[1024,512]{1,0:T(8,128)(2,1)}, bf16[1024,512]{1,0:T(8,128)(2,1)}, bf1...) custom-call(s32[3]{0:T(128)S(1)} %pad_add_fusion.me_ref.refs_0_, ...), custom_call_target="tpu_custom_call" | custom-call | flops 16000000000 | tf_op jit(solution)/shard_map/pallas_call | solution.py:261
  71.4 7.5 %shard_map.280 = (f32[1024,512]{1,0:T(8,128)}, bf16[1024,512]{1,0:T(8,128)(2,1)}, f32[8,1024]{1,0:T(8,128)S(1)}, bf16[1024,512]{1,0:T(8,128)(2,1)}, bf16[1024,512]{1,0:T(8,128)(2,1)}) custom-call(s32[3]{0:T(128)S(1)} %pad_add_fusion.me_ref.refs_0_, bf16[1024,256]{1,0:T(8,128)(2,1)S(1)} %copy-done.3, bf16[1024,256]{1,0:T(8,128)(2,1)} %copy-done.37, ...), custom_call_target="tpu_custom_call" | custom-call | flops 8000000000 | tf_op jit(solution)/shard_map/pallas_call | solution.py:328
  81.0 3.2 %collective-permute-done.18 = f32[8,1024]{1,0:T(8,128)S(1)} collective-permute-done((f32[8,1024]{1,0:T(8,128)S(1)}, f32[8,1024]{1,0:T(8,128)S(1)}, u32[]{:S(2)}, u32[]{:S(2)}) %collective-permute-start.18) | collective-permute-done | bytes 32800 | tf_op jit(solution)/shard_map/ppermute | solution.py:779
  84.2 11.2 %shard_map.281 = (bf16[1024,512]{1,0:T(8,128)(2,1)}, bf16[1024,512]{1,0:T(8,128)(2,1)}, bf16[2,1024,256]{2,1,0:T(8,128)(2,1)}, bf16[2,1024,256]{2,1,0:T(8,128)(2...) custom-call(s32[3]{0:T(128)S(1)} %pad_add_fusion.me_ref.refs_0_, ...), custom_call_target="tpu_custom_call" | custom-call | flops 10000000000 | tf_op jit(solution)/shard_map/pallas_call | solution.py:424
  96.4 12.0 %shard_map.282 = (bf16[1024,896]{1,0:T(8,128)(2,1)}, bf16[4,512,128]{2,1,0:T(8,128)(2,1)}, f32[8,512]{1,0:T(8,128)S(1)}, f32[8,256]{1,0:T(8,128)S(1)}, f32[8,128...) custom-call(s32[3]{0:T(128)S(1)} %pad_add_fusion.me_ref.refs_0_, ...), custom_call_target="tpu_custom_call" | custom-call | flops 12000000000 | tf_op jit(solution)/shard_map/pallas_call | solution.py:647
  113.6 12.0 %shard_map.283 = (bf16[1024,896]{1,0:T(8,128)(2,1)}, bf16[4,512,128]{2,1,0:T(8,128)(2,1)}, f32[8,512]{1,0:T(8,128)S(1)}, f32[8,256]{1,0:T(8,128)S(1)}, f32[8,128...) custom-call(s32[3]{0:T(128)S(1)} %pad_add_fusion.me_ref.refs_0_, ...), custom_call_target="tpu_custom_call", output_to_operand_aliasing={{0}: (22, {})} | custom-call | flops 12000000000 | tf_op jit(solution)/shard_map/pallas_call | solution.py:647
  128.6 8.1 %shard_map.284 = (bf16[2,1024,256]{2,1,0:T(8,128)(2,1)}, bf16[2,1024,256]{2,1,0:T(8,128)(2,1)}, f32[8,1024]{1,0:T(8,128)S(1)}, f32[8,1024]{1,0:T(8,128)S(1)}) custom-call(s32[3]{0:T(128)S(1)} %pad_add_fusion.me_ref.refs_0_, bf16[1024,256]{1,0:T(8,128)(2,1)S(1)} %copy-done.1, bf16[1024,256]{1,0:T(8,128)(2,1)} %copy-done.36, bf16[1024,256]{1,0:T(8,128)(2,1)} %copy-done.35, ...), custom_call_target="tpu_custom_call" | custom-call | flops 6000000000 | tf_op jit(solution)/shard_map/pallas_call | solution.py:754
  140.7 5.0 %shard_map.285 = (bf16[4,128,256]{2,1,0:T(8,128)(2,1)S(1)}, bf16[4,128,256]{2,1,0:T(8,128)(2,1)}, bf16[4,128,384]{2,1,0:T(8,128)(2,1)}, bf16[4,128,384]{2,1,0:T(8,128)(2,1)}) custom-call(s32[3]{0:T(128)S(1)} %pad_add_fusion.me_ref.refs_0_, bf16[1024,896]{1,0:T(8,128)(2,1)} %get-tuple-element.264.refs_4_.refs_0_, ...), custom_call_target="tpu_custom_call" | custom-call | flops 5000000000 | tf_op jit(solution)/shard_map/pallas_call | solution.py:711
  148.2 1.7 collective-permute-start.36
  149.9 1.7 collective-permute-start.33
  151.6 1.5 collective-permute-start.32
  154.6 5.2 %collective-permute-done.35 = f32[4632]{0:T(1024)S(1)} collective-permute-done((f32[4632]{0:T(1024)S(1)}, f32[4632]{0:T(1024)S(1)}, u32[]{:S(2)}, u32[]{:S(2)}) %collective-permute-start.35) | collective-permute-done | bytes 18560 | tf_op jit(solution)/shard_map/ppermute | solution.py:779
  159.8 1.5 collective-permute-start.37
  161.3 2.0 %collective-permute-done.33 = bf16[4,128,384]{2,1,0:T(8,128)(2,1)} collective-permute-done((bf16[4,128,384]{2,1,0:T(8,128)(2,1)}, bf16[4,128,384]{2,1,0:T(8,128)(2,1)}, u32[]{:S(2)}, u32[]{:S(2)}) %collective-permute-start.33) | collective-permute-done | bytes 393248 | tf_op jit(solution)/shard_map/ppermute | solution.py:779
  165.4 3.0 %collective-permute-start.39 = (bf16[2,128,384]{2,1,0:T(8,128)(2,1)S(1)}, bf16[2,128,384]{2,1,0:T(8,128)(2,1)S(1)}, u32[]{:S(2)}, u32[]{:S(2)}) collective-permute-start(bf16[2,128,384]{2,1,0:T(8,128)(2,1)S(1)} %slice.302), channel_id=1, source_target_pairs={{0,16},{4,20},{8,24},{12,28},{16,0},{20,4},{24,8},{28,12},{1,17},{... | collective-permute-start | bytes 589832 | tf_op jit(solution)/shard_map/ppermute | solution.py:779
  169.7 2.4 %fusion.5 = bf16[1024,256]{1,0:T(8,128)(2,1)} fusion(bf16[1024,256]{1,0:T(8,128)(2,1)S(1)} %copy-done.1, bf16[1,1024,256]{2,1,0:T(8,128)(2,1)} %collective-permute-done.34, bf16[1024,256]{1,0:T(8,128)(2,1)S(1)} %copy-done.4, f32[1024]{0:T(1024)S(1)} %broadcast_multiply_fusion, f32[256]{0:T(256)S(1)} %dynamic_slice.11, ...), kind=kLoop, calls=%fused_computation.8 | loop fusion | flops 3670016 | bytes 3154944 | tf_op jit(solution)/shard_map/convert_element_type | solution.py:1100
  172.8 4.1 %collective-permute-done.38 = bf16[2,128,256]{2,1,0:T(8,128)(2,1)S(1)} collective-permute-done((bf16[2,128,256]{2,1,0:T(8,128)(2,1)S(1)}, bf16[2,128,256]{2,1,0:T(8,128)(2,1)S(1)}, u32[]{:S(2)}, u32[]{:S(2)}) %collective-permute-start.38) | collective-permute-done | bytes 131104 | tf_op jit(solution)/shard_map/ppermute | solution.py:779
  178.0 3.0 %collective-permute-start.41 = (bf16[1,128,256]{2,1,0:T(8,128)(2,1)S(1)}, bf16[1,128,256]{2,1,0:T(8,128)(2,1)S(1)}, u32[]{:S(2)}, u32[]{:S(2)}) collective-permute-start(bf16[1,128,256]{2,1,0:T(8,128)(2,1)S(1)} %slice.307), channel_id=1, source_target_pairs={{0,16},{4,20},{8,24},{12,28},{16,0},{20,4},{24,8},{28,12},{1,17},{... | collective-permute-start | bytes 196616 | tf_op jit(solution)/shard_map/ppermute | solution.py:779
  181.0 1.6 collective-permute-start.42
  (247 shorter events, 40.9 us)
Async XLA Ops:
  0.7 17.3 %collective-permute-start.2 = (bf16[1024,256]{1,0:T(8,128)(2,1)}, bf16[1024,256]{1,0:T(8,128)(2,1)S(1)}, u32[]{:S(2)}, u32[]{:S(2)}) collective-permute-start(bf16[1024,256]{1,0:T(8,128)(2,1)} %refs_0_.7), channel_id=1, source_target_pairs={{0,2},{1,3},{2,0},{3,1},{4,6},{5,7},{6,4},{7,5},{8,10},{9,11},{10,... | collective-permute-start | bytes 1572872 | tf_op jit(solution)/shard_map/ppermute | solution.py:779
  3.7 14.3 %collective-permute-start.3 = (bf16[1024,256]{1,0:T(8,128)(2,1)}, bf16[1024,256]{1,0:T(8,128)(2,1)S(1)}, u32[]{:S(2)}, u32[]{:S(2)}) collective-permute-start(bf16[1024,256]{1,0:T(8,128)(2,1)} %refs_0_.7), channel_id=1, source_target_pairs={{0,1},{1,0},{2,3},{3,2},{4,5},{5,4},{6,7},{7,6},{8,9},{9,8},{10,11... | collective-permute-start | bytes 1572872 | tf_op jit(solution)/shard_map/ppermute | solution.py:779
  5.5 12.5 %collective-permute-start = (bf16[1,128,768]{2,1,0:T(8,128)(2,1)S(1)}, bf16[1,128,768]{2,1,0:T(8,128)(2,1)S(1)}, u32[]{:S(2)}, u32[]{:S(2)}) collective-permute-start(bf16[1,128,768]{2,1,0:T(8,128)(2,1)S(1)} %fusion.8), channel_id=1, source_target_pairs={{0,16},{4,20},{8,24},{12,28},{16,0},{20,4},{24,8},{28,12},{1,17},{... | collective-permute-start | bytes 589832 | tf_op jit(solution)/shard_map/ppermute | solution.py:779
  18.1 13.6 %collective-permute-start.4 = (bf16[2,128,768]{2,1,0:T(8,128)(2,1)S(1)}, bf16[2,128,768]{2,1,0:T(8,128)(2,1)S(1)}, u32[]{:S(2)}, u32[]{:S(2)}) collective-permute-start(bf16[2,128,768]{2,1,0:T(8,128)(2,1)S(1)} %constant_dynamic-update-slice_fusion), channel_id=1, source_target_pairs={{0,8},{4,12},{8,0},{12,4},{16,24},{20,28},{24,16},{28,20},{1,9},{5... | collective-permute-start | bytes 1179656 | tf_op jit(solution)/shard_map/ppermute | solution.py:779
  18.8 11.5 %collective-permute-start.5 = (bf16[1,128,512]{2,1,0:T(8,128)(2,1)}, bf16[1,128,512]{2,1,0:T(8,128)(2,1)S(1)}, u32[]{:S(2)}, u32[]{:S(2)}) collective-permute-start(bf16[1,128,512]{2,1,0:T(8,128)(2,1)} %bitcast.64), channel_id=1, source_target_pairs={{0,16},{4,20},{8,24},{12,28},{16,0},{20,4},{24,8},{28,12},{1,17},{... | collective-permute-start | bytes 393224 | tf_op jit(solution)/shard_map/ppermute | solution.py:779
  31.8 18.5 %collective-permute-start.6 = (bf16[4,128,768]{2,1,0:T(8,128)(2,1)S(1)}, bf16[4,128,768]{2,1,0:T(8,128)(2,1)}, u32[]{:S(2)}, u32[]{:S(2)}) collective-permute-start(bf16[4,128,768]{2,1,0:T(8,128)(2,1)S(1)} %constant_dynamic-update-slice_fusion.2.refs_4_), channel_id=1, source_target_pairs={{0,4},{4,0},{8,12},{12,8},{16,20},{20,16},{24,28},{28,24},{1,5},{5... | collective-permute-start | bytes 2359304 | tf_op jit(solution)/shard_map/ppermute | solution.py:779
  33.4 13.5 %collective-permute-start.8 = (bf16[2,128,512]{2,1,0:T(8,128)(2,1)S(1)}, bf16[2,128,512]{2,1,0:T(8,128)(2,1)S(1)}, u32[]{:S(2)}, u32[]{:S(2)}) collective-permute-start(bf16[2,128,512]{2,1,0:T(8,128)(2,1)S(1)} %constant_dynamic-update-slice_fusion.6), channel_id=1, source_target_pairs={{0,16},{4,20},{8,24},{12,28},{16,0},{20,4},{24,8},{28,12},{1,17},{... | collective-permute-start | bytes 786440 | tf_op jit(solution)/shard_map/ppermute | solution.py:779
  35.4 13.0 %collective-permute-start.9 = (bf16[1024,256]{1,0:T(8,128)(2,1)S(1)}, bf16[1024,256]{1,0:T(8,128)(2,1)}, u32[]{:S(2)}, u32[]{:S(2)}) collective-permute-start(bf16[1024,256]{1,0:T(8,128)(2,1)S(1)} %collective-permute-done.2.refs_2_), channel_id=1, source_target_pairs={{0,1},{1,0},{2,3},{3,2},{4,5},{5,4},{6,7},{7,6},{8,9},{9,8},{10,11... | collective-permute-start | bytes 1572872 | tf_op jit(solution)/shard_map/ppermute | solution.py:779
  35.4 14.4 %collective-permute-start.10 = (bf16[1024,256]{1,0:T(8,128)(2,1)S(1)}, bf16[1024,256]{1,0:T(8,128)(2,1)}, u32[]{:S(2)}, u32[]{:S(2)}) collective-permute-start(bf16[1024,256]{1,0:T(8,128)(2,1)S(1)} %copy-done.3), channel_id=1, source_target_pairs={{0,2},{1,3},{2,0},{3,1},{4,6},{5,7},{6,4},{7,5},{8,10},{9,11},{10,... | collective-permute-start | bytes 1572872 | tf_op jit(solution)/shard_map/ppermute | solution.py:779
  35.9 12.4 %collective-permute-start.7 = (bf16[2,128,512]{2,1,0:T(8,128)(2,1)S(1)}, bf16[2,128,512]{2,1,0:T(8,128)(2,1)S(1)}, u32[]{:S(2)}, u32[]{:S(2)}) collective-permute-start(bf16[2,128,512]{2,1,0:T(8,128)(2,1)S(1)} %constant_dynamic-update-slice_fusion.4), channel_id=1, source_target_pairs={{0,8},{4,12},{8,0},{12,4},{16,24},{20,28},{24,16},{28,20},{1,9},{5... | collective-permute-start | bytes 786440 | tf_op jit(solution)/shard_map/ppermute | solution.py:779
  48.2 21.8 %collective-permute-start.15 = (bf16[1024,256]{1,0:T(8,128)(2,1)S(1)}, bf16[1024,256]{1,0:T(8,128)(2,1)S(1)}, u32[]{:S(2)}, u32[]{:S(2)}) collective-permute-start(bf16[1024,256]{1,0:T(8,128)(2,1)S(1)} %copy-done.3), channel_id=1, source_target_pairs={{0,1},{1,0},{2,3},{3,2},{4,5},{5,4},{6,7},{7,6},{8,9},{9,8},{10,11... | collective-permute-start | bytes 1572872 | tf_op jit(solution)/shard_map/ppermute | solution.py:779
  51.4 18.6 %collective-permute-start.13 = (bf16[4,128,512]{2,1,0:T(8,128)(2,1)S(1)}, bf16[4,128,512]{2,1,0:T(8,128)(2,1)S(1)}, u32[]{:S(2)}, u32[]{:S(2)}) collective-permute-start(bf16[4,128,512]{2,1,0:T(8,128)(2,1)S(1)} %constant_dynamic-update-slice_fusion.10.refs_6_), channel_id=1, source_target_pairs={{0,8},{4,12},{8,0},{12,4},{16,24},{20,28},{24,16},{28,20},{1,9},{5... | collective-permute-start | bytes 1572872 | tf_op jit(solution)/shard_map/ppermute | solution.py:779
  54.9 15.2 %collective-permute-start.12 = (bf16[4,128,512]{2,1,0:T(8,128)(2,1)S(1)}, bf16[4,128,512]{2,1,0:T(8,128)(2,1)S(1)}, u32[]{:S(2)}, u32[]{:S(2)}) collective-permute-start(bf16[4,128,512]{2,1,0:T(8,128)(2,1)S(1)} %constant_dynamic-update-slice_fusion.8.refs_4_), channel_id=1, source_target_pairs={{0,4},{4,0},{8,12},{12,8},{16,20},{20,16},{24,28},{28,24},{1,5},{5... | collective-permute-start | bytes 1572872 | tf_op jit(solution)/shard_map/ppermute | solution.py:779
  56.4 13.6 %collective-permute-start.16 = (bf16[1024,256]{1,0:T(8,128)(2,1)}, bf16[1024,256]{1,0:T(8,128)(2,1)S(1)}, u32[]{:S(2)}, u32[]{:S(2)}) collective-permute-start(bf16[1024,256]{1,0:T(8,128)(2,1)} %collective-permute-done.10.refs_2_), channel_id=1, source_target_pairs={{0,1},{1,0},{2,3},{3,2},{4,5},{5,4},{6,7},{7,6},{8,9},{9,8},{10,11... | collective-permute-start | bytes 1572872 | tf_op jit(solution)/shard_map/ppermute | solution.py:779
  95.3 14.9 %collective-permute-start.21 = (bf16[2,1024,256]{2,1,0:T(8,128)(2,1)}, bf16[2,1024,256]{2,1,0:T(8,128)(2,1)S(1)}, u32[]{:S(2)}, u32[]{:S(2)}) collective-permute-start(bf16[2,1024,256]{2,1,0:T(8,128)(2,1)} %get-tuple-element.226), channel_id=1, source_target_pairs={{0,1},{1,0},{2,3},{3,2},{4,5},{5,4},{6,7},{7,6},{8,9},{9,8},{10,11... | collective-permute-start | bytes 3145736 | tf_op jit(solution)/shard_map/ppermute | solution.py:779
  95.4 14.3 %collective-permute-start.19 = (bf16[4,128,512]{2,1,0:T(8,128)(2,1)S(1)}, bf16[4,128,512]{2,1,0:T(8,128)(2,1)S(1)}, u32[]{:S(2)}, u32[]{:S(2)}) collective-permute-start(bf16[4,128,512]{2,1,0:T(8,128)(2,1)S(1)} %get-tuple-element.222), channel_id=1, source_target_pairs={{0,4},{4,0},{8,12},{12,8},{16,20},{20,16},{24,28},{28,24},{1,5},{5... | collective-permute-start | bytes 1572872 | tf_op jit(solution)/shard_map/ppermute | solution.py:779
  96.0 14.2 %collective-permute-start.20 = (bf16[4,128,512]{2,1,0:T(8,128)(2,1)}, bf16[4,128,512]{2,1,0:T(8,128)(2,1)S(1)}, u32[]{:S(2)}, u32[]{:S(2)}) collective-permute-start(bf16[4,128,512]{2,1,0:T(8,128)(2,1)} %get-tuple-element.224), channel_id=1, source_target_pairs={{0,8},{4,12},{8,0},{12,4},{16,24},{20,28},{24,16},{28,20},{1,9},{5... | collective-permute-start | bytes 1572872 | tf_op jit(solution)/shard_map/ppermute | solution.py:779
  110.6 15.5 %collective-permute-start.24 = (bf16[1,1024,256]{2,1,0:T(8,128)(2,1)S(1)}, bf16[1,1024,256]{2,1,0:T(8,128)(2,1)S(1)}, u32[]{:S(2)}, u32[]{:S(2)}) collective-permute-start(bf16[1,1024,256]{2,1,0:T(8,128)(2,1)S(1)} %slice.299), channel_id=1, source_target_pairs={{0,2},{1,3},{2,0},{3,1},{4,6},{5,7},{6,4},{7,5},{8,10},{9,11},{10,... | collective-permute-start | bytes 1572872 | tf_op jit(solution)/shard_map/ppermute | solution.py:779
  111.5 14.2 %collective-permute-start.23 = (bf16[2,128,512]{2,1,0:T(8,128)(2,1)S(1)}, bf16[2,128,512]{2,1,0:T(8,128)(2,1)S(1)}, u32[]{:S(2)}, u32[]{:S(2)}) collective-permute-start(bf16[2,128,512]{2,1,0:T(8,128)(2,1)S(1)} %slice.300), channel_id=1, source_target_pairs={{0,16},{4,20},{8,24},{12,28},{16,0},{20,4},{24,8},{28,12},{1,17},{... | collective-permute-start | bytes 786440 | tf_op jit(solution)/shard_map/ppermute | solution.py:779
  113.1 12.9 %collective-permute-start.22 = (bf16[2,128,512]{2,1,0:T(8,128)(2,1)S(1)}, bf16[2,128,512]{2,1,0:T(8,128)(2,1)S(1)}, u32[]{:S(2)}, u32[]{:S(2)}) collective-permute-start(bf16[2,128,512]{2,1,0:T(8,128)(2,1)S(1)} %slice.301), channel_id=1, source_target_pairs={{0,8},{4,12},{8,0},{12,4},{16,24},{20,28},{24,16},{28,20},{1,9},{5... | collective-permute-start | bytes 786440 | tf_op jit(solution)/shard_map/ppermute | solution.py:779
  126.7 10.1 %collective-permute-start.25 = (bf16[512,128]{1,0:T(8,128)(2,1)S(1)}, bf16[512,128]{1,0:T(8,128)(2,1)S(1)}, u32[]{:S(2)}, u32[]{:S(2)}) collective-permute-start(bf16[512,128]{1,0:T(8,128)(2,1)S(1)} %get-tuple-element.367), channel_id=1, source_target_pairs={{0,1},{1,0},{2,3},{3,2},{4,5},{5,4},{6,7},{7,6},{8,9},{9,8},{10,11... | collective-permute-start | bytes 393224 | tf_op jit(solution)/shard_map/ppermute | solution.py:779
  126.8 10.0 %collective-permute-start.26 = (bf16[512,128]{1,0:T(8,128)(2,1)S(1)}, bf16[512,128]{1,0:T(8,128)(2,1)S(1)}, u32[]{:S(2)}, u32[]{:S(2)}) collective-permute-start(bf16[512,128]{1,0:T(8,128)(2,1)S(1)} %get-tuple-element.366), channel_id=1, source_target_pairs={{0,2},{1,3},{2,0},{3,1},{4,6},{5,7},{6,4},{7,5},{8,10},{9,11},{10,... | collective-permute-start | bytes 393224 | tf_op jit(solution)/shard_map/ppermute | solution.py:779
  128.2 8.6 %collective-permute-start.27 = (bf16[512,128]{1,0:T(8,128)(2,1)S(1)}, bf16[512,128]{1,0:T(8,128)(2,1)S(1)}, u32[]{:S(2)}, u32[]{:S(2)}) collective-permute-start(bf16[512,128]{1,0:T(8,128)(2,1)S(1)} %get-tuple-element.365), channel_id=1, source_target_pairs={{0,3},{1,2},{2,1},{3,0},{4,7},{5,6},{6,5},{7,4},{8,11},{9,10},{10,... | collective-permute-start | bytes 393224 | tf_op jit(solution)/shard_map/ppermute | solution.py:779
  136.8 8.9 %collective-permute-start.28 = (bf16[2,1024,256]{2,1,0:T(8,128)(2,1)}, bf16[2,1024,256]{2,1,0:T(8,128)(2,1)S(1)}, u32[]{:S(2)}, u32[]{:S(2)}) collective-permute-start(bf16[2,1024,256]{2,1,0:T(8,128)(2,1)} %get-tuple-element.275), channel_id=1, source_target_pairs={{0,1},{1,0},{2,3},{3,2},{4,5},{5,4},{6,7},{7,6},{8,9},{9,8},{10,11... | collective-permute-start | bytes 3145736 | tf_op jit(solution)/shard_map/ppermute | solution.py:779
  146.7 16.6 %collective-permute-start.34 = (bf16[1,1024,256]{2,1,0:T(8,128)(2,1)}, bf16[1,1024,256]{2,1,0:T(8,128)(2,1)}, u32[]{:S(2)}, u32[]{:S(2)}) collective-permute-start(bf16[1,1024,256]{2,1,0:T(8,128)(2,1)} %add_convert_fusion), channel_id=1, source_target_pairs={{0,2},{1,3},{2,0},{3,1},{4,6},{5,7},{6,4},{7,5},{8,10},{9,11},{10,... | collective-permute-start | bytes 1572872 | tf_op jit(solution)/shard_map/ppermute | solution.py:779
  148.2 13.1 %collective-permute-start.36 = (bf16[1,128,512]{2,1,0:T(8,128)(2,1)S(1)}, bf16[1,128,512]{2,1,0:T(8,128)(2,1)S(1)}, u32[]{:S(2)}, u32[]{:S(2)}) collective-permute-start(bf16[1,128,512]{2,1,0:T(8,128)(2,1)S(1)} %slice.305), channel_id=1, source_target_pairs={{0,16},{4,20},{8,24},{12,28},{16,0},{20,4},{24,8},{28,12},{1,17},{... | collective-permute-start | bytes 393224 | tf_op jit(solution)/shard_map/ppermute | solution.py:779
  149.9 13.4 %collective-permute-start.33 = (bf16[4,128,384]{2,1,0:T(8,128)(2,1)}, bf16[4,128,384]{2,1,0:T(8,128)(2,1)}, u32[]{:S(2)}, u32[]{:S(2)}) collective-permute-start(bf16[4,128,384]{2,1,0:T(8,128)(2,1)} %get-tuple-element.293), channel_id=1, source_target_pairs={{0,8},{4,12},{8,0},{12,4},{16,24},{20,28},{24,16},{28,20},{1,9},{5... | collective-permute-start | bytes 1179656 | tf_op jit(solution)/shard_map/ppermute | solution.py:779
  151.6 9.7 %collective-permute-start.32 = (bf16[4,128,256]{2,1,0:T(8,128)(2,1)S(1)}, bf16[4,128,256]{2,1,0:T(8,128)(2,1)}, u32[]{:S(2)}, u32[]{:S(2)}) collective-permute-start(bf16[4,128,256]{2,1,0:T(8,128)(2,1)S(1)} %get-tuple-element.291), channel_id=1, source_target_pairs={{0,4},{4,0},{8,12},{12,8},{16,20},{20,16},{24,28},{28,24},{1,5},{5... | collective-permute-start | bytes 786440 | tf_op jit(solution)/shard_map/ppermute | solution.py:779
  159.8 13.0 %collective-permute-start.37 = (bf16[1,128,512]{2,1,0:T(8,128)(2,1)S(1)}, bf16[1,128,512]{2,1,0:T(8,128)(2,1)S(1)}, u32[]{:S(2)}, u32[]{:S(2)}) collective-permute-start(bf16[1,128,512]{2,1,0:T(8,128)(2,1)S(1)} %slice.304), channel_id=1, source_target_pairs={{0,4},{4,0},{8,12},{12,8},{16,20},{20,16},{24,28},{28,24},{1,5},{5... | collective-permute-start | bytes 393224 | tf_op jit(solution)/shard_map/ppermute | solution.py:779
  163.3 9.5 %collective-permute-start.40 = (f32[4632]{0:T(1024)S(1)}, f32[4632]{0:T(1024)S(1)}, u32[]{:S(2)}, u32[]{:S(2)}) collective-permute-start(f32[4632]{0:T(1024)S(1)} %add.122), channel_id=1, source_target_pairs={{0,8},{4,12},{8,0},{12,4},{16,24},{20,28},{24,16},{28,20},{1,9},{5... | collective-permute-start | bytes 55592 | tf_op jit(solution)/shard_map/ppermute | solution.py:779
  165.4 11.5 %collective-permute-start.39 = (bf16[2,128,384]{2,1,0:T(8,128)(2,1)S(1)}, bf16[2,128,384]{2,1,0:T(8,128)(2,1)S(1)}, u32[]{:S(2)}, u32[]{:S(2)}) collective-permute-start(bf16[2,128,384]{2,1,0:T(8,128)(2,1)S(1)} %slice.302), channel_id=1, source_target_pairs={{0,16},{4,20},{8,24},{12,28},{16,0},{20,4},{24,8},{28,12},{1,17},{... | collective-permute-start | bytes 589832 | tf_op jit(solution)/shard_map/ppermute | solution.py:779
  178.0 7.6 %collective-permute-start.41 = (bf16[1,128,256]{2,1,0:T(8,128)(2,1)S(1)}, bf16[1,128,256]{2,1,0:T(8,128)(2,1)S(1)}, u32[]{:S(2)}, u32[]{:S(2)}) collective-permute-start(bf16[1,128,256]{2,1,0:T(8,128)(2,1)S(1)} %slice.307), channel_id=1, source_target_pairs={{0,16},{4,20},{8,24},{12,28},{16,0},{20,4},{24,8},{28,12},{1,17},{... | collective-permute-start | bytes 196616 | tf_op jit(solution)/shard_map/ppermute | solution.py:779
  (60 other events, 745.5 us)
